TPU v7x, 32 devices: a whole 2x2x4 slice. The times are simulated.
32 devices in a mesh: dp: 4 (over z), ctx: 4 (over x, core), expert: 2 (over y).
Axes of the slice: x: 2, y: 2, z: 4, core: 2. Of those that a mesh axis runs over, the one named last changes fastest.
Arguments:
- tokens: bfloat16 [8, 2048, 768], P(('dp', 'expert'), 'ctx'), may hold values from -6 to 6
- cotangent: bfloat16 [8, 2048, 768], P(('dp', 'expert'), 'ctx'), may hold values from -6 to 6
- routes: int32 [8, 2048, 1], P(('dp', 'expert'), 'ctx'), may hold values from 0 to 3, as said below
- norm1_gain: float32 [768], replicated, may hold values from 0.5 to 1.5
- w_query: bfloat16 [768, 768], replicated, may hold values from -0.21875 to 0.21875
- w_key: bfloat16 [768, 768], replicated, may hold values from -0.21875 to 0.21875
- w_value: bfloat16 [768, 768], replicated, may hold values from -0.21875 to 0.21875
- w_output: bfloat16 [768, 768], replicated, may hold values from -1.75 to 1.75
- norm2_gain: float32 [768], replicated, may hold values from 0.5 to 1.5
- w_router: bfloat16 [768, 4], replicated, may hold values from -0.15625 to 0.15625
- w_in: bfloat16 [4, 768, 3072], P('expert'), may hold values from -0.21875 to 0.21875
- w_out: bfloat16 [4, 3072, 768], P('expert'), may hold values from -0.21875 to 0.21875
Outputs:
- output: bfloat16 [8, 2048, 768], P(('dp', 'expert'), 'ctx')
- grad_tokens: float32 [8, 2048, 768], P(('dp', 'expert'), 'ctx')
- grad_norm1: float32 [768], replicated
- grad_query: float32 [768, 768], replicated
- grad_key: float32 [768, 768], replicated
- grad_value: float32 [768, 768], replicated
- grad_output: float32 [768, 768], replicated
- grad_norm2: float32 [768], replicated
- grad_router: float32 [768, 4], replicated
- grad_in: float32 [4, 768, 3072], P('expert', None, ('dp', 'ctx'))
- grad_out: float32 [4, 3072, 768], P('expert', ('dp', 'ctx'))
- balance: float32 [], replicated
Inputs may be any that keep to these rules, and one draw needn't show every extreme that they name: `routes`: among the tokens of one device (an aligned block of 512 positions of one sequence) no expert is chosen more than 256 times, and in every such block some expert is chosen exactly 256 times.
All inputs are finite; a program needn't handle non-finite values.
Results may differ from a plain program's by a relative error of at most 0.024.
Values may be sent and summed in bfloat16 or wider, within the bound.
No kernel may reach another device: no remote copies, remote signals or barrier semaphores. Data moves between devices by JAX's collectives and lax.ppermute only.
A program may use at most 192 MiB of HBM per device.

v0:
```python
import math

import jax
import jax.numpy as jnp
from jax import lax
from jax.sharding import PartitionSpec as P

D = 768
HEADS = 12
HEAD_DIM = 64


norm_eps = 1e-05
masked_score = -1e30
balance_weight = 1.0


def layer_norm(inputs, scaling):
    centred = inputs - jnp.mean(inputs, axis=-1, keepdims=True)
    spread = jnp.mean(centred * centred, axis=-1, keepdims=True)
    return centred * lax.rsqrt(spread + norm_eps) * scaling


def fold_block(state_now, key_block, value_block, first_row, query_heads, query_place, score_scale):
    run_max, run_sum, run_acc = state_now
    block_rows = key_block.shape[0]
    key_heads = key_block.reshape(block_rows, HEADS, HEAD_DIM)
    value_heads = value_block.reshape(block_rows, HEADS, HEAD_DIM)
    scores = (
        jnp.einsum("qhd,khd->hqk", query_heads, key_heads, preferred_element_type=jnp.float32)
        * score_scale
    )
    key_place = first_row + jnp.arange(block_rows, dtype=jnp.int32)
    allowed = key_place[None, :] <= query_place[:, None]
    scores = jnp.where(allowed[None], scores, masked_score)
    new_max = jnp.maximum(run_max, jnp.max(scores, axis=-1))
    shrink = jnp.exp(run_max - new_max)
    weights = jnp.exp(scores - new_max[..., None])
    new_sum = run_sum * shrink + jnp.sum(weights, axis=-1)
    added = jnp.einsum(
        "hqk,khd->qhd",
        weights.astype(jnp.bfloat16),
        value_heads,
        preferred_element_type=jnp.float32,
    )
    new_acc = run_acc * jnp.transpose(shrink)[:, :, None] + added
    return (new_max, new_sum, new_acc)


def fold_piece(state_now, pieces, query_heads, query_place, score_scale):
    key_piece, value_piece = pieces
    piece_rows = key_piece.shape[0]
    block_rows = math.gcd(piece_rows, 512)
    block_count = piece_rows // block_rows

    def fold_scan_block(state_in, packed):
        key_block, value_block, offset = packed
        return (
            fold_block(
                state_in, key_block, value_block, offset, query_heads, query_place, score_scale
            ),
            None,
        )

    offsets = jnp.arange(block_count, dtype=jnp.int32) * block_rows
    state_out, unused = lax.scan(
        fold_scan_block,
        state_now,
        (
            key_piece.reshape(block_count, block_rows, -1),
            value_piece.reshape(block_count, block_rows, -1),
            offsets,
        ),
    )
    return state_out


def attention_back(
    query_heads, key_all, value_all, log_total, row_delta, grad_heads, query_place, score_scale
):
    length = key_all.shape[0]
    block_rows = math.gcd(length, 512)
    block_count = length // block_rows

    def attention_scan_block(grad_acc, packed):
        key_block, value_block, first_row = packed
        key_heads = key_block.reshape(block_rows, HEADS, HEAD_DIM)
        value_heads = value_block.reshape(block_rows, HEADS, HEAD_DIM)
        scores = (
            jnp.einsum("qhd,khd->hqk", query_heads, key_heads, preferred_element_type=jnp.float32)
            * score_scale
        )
        key_place = first_row + jnp.arange(block_rows, dtype=jnp.int32)
        allowed = key_place[None, :] <= query_place[:, None]
        probabilities = jnp.where(allowed[None], jnp.exp(scores - log_total[..., None]), 0.0)
        grad_probs = jnp.einsum(
            "qhd,khd->hqk", grad_heads, value_heads, preferred_element_type=jnp.float32
        )
        grad_scores = (probabilities * (grad_probs - row_delta[..., None])).astype(jnp.bfloat16)
        grad_acc = grad_acc + jnp.einsum(
            "hqk,khd->qhd", grad_scores, key_heads, preferred_element_type=jnp.float32
        )
        grad_keys = (
            jnp.einsum("hqk,qhd->khd", grad_scores, query_heads, preferred_element_type=jnp.float32)
            * score_scale
        )
        grad_values = jnp.einsum(
            "hqk,qhd->khd",
            probabilities.astype(jnp.bfloat16),
            grad_heads,
            preferred_element_type=jnp.float32,
        )
        return (grad_acc, (grad_keys.reshape(block_rows, -1), grad_values.reshape(block_rows, -1)))

    offsets = jnp.arange(block_count, dtype=jnp.int32) * block_rows
    start_acc = jnp.zeros(query_heads.shape, jnp.float32)
    grad_acc, (grad_keys, grad_values) = lax.scan(
        attention_scan_block,
        start_acc,
        (
            key_all.reshape(block_count, block_rows, -1),
            value_all.reshape(block_count, block_rows, -1),
            offsets,
        ),
    )
    return (grad_acc * score_scale, grad_keys.reshape(length, -1), grad_values.reshape(length, -1))


def per_device(
    tokens,
    cotangent,
    routes,
    norm1_gain,
    w_query,
    w_key,
    w_value,
    w_output,
    norm2_gain,
    w_router,
    w_in,
    w_out,
):
    tok_rows = tokens.shape[1]
    score_scale = HEAD_DIM ** (-0.5)
    flat_in = tokens.reshape(tok_rows, D).astype(jnp.float32)
    routes_flat = routes.reshape(tok_rows)
    experts_all = w_router.shape[1]
    per_dev = w_in.shape[0]
    owners = lax.axis_size("expert")
    capacity = 2 * tok_rows // experts_all
    normed_f, norm1_back = jax.vjp(layer_norm, flat_in, norm1_gain)
    normed = normed_f.astype(jnp.bfloat16)
    queries = jnp.dot(normed, w_query, preferred_element_type=jnp.float32).astype(jnp.bfloat16)
    key_rows = jnp.dot(normed, w_key, preferred_element_type=jnp.float32).astype(jnp.bfloat16)
    value_rows = jnp.dot(normed, w_value, preferred_element_type=jnp.float32).astype(jnp.bfloat16)
    query_heads = queries.reshape(tok_rows, HEADS, HEAD_DIM)
    query_place = lax.axis_index("ctx") * tok_rows + jnp.arange(tok_rows, dtype=jnp.int32)
    start_state = (
        jnp.full((HEADS, tok_rows), masked_score, jnp.float32),
        jnp.zeros((HEADS, tok_rows), jnp.float32),
        jnp.zeros((tok_rows, HEADS, HEAD_DIM), jnp.float32),
    )
    run_max, run_sum, run_acc = fold_piece(
        start_state,
        (
            lax.all_gather(key_rows, "ctx", axis=0, tiled=True),
            lax.all_gather(value_rows, "ctx", axis=0, tiled=True),
        ),
        query_heads,
        query_place,
        score_scale,
    )
    out_heads = run_acc / jnp.transpose(run_sum)[:, :, None]
    log_total = run_max + jnp.log(run_sum)
    attended = out_heads.reshape(tok_rows, D).astype(jnp.bfloat16)
    middle = flat_in + jnp.dot(attended, w_output, preferred_element_type=jnp.float32)
    second_f, norm2_back = jax.vjp(layer_norm, middle, norm2_gain)
    second = second_f.astype(jnp.bfloat16)
    logits = jnp.dot(second, w_router, preferred_element_type=jnp.float32)
    one_hot = routes_flat[:, None] == jnp.arange(experts_all, dtype=jnp.int32)[None, :]
    hot_float = one_hot.astype(jnp.float32)
    hot_int = one_hot.astype(jnp.int32)
    gating = jax.nn.sigmoid(jnp.sum(hot_float * logits, axis=1))
    slot_rank = jnp.sum((jnp.cumsum(hot_int, axis=0) - 1) * hot_int, axis=1)
    slot_index = routes_flat * capacity + slot_rank
    outgoing = (
        jnp.zeros((experts_all * capacity, D), jnp.bfloat16)
        .at[slot_index]
        .set(second)
        .reshape(owners, per_dev, capacity, D)
    )
    arrived_rows = lax.all_to_all(outgoing, "expert", split_axis=0, concat_axis=0, tiled=True)
    hidden_rows = jnp.einsum(
        "secd,edf->secf", arrived_rows, w_in, preferred_element_type=jnp.float32
    )
    active_rows = jax.nn.gelu(hidden_rows).astype(jnp.bfloat16)
    produced_rows = jnp.einsum(
        "secf,efd->secd", active_rows, w_out, preferred_element_type=jnp.float32
    ).astype(jnp.bfloat16)
    came_back = lax.all_to_all(produced_rows, "expert", split_axis=0, concat_axis=0, tiled=True)
    expert_tok = came_back.reshape(experts_all * capacity, D)[slot_index].astype(jnp.float32)
    output = (middle + gating[:, None] * expert_tok).astype(jnp.bfloat16)
    total_counts, total_sig = lax.psum(
        (jnp.sum(hot_float, axis=0), jnp.sum(hot_float * gating[:, None], axis=0)),
        ("dp", "ctx", "expert"),
    )
    total_tokens = tok_rows * lax.axis_size(("dp", "ctx", "expert"))
    mean_load = total_tokens / experts_all
    balance = (
        balance_weight * jnp.sum((total_counts - mean_load) / mean_load * total_sig) / mean_load
    )
    grad_flat = cotangent.reshape(tok_rows, D).astype(jnp.float32)
    grad_expert = (gating[:, None] * grad_flat).astype(jnp.bfloat16)
    grad_gating = jnp.sum(grad_flat * expert_tok, axis=1)
    load_term = balance_weight * (total_counts - mean_load) / (mean_load * mean_load)
    grad_select = (
        gating * (1.0 - gating) * (grad_gating + jnp.sum(hot_float * load_term[None, :], axis=1))
    )
    grad_logits = (hot_float * grad_select[:, None]).astype(jnp.bfloat16)
    grad_outgoing = (
        jnp.zeros((experts_all * capacity, D), jnp.bfloat16)
        .at[slot_index]
        .set(grad_expert)
        .reshape(owners, per_dev, capacity, D)
    )
    arrived, grad_arrived = (
        lax.all_to_all(outgoing, "expert", split_axis=0, concat_axis=0, tiled=True),
        lax.all_to_all(grad_outgoing, "expert", split_axis=0, concat_axis=0, tiled=True),
    )
    hidden = jnp.einsum("secd,edf->secf", arrived, w_in, preferred_element_type=jnp.float32)
    active = jax.nn.gelu(hidden).astype(jnp.bfloat16)
    grad_active = jnp.einsum(
        "secd,efd->secf", grad_arrived, w_out, preferred_element_type=jnp.float32
    )
    grad_hidden = jax.vjp(jax.nn.gelu, hidden)[1](grad_active)[0].astype(jnp.bfloat16)
    grad_dispatched = jnp.einsum(
        "secf,edf->secd", grad_hidden, w_in, preferred_element_type=jnp.float32
    ).astype(jnp.bfloat16)
    returned = lax.all_to_all(grad_dispatched, "expert", split_axis=0, concat_axis=0, tiled=True)
    part_in = jnp.einsum("secd,secf->edf", arrived, grad_hidden, preferred_element_type=jnp.float32)
    part_out = jnp.einsum(
        "secf,secd->efd", active, grad_arrived, preferred_element_type=jnp.float32
    )
    grad_in_w, grad_out_w = (
        lax.psum_scatter(
            part_in.astype(jnp.bfloat16), ("dp", "ctx"), scatter_dimension=2, tiled=True
        ).astype(jnp.float32),
        lax.psum_scatter(
            part_out.astype(jnp.bfloat16), ("dp", "ctx"), scatter_dimension=1, tiled=True
        ).astype(jnp.float32),
    )
    grad_second = returned.reshape(experts_all * capacity, D)[slot_index].astype(jnp.float32)
    grad_second = grad_second + jnp.einsum(
        "te,de->td", grad_logits, w_router, preferred_element_type=jnp.float32
    )
    grad_router_w = jnp.einsum("td,te->de", second, grad_logits, preferred_element_type=jnp.float32)
    grad_middle_norm, grad_gain_two = norm2_back(grad_second)
    grad_middle = grad_flat + grad_middle_norm
    grad_branch = grad_middle.astype(jnp.bfloat16)
    grad_out_proj = jnp.einsum(
        "td,te->de", attended, grad_branch, preferred_element_type=jnp.float32
    )
    grad_attended = jnp.einsum(
        "te,de->td", grad_branch, w_output, preferred_element_type=jnp.float32
    ).astype(jnp.bfloat16)
    grad_heads = grad_attended.reshape(tok_rows, HEADS, HEAD_DIM)
    row_delta = jnp.transpose(jnp.sum(grad_heads.astype(jnp.float32) * out_heads, axis=-1))
    key_back, value_back = (
        lax.all_gather(key_rows, "ctx", axis=0, tiled=True),
        lax.all_gather(value_rows, "ctx", axis=0, tiled=True),
    )
    grad_query_heads, grad_key_all, grad_value_all = attention_back(
        query_heads,
        key_back,
        value_back,
        log_total,
        row_delta,
        grad_heads,
        query_place,
        score_scale,
    )
    grad_key_rows, grad_value_rows = (
        lax.psum_scatter(
            grad_key_all.astype(jnp.bfloat16), "ctx", scatter_dimension=0, tiled=True
        ).astype(jnp.float32),
        lax.psum_scatter(
            grad_value_all.astype(jnp.bfloat16), "ctx", scatter_dimension=0, tiled=True
        ).astype(jnp.float32),
    )
    grad_queries = grad_query_heads.reshape(tok_rows, D).astype(jnp.bfloat16)
    grad_keys = grad_key_rows.astype(jnp.bfloat16)
    grad_values = grad_value_rows.astype(jnp.bfloat16)
    grad_q_w = jnp.einsum("td,te->de", normed, grad_queries, preferred_element_type=jnp.float32)
    grad_k_w = jnp.einsum("td,te->de", normed, grad_keys, preferred_element_type=jnp.float32)
    grad_v_w = jnp.einsum("td,te->de", normed, grad_values, preferred_element_type=jnp.float32)
    grad_normed = jnp.einsum("te,de->td", grad_queries, w_query, preferred_element_type=jnp.float32)
    grad_normed = grad_normed + jnp.einsum(
        "te,de->td", grad_keys, w_key, preferred_element_type=jnp.float32
    )
    grad_normed = grad_normed + jnp.einsum(
        "te,de->td", grad_values, w_value, preferred_element_type=jnp.float32
    )
    grad_input_norm, grad_gain_one = norm1_back(grad_normed)
    grad_input = grad_middle + grad_input_norm
    summed = lax.psum(
        (grad_q_w, grad_k_w, grad_v_w, grad_out_proj, grad_router_w, grad_gain_one, grad_gain_two),
        ("dp", "ctx", "expert"),
    )
    return (
        output.reshape(1, tok_rows, D),
        grad_input.reshape(1, tok_rows, D),
        summed[5],
        summed[0],
        summed[1],
        summed[2],
        summed[3],
        summed[6],
        summed[4],
        grad_in_w,
        grad_out_w,
        balance,
    )


def solution(mesh):
    return jax.shard_map(
        per_device,
        mesh=mesh,
        in_specs=(
            P(("dp", "expert"), "ctx", None),
            P(("dp", "expert"), "ctx", None),
            P(("dp", "expert"), "ctx", None),
            P(),
            P(),
            P(),
            P(),
            P(),
            P(),
            P(),
            P("expert", None, None),
            P("expert", None, None),
        ),
        out_specs=(
            P(("dp", "expert"), "ctx", None),
            P(("dp", "expert"), "ctx", None),
            P(),
            P(),
            P(),
            P(),
            P(),
            P(),
            P(),
            P("expert", None, ("dp", "ctx")),
            P("expert", ("dp", "ctx"), None),
            P(),
        ),
        check_vma=False,
    )
```

profile of v0, /device:TPU:0, one launch (start us, length us, event | category | flops | bytes accessed | tf_op | source)
XLA Modules:
  0.0 965.2 jit_solution(971982528564066759)
XLA Ops:
  21.2 23.5 %all-gather.5.cloned.1.call-done = bf16[2048,768]{1,0:T(8,128)(2,1)} async-done(((bf16[512,768]{1,0:T(8,128)(2,1)}), bf16[2048,768]{1,0:T(8,128)(2,1)}) %all-gather.5.cloned.1.call-update) | async-done | bytes 3145744 | tf_op jit(solution)/shard_map/all_gather | solution.py:167
  49.3 26.0 %all-gather.3.cloned.1.call-done = bf16[2048,768]{1,0:T(8,128)(2,1)} async-done(((bf16[512,768]{1,0:T(8,128)(2,1)}), bf16[2048,768]{1,0:T(8,128)(2,1)}) %all-gather.3.cloned.1.call-update) | async-done | bytes 3145744 | tf_op jit(solution)/shard_map/all_gather | solution.py:166
  80.0 51.2 %while.30 = (s32[]{:T(128)}, f32[12,512]{1,0:T(8,128)S(1)}, f32[12,512]{1,0:T(8,128)S(1)}, f32[512,12,64]{0,2,1:T(8,128)}, s32[4]{0:T(128)S(1)}, /*index=5*/bf16...) while((s32[]{:T(128)}, f32[12,512]{1,0:T(8,128)S(1)}, ...), condition=%wide.region_5.6_spmd.clone, body=%wide.region_2.5_spmd.clone.sunk | while | flops 841389056 | bytes 47849620 | solution.py:66
  99.6 5.4 bitcast_add_fusion.5
  112.7 5.4 bitcast_add_fusion.5
  125.8 5.4 bitcast_add_fusion.5
  151.5 12.2 %all-to-all-done = bf16[2,2,256,768]{3,2,1,0:T(8,128)(2,1)} async-done(((bf16[2,2,256,768]{3,2,1,0:T(8,128)(2,1)}), bf16[2,2,256,768]{3,2,1,0:T(8,128)(2,1)}, u32[]{:S(2)}, u32[]{:S(2)}) %all-to-all-start) | async-done | bytes 1572896 | tf_op jit(solution)/shard_map/all_to_all | solution.py:192
  168.3 8.1 fusion.36
  176.4 13.4 %fusion.74 = bf16[2,2,256,768]{3,2,0,1:T(8,128)(2,1)S(1)} fusion(bf16[2,3072,768]{2,1,0:T(8,128)(2,1)} %param.27, f32[2,2,256,3072]{3,2,1,0:T(8,128)S(1)} %fusion.36), kind=kOutput, calls=%fused_computation.112 | convolution fusion | flops 4860936192 | bytes 23592960 | tf_op jit(solution)/shard_map/secf,efd->secd/dot_general | solution.py:197
  195.7 17.9 %fusion.29 = bf16[2,2,256,3072]{3,2,0,1:T(8,128)(2,1)} fusion(f32[2,2,256,3072]{3,2,1,0:T(8,128)} %copy-done.60, bf16[2,3072,768]{2,1,0:T(8,128)(2,1)} %param.27, bf16[2,2,256,768]{3,2,1,0:T(8,128)(2,1)} %all-to-all-done.2), kind=kOutput, calls=%fused_computation.54 | convolution fusion | flops 4894752768 | bytes 29884416 | tf_op jit(solution)/shard_map/secd,efd->secf/dot_general | solution.py:232
  213.6 9.9 %fusion.71 = bf16[2,2,256,768]{3,2,0,1:T(8,128)(2,1)S(1)} fusion(bf16[2,2,256,3072]{3,2,0,1:T(8,128)(2,1)} %fusion.29, bf16[2,768,3072]{2,1,0:T(8,128)(2,1)} %param.26), kind=kOutput, calls=%fused_computation.111 | convolution fusion | flops 4832624640 | bytes 17301504 | tf_op jit(solution)/shard_map/secf,edf->secd/dot_general | solution.py:236
  224.8 4.7 all-to-all-start.3
  230.8 51.1 %psum.63 = f32[4]{0:T(128)} all-reduce(f32[4]{0:T(128)} %convert_reduce_fusion.1), channel_id=1, replica_groups=mesh['dp'=4,'ctx'=4,'expert'=2] {'dp','ctx','expert'}, use_global_device_ids=true, to_apply=%region_16.17 | all-reduce | flops 4 | bytes 32 | tf_op jit(solution)/shard_map/psum | solution.py:203
  285.4 4.8 gather_fusion
  292.5 4.8 gather_fusion.1
  310.7 127.8 %while.31 = (s32[]{:T(128)}, f32[512,12,64]{0,2,1:T(8,128)}, bf16[4,512,768]{2,1,0:T(8,128)(2,1)}, bf16[4,512,768]{2,1,0:T(8,128)(2,1)}, bf16[4,512,768]{1,2,0:T...) while((s32[]{:T(128)}, f32[512,12,64]{0,2,1:T(8,128)}, ...), condition=%wide.region_22.23_spmd.clone, body=%wide.region_21.22_spmd.clone.sunk | while | flops 2046559232 | bytes 115097976 | solution.py:117
  324.1 8.1 fusion.203
  333.7 5.2 bitcast_add_fusion.6
  355.7 8.1 fusion.203
  365.2 5.6 bitcast_add_fusion.6
  387.7 8.1 fusion.203
  397.3 5.6 bitcast_add_fusion.6
  419.7 8.1 fusion.203
  429.3 5.6 bitcast_add_fusion.6
  439.1 12.4 %bitcast_convert_fusion = bf16[2,3072,768]{2,1,0:T(8,128)(2,1)} fusion(bf16[2,2,256,768]{3,2,1,0:T(8,128)(2,1)} %all-to-all-done.2, f32[2,2,256,3072]{3,2,1,0:T(8,128)} %copy-done.60), kind=kOutput, calls=%fused_computation.44 | convolution fusion | flops 4864868352 | bytes 23592960 | tf_op jit(solution)/shard_map/secf,secd->efd/dot_general | solution.py:241
  451.6 9.9 %bitcast_convert_fusion.1 = bf16[2,768,3072]{1,2,0:T(8,128)(2,1)} fusion(bf16[2,2,256,768]{3,2,1,0:T(8,128)(2,1)} %all-to-all-done, bf16[2,2,256,3072]{3,2,0,1:T(8,128)(2,1)} %fusion.29), kind=kOutput, calls=%fused_computation.45 | convolution fusion | flops 4836556800 | bytes 17301504 | tf_op jit(solution)/shard_map/secd,secf->edf/dot_general | solution.py:240
  468.0 8.7 reduce-scatter.7.cloned.1.call-done
  480.2 37.0 %reduce-scatter.5.cloned.1.call-done = bf16[512,768]{1,0:T(8,128)(2,1)} async-done(((bf16[2048,768]{1,0:T(8,128)(2,1)}), bf16[512,768]{1,0:T(8,128)(2,1)}) %reduce-scatter.5.cloned.1.call-update) | async-done | bytes 786448 | tf_op jit(solution)/shard_map/reduce_scatter | solution.py:283
  527.9 40.3 %all-reduce = (f32[768]{0:T(1024)}, f32[768]{0:T(1024)}, f32[768,4]{0,1:T(4,128)}, f32[4]{0:T(128)S(1)}) all-reduce(f32[768]{0:T(1024)S(1)} %get-tuple-element.271, f32[768]{0:T(1024)S(1)} %copy-done.51, f32[768,4]{0,1:T(4,128)S(1)} %fusion.99, f32[4]{0:T(128)S(1)} %copy-done.54), channel_id=1, replica_groups=mesh['dp'=4,'ctx'=4,'expert'=2] {'dp','ctx','expert'}, use_global_device_ids=true, to_apply=%region_28.29 | all-reduce | flops 4612 | bytes 36896 | tf_op jit(solution)/shard_map/psum | solution.py:305
  572.7 60.1 %reduce-scatter.11.cloned.1.call-done = bf16[2,192,768]{2,1,0:T(8,128)(2,1)} async-done(((bf16[2,3072,768]{2,1,0:T(8,128)(2,1)}), bf16[2,192,768]{2,1,0:T(8,128)(2,1)}) %reduce-scatter.11.cloned.1.call-update) | async-done | bytes 589840 | tf_op jit(solution)/shard_map/reduce_scatter | solution.py:248
  634.9 113.5 %reduce-scatter.9.cloned.1.call-done = bf16[2,768,192]{1,2,0:T(8,128)(2,1)} async-done(((bf16[2,768,3072]{1,2,0:T(8,128)(2,1)}), bf16[2,768,192]{1,2,0:T(8,128)(2,1)}) %reduce-scatter.9.cloned.1.call-update) | async-done | bytes 589840 | tf_op jit(solution)/shard_map/reduce_scatter | solution.py:245
  750.5 196.4 %all-reduce.4.cloned.1.call-done = (f32[768,768]{1,0:T(8,128)}, f32[768,768]{1,0:T(8,128)}, f32[768,768]{1,0:T(8,128)}, f32[768,768]{1,0:T(8,128)}) async-done(((f32[768,768]{1,0:T(8,128)}, f32[768,768]{1,0:T(8,128)}, f32[768,768]{1,0:T(8,128)}, f32[768,768]{1,0:T(8,128)}), (f32[768,768]{1,0:T(8,128)}, f32[768,768]{1,0:T(8,128)}, f32[768,768]{1,0:T(8,128)}, ...) | async-done | bytes 9437200 | tf_op jit(solution)/shard_map/psum | solution.py:305
  (340 shorter events, 222.0 us)
Async XLA Ops:
  7.2 125.8 %copy-start = (bf16[768,768]{1,0:T(8,128)(2,1)S(1)}, bf16[768,768]{1,0:T(8,128)(2,1)}, u32[]{:S(2)}) copy-start(bf16[768,768]{1,0:T(8,128)(2,1)} %param.23) | copy-start | bytes 3538948
  7.2 37.5 %all-gather.5.cloned.1.call-start = ((), (), s32[]{:S(2)}) async-start(), calls=%async_computation.9 | async-start | bytes 3932160 | tf_op jit(solution)/shard_map/all_gather | solution.py:167
  8.7 9.4 copy-start.34
  10.3 7.8 copy-start.42
  13.3 62.1 %all-gather.3.cloned.1.call-start = ((), (), s32[]{:S(2)}) async-start(), calls=%async_computation.8 | async-start | bytes 3932160 | tf_op jit(solution)/shard_map/all_gather | solution.py:166
  139.1 24.6 %all-to-all-start = ((bf16[2,2,256,768]{3,2,1,0:T(8,128)(2,1)}), bf16[2,2,256,768]{3,2,1,0:T(8,128)(2,1)}, u32[]{:S(2)}, u32[]{:S(2)}) async-start(bf16[2,2,256,768]{3,2,1,0:T(8,128)(2,1)} %bitcast.296), calls=%async_computation | async-start | bytes 3145728 | tf_op jit(solution)/shard_map/all_to_all | solution.py:192
  163.7 27.4 %all-to-all-start.2 = ((bf16[2,2,256,768]{3,2,1,0:T(8,128)(2,1)}), bf16[2,2,256,768]{3,2,1,0:T(8,128)(2,1)}, u32[]{:S(2)}, u32[]{:S(2)}) async-start(bf16[2,2,256,768]{3,2,1,0:T(8,128)(2,1)} %bitcast.295), calls=%async_computation.2 | async-start | bytes 3145728 | tf_op jit(solution)/shard_map/all_to_all | solution.py:228
  176.4 13.4 %copy-start.60 = (f32[2,2,256,3072]{3,2,1,0:T(8,128)}, f32[2,2,256,3072]{3,2,1,0:T(8,128)S(1)}, u32[]{:S(2)}) copy-start(f32[2,2,256,3072]{3,2,1,0:T(8,128)S(1)} %fusion.36) | copy-start | bytes 37748740
  191.1 33.8 %all-to-all-start.1 = ((bf16[2,2,256,768]{3,2,1,0:T(8,128)(2,1)}), bf16[2,2,256,768]{3,2,1,0:T(8,128)(2,1)}, u32[]{:S(2)}, u32[]{:S(2)}) async-start(bf16[2,2,256,768]{3,2,1,0:T(8,128)(2,1)} %copy.64), calls=%async_computation.1 | async-start | bytes 3145728 | tf_op jit(solution)/shard_map/all_to_all | solution.py:200
  224.8 67.7 %all-to-all-start.3 = ((bf16[2,2,256,768]{3,2,1,0:T(8,128)(2,1)}), bf16[2,2,256,768]{3,2,1,0:T(8,128)(2,1)}, u32[]{:S(2)}, u32[]{:S(2)}) async-start(bf16[2,2,256,768]{3,2,1,0:T(8,128)(2,1)} %copy.66), calls=%async_computation.3 | async-start | bytes 3145728 | tf_op jit(solution)/shard_map/all_to_all | solution.py:239
  229.5 247.2 %reduce-scatter.7.cloned.1.call-start = ((), (), s32[]{:S(2)}) async-start(), calls=%async_computation.11 | async-start | bytes 3932160 | tf_op jit(solution)/shard_map/reduce_scatter | solution.py:286
  310.9 4.8 copy-start.5
  333.7 5.2 copy-start.4
  333.7 5.2 copy-start.6
  342.4 4.8 copy-start.5
  351.1 4.5 copy-start.39
  365.2 5.6 copy-start.4
  365.2 5.6 copy-start.6
  374.5 4.8 copy-start.5
  397.3 5.6 copy-start.4
  397.3 5.6 copy-start.6
  406.5 4.8 copy-start.5
  415.2 4.5 copy-start.39
  429.3 5.6 copy-start.4
  429.3 5.6 copy-start.6
  438.5 78.8 %reduce-scatter.5.cloned.1.call-start = ((), (), s32[]{:S(2)}) async-start(), calls=%async_computation.10 | async-start | bytes 3932160 | tf_op jit(solution)/shard_map/reduce_scatter | solution.py:283
  439.1 193.6 %reduce-scatter.11.cloned.1.call-start = ((), (), s32[]{:S(2)}) async-start(), calls=%async_computation.13 | async-start | bytes 10027008 | tf_op jit(solution)/shard_map/reduce_scatter | solution.py:248
  451.5 296.8 %reduce-scatter.9.cloned.1.call-start = ((), (), s32[]{:S(2)}) async-start(), calls=%async_computation.12 | async-start | bytes 10027008 | tf_op jit(solution)/shard_map/reduce_scatter | solution.py:245
  461.5 485.4 %all-reduce.4.cloned.1.call-start = ((), (), s32[]{:S(2)}) async-start(), calls=%async_computation.14 | async-start | bytes 18874368 | tf_op jit(solution)/shard_map/psum | solution.py:305
  527.0 41.2 %copy-start.59 = (f32[4]{0:T(128)S(1)}, f32[4]{0:T(128)}, u32[]{:S(2)}) copy-start(f32[4]{0:T(128)} %psum.63) | copy-start | bytes 52
  527.0 42.4 %copy-start.13 = (bf16[1,512,768]{2,1,0:T(8,128)(2,1)S(1)}, bf16[1,512,768]{2,1,0:T(8,128)(2,1)}, u32[]{:S(2)}) copy-start(bf16[1,512,768]{2,1,0:T(8,128)(2,1)} %param.17) | copy-start | bytes 2359300
  527.0 42.4 %copy-start.45 = (f32[512]{0:T(512)S(1)}, f32[512]{0:T(512)}, u32[]{:S(2)}) copy-start(f32[512]{0:T(512)} %copy-done.44) | copy-start | bytes 6148
  (61 other events, 118.5 us)
Sparse Core Ops, SparseCore 0:
  13.4 31.2 all-gather.4
  46.8 28.5 all-gather.2
  438.6 38.0 reduce-scatter.6
  479.3 37.9 reduce-scatter.4
  521.2 111.4 reduce-scatter.10
  637.2 111.0 reduce-scatter.8
  755.2 191.6 all-reduce.3
where the time goes:
time: 978 us; the launch traced here: 965 us
  waiting for transfers between devices  478 us (49%)
  matrix products  222 us (23%)
  blocking collectives  91.4 us (9%)
  local copies, waits for them, and re-layouts  81 us (8%)
  other arithmetic  55.5 us (6%)
  starting transfers between devices  19.1 us (2%)
  between operations  17.1 us (2%)
    psum x1, waiting for transfers between devices, per_device(): lax.psum((grad_q_w, grad_k_w, grad_v_w, grad_out_proj, grad_router_w, gra...  196 us
    reduce_scatter x1, waiting for transfers between devices, per_device(): lax.psum_scatter(part_in.astype(jnp.bfloat16), ('dp', 'ctx'), scatter_dim...  113 us
    reduce_scatter x1, waiting for transfers between devices, per_device(): lax.psum_scatter(part_out.astype(jnp.bfloat16), ('dp', 'ctx'), scatter_di...  60.1 us
    psum x1, blocking collectives, per_device(): lax.psum((jnp.sum(hot_float, axis=0), jnp.sum(hot_float * gating[:, None]...  51.1 us
    psum x1, blocking collectives, per_device(): lax.psum((grad_q_w, grad_k_w, grad_v_w, grad_out_proj, grad_router_w, gra...  40.3 us
    reduce_scatter x1, waiting for transfers between devices, per_device(): lax.psum_scatter(grad_key_all.astype(jnp.bfloat16), 'ctx', scatter_dimens...  37 us
    dot_general x4, matrix products, attention_scan_block(): jnp.einsum('qhd,khd->hqk', grad_heads, value_heads, preferred_element_typ...  32.2 us
    unnamed x114, local copies, waits for them, and re-layouts  26.2 us
  transfers between devices with their start and end apart: 11, of which 8 were waited for; matrix products, arithmetic and copies ran while one was open for 13% of the time, Pallas kernels for 0%

commit v1 on v0

v1 whole, which is shorter than its diff:
```python
import functools

import jax
import jax.numpy as jnp
from jax import lax
from jax.experimental import pallas as pl
from jax.experimental.pallas import tpu as pltpu
from jax.sharding import Mesh
from jax.sharding import PartitionSpec as P

D = 768
HEADS = 12
HD = 64
norm_eps = 1e-05
balance_weight = 1.0
LOG2E = 1.4426950408889634
MASKED = -1e30
GELU_A = 0.7978845608028654
GELU_B = 0.044715
VMEM = 56 * 1024 * 1024
f32 = jnp.float32
bf16 = jnp.bfloat16


def dg(a, b, ca, cb):
    return lax.dot_general(a, b, (((ca,), (cb,)), ((), ())), preferred_element_type=f32)


def attend_kernel(lane, blk, qT_ref, k_ref, vT_ref, oT_ref, osend_ref, lse_ref):
    length = qT_ref.shape[1]
    per = osend_ref.shape[2]
    c = (HD**-0.5) * LOG2E
    rows = lax.broadcasted_iota(jnp.int32, (blk, blk), 0)
    cols = lax.broadcasted_iota(jnp.int32, (blk, blk), 1)
    keep = rows <= cols
    for i in range(length // blk):
        a, b = i * blk, (i + 1) * blk
        q = qT_ref[:, a:b]
        sd = dg(k_ref[a:b, lane : lane + HD], q, 1, 0)
        sd = jnp.where(keep, sd, MASKED)
        m = jnp.max(sd, axis=0, keepdims=True)
        if i:
            s = dg(k_ref[:a, lane : lane + HD], q, 1, 0)
            m = jnp.maximum(m, jnp.max(s, axis=0, keepdims=True))
        mc = m * c
        pd = jnp.exp2(sd * c - mc)
        total = jnp.sum(pd, axis=0, keepdims=True)
        o = dg(vT_ref[:, a:b], pd.astype(bf16), 1, 0)
        if i:
            p = jnp.exp2(s * c - mc)
            total = total + jnp.sum(p, axis=0, keepdims=True)
            o = o + dg(vT_ref[:, :a], p.astype(bf16), 1, 0)
        o = o / total
        oT_ref[:, a:b] = o
        d, off = a // per, a % per
        osend_ref[d, :, off : off + blk] = o.astype(bf16)
        lse_ref[:, a:b] = mc + jnp.log2(total)


def attend(qkvT, kv, h, dests):
    length = kv.shape[0]
    n = qkvT.shape[0] // (3 * HD)
    blk = length // dests
    return pl.pallas_call(
        functools.partial(attend_kernel, (h % 2) * HD, blk),
        out_shape=(
            jax.ShapeDtypeStruct((HD, length), f32),
            jax.ShapeDtypeStruct((dests, HD, length // dests), bf16),
            jax.ShapeDtypeStruct((1, length), f32),
        ),
        grid=(1,),
        in_specs=[
            pl.BlockSpec((HD, length), lambda i: (h, 0)),
            pl.BlockSpec((length, 2 * HD), lambda i: (0, h // 2)),
            pl.BlockSpec((HD, length), lambda i: (2 * n + h, 0)),
        ],
        out_specs=(
            pl.BlockSpec((HD, length), lambda i: (0, 0)),
            pl.BlockSpec((dests, HD, length // dests), lambda i: (0, 0, 0)),
            pl.BlockSpec((1, length), lambda i: (0, 0)),
        ),
        compiler_params=pltpu.CompilerParams(vmem_limit_bytes=VMEM),
        cost_estimate=pl.CostEstimate(
            flops=8 * length * length * HD, bytes_accessed=length * HD * 14, transcendentals=length * length // 2
        ),
        name=f"attend_head{h}",
    )(qkvT, kv, qkvT)


def attend_back_kernel(
    lk, lv, blk, qT_ref, k_ref, kT_ref, v_ref, do_ref, oT_ref, lse_ref, dT_ref, dsend_ref, dk_acc, dv_acc
):
    length = qT_ref.shape[1]
    per = do_ref.shape[2]
    sc = HD**-0.5
    c = sc * LOG2E
    rows = lax.broadcasted_iota(jnp.int32, (blk, blk), 0)
    cols = lax.broadcasted_iota(jnp.int32, (blk, blk), 1)
    keep = rows <= cols
    n = length // blk
    for i in reversed(range(n)):
        x0, x1 = i * blk, (i + 1) * blk
        d, off = x0 // per, x0 % per
        q = qT_ref[:, x0:x1]
        do = do_ref[d, :, off : off + blk]
        lse = lse_ref[:, x0:x1]
        delta = jnp.sum(do.astype(f32) * oT_ref[:, x0:x1], axis=0, keepdims=True)
        dq = None
        for a, b, diag in ([(0, x0, False)] if i else []) + [(x0, x1, True)]:
            s = dg(k_ref[a:b, lk : lk + HD], q, 1, 0)
            p = jnp.exp2(s * c - lse)
            if diag:
                p = jnp.where(keep, p, 0.0)
            dp = dg(v_ref[a:b, lv : lv + HD], do, 1, 0)
            ds = (p * (dp - delta)).astype(bf16)
            dvn = dg(do, p.astype(bf16), 1, 1)
            dkn = dg(q, ds, 1, 1)
            if i == n - 1:
                dv_acc[:, a:b] = dvn
                dk_acc[:, a:b] = dkn
            else:
                dv_acc[:, a:b] += dvn
                dk_acc[:, a:b] += dkn
            t = dg(kT_ref[:, a:b], ds, 1, 0)
            dq = t if dq is None else dq + t
        dq = (dq * sc).astype(bf16)
        dT_ref[0:HD, x0:x1] = dq
        dsend_ref[d, 0:HD, off : off + blk] = dq
    for d in range(dsend_ref.shape[0]):
        dk = (dk_acc[:, d * per : (d + 1) * per] * sc).astype(bf16)
        dv = dv_acc[:, d * per : (d + 1) * per].astype(bf16)
        dT_ref[HD : 2 * HD, d * per : (d + 1) * per] = dk
        dT_ref[2 * HD : 3 * HD, d * per : (d + 1) * per] = dv
        dsend_ref[d, HD : 2 * HD, :] = dk
        dsend_ref[d, 2 * HD : 3 * HD, :] = dv


def attend_back(qkvT, kv, do, oT, lse, h):
    length = kv.shape[0]
    n = qkvT.shape[0] // (3 * HD)
    dests, _, per = do.shape
    hv = n + h
    blk = min(256, per)
    return pl.pallas_call(
        functools.partial(attend_back_kernel, (h % 2) * HD, (hv % 2) * HD, blk),
        out_shape=(
            jax.ShapeDtypeStruct((3 * HD, length), bf16),
            jax.ShapeDtypeStruct((dests, 3 * HD, per), bf16),
        ),
        grid=(1,),
        in_specs=[
            pl.BlockSpec((HD, length), lambda i: (h, 0)),
            pl.BlockSpec((length, 2 * HD), lambda i: (0, h // 2)),
            pl.BlockSpec((HD, length), lambda i: (n + h, 0)),
            pl.BlockSpec((length, 2 * HD), lambda i: (0, hv // 2)),
            pl.BlockSpec((dests, HD, per), lambda i: (0, 0, 0)),
            pl.BlockSpec((HD, length), lambda i: (0, 0)),
            pl.BlockSpec((1, length), lambda i: (0, 0)),
        ],
        out_specs=(
            pl.BlockSpec((3 * HD, length), lambda i: (0, 0)),
            pl.BlockSpec((dests, 3 * HD, per), lambda i: (0, 0, 0)),
        ),
        scratch_shapes=[pltpu.VMEM((HD, length), f32)] * 2,
        compiler_params=pltpu.CompilerParams(vmem_limit_bytes=VMEM),
        cost_estimate=pl.CostEstimate(
            flops=20 * length * length * HD, bytes_accessed=length * HD * 24, transcendentals=length * length // 2
        ),
        name=f"attend_back_head{h}",
    )(qkvT, kv, qkvT, kv, do, oT, lse)


def up_kernel(pick_ref, dy_ref, wo_ref, u_ref):
    u_ref[...] = dg(dy_ref[...], wo_ref[0], 1, 1).astype(bf16)


def expert_up(pick, dy, w_out, fc=768):
    rows = dy.shape[0]
    ff = w_out.shape[1]
    return pl.pallas_call(
        up_kernel,
        out_shape=jax.ShapeDtypeStruct((rows, ff), bf16),
        grid_spec=pltpu.PrefetchScalarGridSpec(
            num_scalar_prefetch=1,
            grid=(ff // fc,),
            in_specs=[
                pl.BlockSpec((rows, D), lambda f, p: (0, 0)),
                pl.BlockSpec((1, fc, D), lambda f, p: (p[0], f, 0)),
            ],
            out_specs=pl.BlockSpec((rows, fc), lambda f, p: (0, f)),
        ),
        compiler_params=pltpu.CompilerParams(vmem_limit_bytes=VMEM),
        cost_estimate=pl.CostEstimate(
            flops=2 * rows * D * ff, bytes_accessed=2 * (rows * D + ff * D + rows * ff), transcendentals=0
        ),
        name="expert_up",
    )(pick, dy, w_out)


def mid_kernel(
    pick_ref, x_ref, u_ref, wi_ref, wr_ref, load_ref, act_ref, gh_ref, rows_ref, router_ref, gate_ref, acc, gg, gate
):
    f = pl.program_id(0)
    n = pl.num_programs(0)

    @pl.when(f == 0)
    def _():
        logit = jnp.sum(x_ref[...].astype(f32) * wr_ref[...], axis=1, keepdims=True)
        gate[...] = jnp.broadcast_to(jax.nn.sigmoid(logit), gate.shape)

    h = dg(x_ref[...], wi_ref[0], 1, 0)
    h2 = h * h
    t = jnp.tanh(h * (GELU_A + (GELU_A * GELU_B) * h2))
    hp = 0.5 + 0.5 * t
    dgelu = hp + (0.5 * h) * (1.0 - t * t) * (GELU_A + (3.0 * GELU_A * GELU_B) * h2)
    u = u_ref[...].astype(f32)
    act = (h * hp).astype(bf16)
    act_ref[...] = act
    g1 = jnp.sum(act.astype(f32) * u, axis=1, keepdims=True)
    gh = (gate[:, :1] * u * dgelu).astype(bf16)
    gh_ref[...] = gh
    part = dg(gh, wi_ref[0], 1, 1)

    @pl.when(f == 0)
    def _():
        acc[...] = part
        gg[...] = jnp.broadcast_to(g1, gg.shape)

    @pl.when(f > 0)
    def _():
        acc[...] += part
        gg[...] += g1

    @pl.when(f == n - 1)
    def _():
        g = gate[:, :1]
        sel = (g * (1.0 - g) * (gg[:, :1] + load_ref[:, :1])).astype(bf16).astype(f32)
        rows_ref[...] = (acc[...] + sel * wr_ref[...]).astype(bf16)
        router_ref[...] = jnp.sum(x_ref[...].astype(f32) * sel, axis=0, keepdims=True)
        gate_ref[...] = gate[...]


def expert_mid(pick, x, u, w_in, wr, load, fc=768):
    rows = x.shape[0]
    ff = w_in.shape[2]

    def full(s):
        return pl.BlockSpec(s, lambda f, p: (0, 0))

    wide = pl.BlockSpec((rows, fc), lambda f, p: (0, f))
    return pl.pallas_call(
        mid_kernel,
        out_shape=(
            jax.ShapeDtypeStruct((rows, ff), bf16),
            jax.ShapeDtypeStruct((rows, ff), bf16),
            jax.ShapeDtypeStruct((rows, D), bf16),
            jax.ShapeDtypeStruct((1, D), f32),
            jax.ShapeDtypeStruct((rows, 128), f32),
        ),
        grid_spec=pltpu.PrefetchScalarGridSpec(
            num_scalar_prefetch=1,
            grid=(ff // fc,),
            in_specs=[
                full((rows, D)),
                wide,
                pl.BlockSpec((1, D, fc), lambda f, p: (p[0], 0, f)),
                full((1, D)),
                full((1, 128)),
            ],
            out_specs=(wide, wide, full((rows, D)), full((1, D)), full((rows, 128))),
            scratch_shapes=[
                pltpu.VMEM((rows, D), f32),
                pltpu.VMEM((rows, 128), f32),
                pltpu.VMEM((rows, 128), f32),
            ],
        ),
        compiler_params=pltpu.CompilerParams(vmem_limit_bytes=VMEM),
        cost_estimate=pl.CostEstimate(
            flops=4 * rows * D * ff,
            bytes_accessed=2 * (3 * rows * D + ff * D + 3 * rows * ff),
            transcendentals=rows * ff,
        ),
        name="expert_mid",
    )(pick, x, u, w_in, wr, load)


def grads_kernel(
    pick_ref, x_ref, dy_ref, gate_ref, act_ref, gh_ref, wo_ref, keep_ref, send_ref, prod_ref, acc, go, gi, gexp
):
    f = pl.program_id(0)
    n = pl.num_programs(0)

    @pl.when(f == 0)
    def _():
        gexp[...] = (dy_ref[...].astype(f32) * gate_ref[:, :1]).astype(bf16)

    go[...] = dg(act_ref[...], gexp[...], 0, 0).astype(bf16)
    gi[...] = dg(gh_ref[...], x_ref[...], 0, 0).astype(bf16)
    part = dg(act_ref[...], wo_ref[0], 1, 0)

    @pl.when(f == 0)
    def _():
        acc[...] = part

    @pl.when(f > 0)
    def _():
        acc[...] += part

    w = keep_ref.shape[3]
    me = pick_ref[1]
    for xx in range(keep_ref.shape[2]):
        a = pl.multiple_of((2 * xx + me) * w, w)
        b = pl.multiple_of((2 * xx + 1 - me) * w, w)
        keep_ref[0, 0, xx] = gi[pl.ds(a, w)]
        keep_ref[0, 1, xx] = go[pl.ds(a, w)]
        send_ref[0, 0, xx] = gi[pl.ds(b, w)]
        send_ref[0, 1, xx] = go[pl.ds(b, w)]

    @pl.when(f == n - 1)
    def _():
        prod_ref[...] = acc[...].astype(bf16)


def expert_grads(pick, x, dy, gate, act, gh, w_out, dp, nx):
    rows = x.shape[0]
    ff = w_out.shape[1]
    fc = ff // dp
    w = fc // (2 * nx)

    def full(s):
        return pl.BlockSpec(s, lambda f, p: (0, 0))

    wide = pl.BlockSpec((rows, fc), lambda f, p: (0, f))
    part = jax.ShapeDtypeStruct((dp, 2, nx, w, D), bf16)
    part_spec = pl.BlockSpec((1, 2, nx, w, D), lambda f, p: (f, 0, 0, 0, 0))
    return pl.pallas_call(
        grads_kernel,
        out_shape=(part, part, jax.ShapeDtypeStruct((rows, D), bf16)),
        grid_spec=pltpu.PrefetchScalarGridSpec(
            num_scalar_prefetch=1,
            grid=(dp,),
            in_specs=[
                full((rows, D)),
                full((rows, D)),
                full((rows, 128)),
                wide,
                wide,
                pl.BlockSpec((1, fc, D), lambda f, p: (p[0], f, 0)),
            ],
            out_specs=(part_spec, part_spec, full((rows, D))),
            scratch_shapes=[
                pltpu.VMEM((rows, D), f32),
                pltpu.VMEM((fc, D), bf16),
                pltpu.VMEM((fc, D), bf16),
                pltpu.VMEM((rows, D), bf16),
            ],
        ),
        compiler_params=pltpu.CompilerParams(vmem_limit_bytes=VMEM),
        cost_estimate=pl.CostEstimate(
            flops=6 * rows * D * ff,
            bytes_accessed=2 * (3 * rows * D + 3 * ff * D + 2 * rows * ff),
            transcendentals=0,
        ),
        name="expert_grads",
    )(pick, x, dy, gate, act, gh, w_out)


def swap(v, axis):
    return lax.ppermute(v, axis, [(0, 1), (1, 0)])


def shift(v, axis, step):
    n = lax.axis_size(axis)
    return lax.ppermute(v, axis, [(i, (i + step) % n) for i in range(n)])


def at(v, index):
    return lax.dynamic_index_in_dim(v, index, 0, keepdims=False)


def place(pieces, n):
    out = jnp.zeros((n,) + pieces[0][1].shape, pieces[0][1].dtype)
    for index, piece in pieces:
        out = lax.dynamic_update_index_in_dim(out, piece, index, 0)
    return out


def gather_shifts(v, axis):
    n = lax.axis_size(axis)
    me = lax.axis_index(axis)
    return place([(me, v)] + [((me - s) % n, shift(v, axis, s)) for s in range(1, n)], n)


def sum_all(v):
    v = v + swap(v, "core")
    v = v + swap(v, "x")
    v = v + swap(v, "expert") if lax.axis_size("expert") == 2 else lax.psum(v, "expert")
    out = v
    for s in range(1, lax.axis_size("dp")):
        out = out + shift(v, "dp", s)
    return out


def scatter_sum(v):
    e = lax.axis_size("expert")
    if e == 2:
        me = lax.axis_index("expert")
        halves = v.reshape(2, -1, D)
        v = at(halves, me) + swap(at(halves, 1 - me).astype(bf16), "expert").astype(f32)
    else:
        v = lax.psum_scatter(v.astype(bf16), "expert", scatter_dimension=0, tiled=True).astype(f32)
    n = lax.axis_size("dp")
    me = lax.axis_index("dp")
    parts = v.reshape(n, -1, D)
    out = at(parts, me)
    for s in range(1, n):
        out = out + shift(at(parts, (me + s) % n).astype(bf16), "dp", s).astype(f32)
    return out


def gather_back(v):
    v = gather_shifts(v, "dp")
    v = v.reshape((-1,) + v.shape[2:])
    if lax.axis_size("expert") == 2:
        v = gather_shifts(v, "expert")
    else:
        v = lax.all_gather(v, "expert")
    v = v.reshape((-1,) + v.shape[2:])
    v = gather_shifts(v, "x")
    v = gather_shifts(v, "core")
    return jnp.swapaxes(v, 0, 1)


def ring_scatter(parts):
    n = lax.axis_size("dp")
    me = lax.axis_index("dp")
    moving = at(parts, (me - 1) % n)
    for s in range(n - 1):
        moving = shift(moving, "dp", 1)
        moving = moving.astype(f32) + at(parts, (me - 2 - s) % n).astype(f32)
        if s < n - 2:
            moving = moving.astype(bf16)
    return moving


def normal_form(v):
    centred = v - jnp.mean(v, axis=-1, keepdims=True)
    rstd = lax.rsqrt(jnp.mean(centred * centred, axis=-1, keepdims=True) + norm_eps)
    return centred * rstd, rstd


def norm_back(dn, xh, rstd):
    return rstd * (dn - jnp.mean(dn, axis=-1, keepdims=True) - xh * jnp.mean(dn * xh, axis=-1, keepdims=True))


def per_device(
    tokens,
    cotangent,
    routes,
    norm1_gain,
    w_query,
    w_key,
    w_value,
    w_output,
    norm2_gain,
    w_router,
    w_in,
    w_out,
):
    rows = tokens.shape[1]
    nx, owners, dp = lax.axis_size("x"), lax.axis_size("expert"), lax.axis_size("dp")
    xi, ci, ei = lax.axis_index("x"), lax.axis_index("core"), lax.axis_index("expert")
    ctx = 2 * nx
    ctx_i = xi * 2 + ci
    length = ctx * rows
    experts = w_router.shape[1]
    cap = 2 * rows // experts
    mine = D // ctx
    heads = mine // HD
    pick = jnp.stack([xi, ci]).astype(jnp.int32)

    flat = tokens.reshape(rows, D).astype(f32)
    xh1, rstd1 = normal_form(flat)
    normed = (xh1 * norm1_gain).astype(bf16)
    other = swap(normed, "x")
    near, far = swap(normed, "core"), swap(other, "core")
    normed_all = place(
        [(ctx_i, normed), (ctx_i ^ 1, near), (ctx_i ^ 2, other), (ctx_i ^ 3, far)], ctx
    ).reshape(length, D)

    route = routes.reshape(rows)
    hot = (route[:, None] == jnp.arange(experts, dtype=jnp.int32)[None, :]).astype(f32)
    lower = jnp.arange(rows)[:, None] >= jnp.arange(rows)[None, :]
    before = dg(lower.astype(bf16), hot.astype(bf16), 1, 0)
    rank = (jnp.sum(before * hot, axis=1) - 1.0).astype(jnp.int32)
    slot = ((route % nx) * owners + route // nx) * cap + rank
    spread = (jnp.arange(experts * cap, dtype=jnp.int32)[:, None] == slot[None, :]).astype(bf16)

    def dispatch(v):
        out = dg(spread, v, 1, 0).astype(bf16).reshape(nx * owners, cap, D)
        out = lax.all_to_all(out, ("x", "expert"), split_axis=0, concat_axis=0, tiled=True)
        return out.reshape(-1, D)

    def give_back(v):
        v = v.reshape(nx * owners, cap, D)
        v = lax.all_to_all(v, ("x", "expert"), split_axis=0, concat_axis=0, tiled=True)
        return dg(spread, v.reshape(-1, D), 0, 0)

    dy_low = cotangent.reshape(rows, D)
    dy = dy_low.astype(f32)
    dy_rows = dispatch(dy_low)
    counts = sum_all(jnp.sum(hot, axis=0))
    mean_load = rows * ctx * dp * owners / experts
    load_term = balance_weight * (counts - mean_load) / (mean_load * mean_load)
    expert_id = ei * nx + xi
    load = jnp.broadcast_to(lax.dynamic_slice(load_term, (expert_id,), (1,)).reshape(1, 1), (1, 128))
    wr = lax.dynamic_slice(w_router, (0, expert_id), (D, 1)).astype(f32).reshape(1, D)

    def cut(w):
        return lax.dynamic_slice(w, (0, ctx_i * mine), (D, mine))

    wq, wk, wv = cut(w_query), cut(w_key), cut(w_value)
    qkvT = dg(jnp.concatenate([wq, wk, wv], axis=1), normed_all, 0, 1).astype(bf16)
    kv = dg(normed_all, jnp.concatenate([wk, wv], axis=1), 1, 0).astype(bf16)
    kept, arrived = [], []
    for h in range(heads):
        oT, osend, lse = attend(qkvT, kv, h, ctx)
        kept.append((oT, lse))
        arrived.append(lax.all_to_all(osend, ("x", "core"), split_axis=0, concat_axis=0, tiled=True))
    attT = jnp.stack(arrived, axis=1).reshape(D, rows)

    middle = flat + dg(attT, w_output, 0, 0)
    xh2, rstd2 = normal_form(middle)
    second = (xh2 * norm2_gain).astype(bf16)
    gating = jax.nn.sigmoid(jnp.sum(hot * dg(second, w_router, 1, 0), axis=1))

    up = expert_up(pick, dy_rows, w_out)
    x_rows = dispatch(second)
    active, grad_hidden, back_rows, router_row, gate = expert_mid(pick, x_rows, up, w_in, wr, load)
    grad_second = give_back(back_rows)
    keep, send, produced = expert_grads(pick, x_rows, dy_rows, gate, active, grad_hidden, w_out, dp, nx)
    output = (middle + gating[:, None] * give_back(produced)).astype(bf16)

    pair = (keep.astype(f32) + swap(send, "core").astype(f32)).astype(bf16)
    ringed = ring_scatter(pair)
    own = lax.dynamic_index_in_dim(ringed, xi, 1, keepdims=False)
    moved = swap(lax.dynamic_index_in_dim(ringed, 1 - xi, 1, keepdims=False).astype(bf16), "x").astype(f32)
    first, latter = jnp.where(xi == 0, own, moved), jnp.where(xi == 0, moved, own)
    both = jnp.stack([first, latter], axis=1)
    grad_in = jnp.swapaxes(both[0], 1, 2)
    grad_out = both[1]

    grad_middle = dy + norm_back(grad_second * norm2_gain, xh2, rstd2)
    branch = grad_middle.astype(bf16)
    go = dg(attT, branch, 1, 0)
    go = go.reshape(nx, 2, mine, D)
    go_keep = lax.dynamic_index_in_dim(go, ci, 1, keepdims=False)
    go_send = lax.dynamic_index_in_dim(go, 1 - ci, 1, keepdims=False).astype(bf16)
    go = go_keep + swap(go_send, "core").astype(f32)
    go = at(go, xi) + swap(at(go, 1 - xi).astype(bf16), "x").astype(f32)
    attT_grad = dg(w_output, branch, 1, 1).astype(bf16).reshape(ctx, heads, HD, rows)

    grad_normed = 0.0
    weight_rows = []
    for h in range(heads):
        do = lax.all_to_all(attT_grad[:, h], ("x", "core"), split_axis=0, concat_axis=0, tiled=True)
        dT, dsend = attend_back(qkvT, kv, do, kept[h][0], kept[h][1], h)
        got = lax.all_to_all(dsend, ("x", "core"), split_axis=0, concat_axis=0, tiled=True)
        wide = jnp.stack([w.reshape(D, ctx, heads, HD)[:, :, h] for w in (w_query, w_key, w_value)], axis=2)
        grad_normed = grad_normed + dg(got.reshape(-1, rows), wide.reshape(D, -1), 0, 1)
        weight_rows.append(dg(dT, normed_all, 1, 0))
    grad_tokens = grad_middle + norm_back(grad_normed * norm1_gain, xh1, rstd1)

    shared = gather_back(scatter_sum(jnp.concatenate(weight_rows + [go], axis=0)).astype(bf16))
    sides = shared[:, :, : 3 * mine].reshape(nx, 2, heads, 3, HD, D)
    grads = []
    for p in range(3):
        grads.append(jnp.transpose(sides[:, :, :, p].reshape(D, D)).astype(f32))
    grad_output = shared[:, :, 3 * mine :].reshape(D, D).astype(f32)
    grad_norm1 = 0.0
    for g, w in zip(grads, (w_query, w_key, w_value)):
        grad_norm1 = grad_norm1 + jnp.sum(g * w.astype(f32), axis=1)
    grad_norm1 = grad_norm1 / norm1_gain

    router_rows = (jnp.arange(experts) == expert_id).astype(f32)[:, None] * router_row
    sig = jnp.pad(jnp.sum(hot * gating[:, None], axis=0), (0, D - experts))
    small = sum_all(
        jnp.concatenate([router_rows, jnp.sum(grad_second * xh2, axis=0)[None], sig[None]], axis=0)
    )
    grad_router = jnp.transpose(small[:experts])
    grad_norm2 = small[experts]
    total_sig = small[experts + 1, :experts]
    balance = balance_weight * jnp.sum((counts - mean_load) / mean_load * total_sig) / mean_load

    return (
        output.reshape(1, rows, D),
        grad_tokens.reshape(1, rows, D),
        grad_norm1,
        grads[0],
        grads[1],
        grads[2],
        grad_output,
        grad_norm2,
        grad_router,
        grad_in,
        grad_out,
        balance,
    )


def solution(mesh):
    dp, ctx, owners = mesh.shape["dp"], mesh.shape["ctx"], mesh.shape["expert"]
    split = Mesh(mesh.devices.reshape(dp, ctx // 2, 2, owners), ("dp", "x", "core", "expert"))
    token = P(("dp", "expert"), ("x", "core"), None)
    return jax.shard_map(
        per_device,
        mesh=split,
        in_specs=(token, token, token, P(), P(), P(), P(), P(), P(), P(), P("expert"), P("expert")),
        out_specs=(
            token,
            token,
            P(),
            P(),
            P(),
            P(),
            P(),
            P(),
            P(),
            P("expert", None, ("dp", "x", "core")),
            P("expert", ("dp", "x", "core"), None),
            P(),
        ),
        check_vma=False,
    )
```

time: 978 us -> 512 us (0.52)
  waiting for transfers between devices: 478 us -> 178 us
  matrix products: 222 us -> 38.2 us
  Pallas kernels: 0 us -> 105 us
  blocking collectives: 91.4 us -> 0 us
  starting transfers between devices: 19.1 us -> 86.6 us
  local copies, waits for them, and re-layouts: 81 us -> 53.9 us
  other arithmetic: 55.5 us -> 37.3 us
  between operations: 17.1 us -> 3.89 us
    reduce_scatter x4 -> x0, waiting for transfers between devices: 219 us -> none  [the longest x1 113 us: per_device(): lax.psum_scatter(part_in.astype(jnp.bfloat16), ('dp', 'ctx'), scatter_dim...]
    psum x1 -> x0, waiting for transfers between devices: 196 us -> none  [per_device(): lax.psum((grad_q_w, grad_k_w, grad_v_w, grad_out_proj, grad_router_w, gra...]
    dot_general x49 -> x17, matrix products: 222 us -> 38.2 us  [dg(): lax.dot_general(a, b, (((ca,), (cb,)), ((), ())), preferred_element_type=...]
    ppermute x0 -> x32, waiting for transfers between devices: none -> 125 us  [the longest x18 86.3 us: shift(): return lax.ppermute(v, axis, [(i, (i + step) % n) for i in range(n)])]
    pallas_call x0 -> x9, Pallas kernels: none -> 105 us  [the longest x3 28.3 us: attend_back(): pl.pallas_call(functools.partial(attend_back_kernel, h % 2 * HD, hv % 2 *...]
    psum x2 -> x0, blocking collectives: 91.4 us -> none  [the longest x1 51.1 us: per_device(): lax.psum((jnp.sum(hot_float, axis=0), jnp.sum(hot_float * gating[:, None]...]
    all_gather x2 -> x0, waiting for transfers between devices: 49.5 us -> none  [the longest x1 26 us: per_device(): lax.all_gather(key_rows, 'ctx', axis=0, tiled=True)]
    all_to_all x4 -> x13, waiting for transfers between devices: 12.2 us -> 53.1 us  [the longest x3 26.9 us: per_device(): lax.all_to_all(dsend, ('x', 'core'), split_axis=0, concat_axis=0, tiled=T...]
  transfers between devices with their start and end apart: 11 -> 45, of which waited for: 8 -> 26; matrix products, arithmetic and copies ran while one was open for 13% -> 19% of each run, Pallas kernels for 0% -> 15%
where the time goes in v1:
time: 512 us; the launch traced here: 503 us
  waiting for transfers between devices  178 us (35%)
  Pallas kernels  105 us (21%)
  starting transfers between devices  86.6 us (17%)
  local copies, waits for them, and re-layouts  53.9 us (11%)
  matrix products  38.2 us (7%)
  other arithmetic  37.3 us (7%)
    ppermute x18, waiting for transfers between devices, shift(): return lax.ppermute(v, axis, [(i, (i + step) % n) for i in range(n)])  86.3 us
    ppermute x14, waiting for transfers between devices, swap(): return lax.ppermute(v, axis, [(0, 1), (1, 0)])  38.6 us
    dot_general x17, matrix products, dg(): lax.dot_general(a, b, (((ca,), (cb,)), ((), ())), preferred_element_type=...  38.2 us
    pallas_call x3, Pallas kernels, attend_back(): pl.pallas_call(functools.partial(attend_back_kernel, h % 2 * HD, hv % 2 *...  28.3 us
    all_to_all x3, waiting for transfers between devices, per_device(): lax.all_to_all(dsend, ('x', 'core'), split_axis=0, concat_axis=0, tiled=T...  26.9 us
    pallas_call x1, Pallas kernels, expert_mid(): pl.pallas_call(mid_kernel, out_shape=(jax.ShapeDtypeStruct((rows, ff), bf...  24.8 us
    pallas_call x1, Pallas kernels, expert_grads(): pl.pallas_call(grads_kernel, out_shape=(part, part, jax.ShapeDtypeStruct(...  24.3 us
    ppermute x18, starting transfers between devices, shift(): return lax.ppermute(v, axis, [(i, (i + step) % n) for i in range(n)])  22.1 us
  transfers between devices with their start and end apart: 45, of which 26 were waited for; matrix products, arithmetic and copies ran while one was open for 19% of the time, Pallas kernels for 15%

profile of v1, /device:TPU:0, one launch (start us, length us, event | category | flops | bytes accessed | tf_op | source)
XLA Modules:
  0.0 502.6 jit_solution(16857608189562333328)
XLA Ops:
  11.3 13.2 %collective-permute-done.1 = bf16[512,768]{1,0:T(8,128)(2,1)S(1)} collective-permute-done((bf16[512,768]{1,0:T(8,128)(2,1)S(1)}, bf16[512,768]{1,0:T(8,128)(2,1)S(1)}, u32[]{:S(2)}, u32[]{:S(2)}) %collective-permute-start.1) | collective-permute-done | bytes 786464 | tf_op jit(solution)/shard_map/ppermute | solution.py:369
  29.9 4.0 convolution_convert_fusion.qT_ref.vT_ref.kT_ref
  33.9 5.7 %attend_head2.1 = (f32[64,2048]{1,0:T(8,128)}, bf16[4,64,512]{2,1,0:T(8,128)(2,1)}, f32[1,2048]{1,0:T(1,128)}) custom-call(bf16[576,2048]{1,0:T(8,128)(2,1)} %convolution_convert_fusion.qT_ref.vT_ref.kT_ref, bf16[2048,384]{1,0:T(8,128)(2,1)} %convolution_convert_fusion.1.k_ref.v_ref, bf16[576,2048]{1,0:T(8,128)(2,1)} %convolution_convert_fusion.qT_ref.vT_ref.kT_ref), custom_call_target="tpu_custom_call" | custom-call | flops 2147483648 | bytes 1835008 | tf_op jit(solution)/shard_map/attend_head2/pallas_call | solution.py:64
  43.2 5.7 %attend_head1.1 = (f32[64,2048]{1,0:T(8,128)}, bf16[4,64,512]{2,1,0:T(8,128)(2,1)}, f32[1,2048]{1,0:T(1,128)}) custom-call(bf16[576,2048]{1,0:T(8,128)(2,1)} %convolution_convert_fusion.qT_ref.vT_ref.kT_ref, bf16[2048,384]{1,0:T(8,128)(2,1)} %convolution_convert_fusion.1.k_ref.v_ref, bf16[576,2048]{1,0:T(8,128)(2,1)} %convolution_convert_fusion.qT_ref.vT_ref.kT_ref), custom_call_target="tpu_custom_call" | custom-call | flops 2147483648 | bytes 1835008 | tf_op jit(solution)/shard_map/attend_head1/pallas_call | solution.py:64
  52.6 5.8 %attend_head0.1 = (f32[64,2048]{1,0:T(8,128)}, bf16[4,64,512]{2,1,0:T(8,128)(2,1)}, f32[1,2048]{1,0:T(1,128)}) custom-call(bf16[576,2048]{1,0:T(8,128)(2,1)} %convolution_convert_fusion.qT_ref.vT_ref.kT_ref, bf16[2048,384]{1,0:T(8,128)(2,1)} %convolution_convert_fusion.1.k_ref.v_ref, bf16[576,2048]{1,0:T(8,128)(2,1)} %convolution_convert_fusion.qT_ref.vT_ref.kT_ref), custom_call_target="tpu_custom_call" | custom-call | flops 2147483648 | bytes 1835008 | tf_op jit(solution)/shard_map/attend_head0/pallas_call | solution.py:64
  68.0 4.4 all-to-all-start.4
  76.9 14.9 %all-to-all-done.4 = bf16[4,256,768]{2,1,0:T(8,128)(2,1)} async-done(((bf16[4,256,768]{2,1,0:T(8,128)(2,1)}), bf16[4,256,768]{2,1,0:T(8,128)(2,1)}, u32[]{:S(2)}, u32[]{:S(2)}) %all-to-all-start.4) | async-done | bytes 1572896 | tf_op jit(solution)/shard_map/all_to_all | solution.py:501
  91.8 4.6 all-to-all-start.3
  97.0 10.0 %expert_up.1.u_ref = bf16[1024,3072]{1,0:T(8,128)(2,1)} custom-call(s32[2]{0:T(128)} %pad_add_fusion.pick_ref, bf16[1024,768]{1,0:T(8,128)(2,1)} %bitcast.16.dy_ref, bf16[2,3072,768]{2,1,0:T(8,128)(2,1)} %wo_ref.3), custom_call_target="tpu_custom_call" | custom-call | flops 4831838208 | bytes 12582912 | tf_op jit(solution)/shard_map/expert_up/pallas_call | solution.py:180
  111.2 4.6 collective-permute-done.4
  119.4 3.9 collective-permute-start.8
  130.9 24.8 %expert_mid.1 = (bf16[1024,3072]{1,0:T(8,128)(2,1)}, bf16[1024,3072]{1,0:T(8,128)(2,1)}, bf16[1024,768]{1,0:T(8,128)(2,1)}, f32[1,768]{1,0:T(1,128)}, f32[1024,128]{1,0:T(8,128)}) custom-call(s32[2]{0:T(128)} %pad_add_fusion.pick_ref, bf16[1024,768]{1,0:T(8,128)(2,1)} %bitcast.13.x_ref, bf16[1024,3072]{1,0:T(8,128)(2,1)} %expert_up.1.u_ref, ...), custom_call_target="tpu_custom_call" | custom-call | flops 9663676416 | bytes 28311552 | tf_op jit(solution)/shard_map/expert_mid/pallas_call | solution.py:251
  155.8 4.4 all-to-all-start.6
  170.3 5.9 %all-to-all-done.6 = bf16[4,256,768]{2,1,0:T(8,128)(2,1)} async-done(((bf16[4,256,768]{2,1,0:T(8,128)(2,1)}), bf16[4,256,768]{2,1,0:T(8,128)(2,1)}, u32[]{:S(2)}, u32[]{:S(2)}) %all-to-all-start.6) | async-done | bytes 1572896 | tf_op jit(solution)/shard_map/all_to_all | solution.py:506
  185.8 3.8 all-to-all-start.11
  199.0 9.5 %attend_back_head2.1 = (bf16[192,2048]{1,0:T(8,128)(2,1)}, bf16[4,192,512]{2,1,0:T(8,128)(2,1)}) custom-call(bf16[576,2048]{1,0:T(8,128)(2,1)} %convolution_convert_fusion.qT_ref.vT_ref.kT_ref, bf16[2048,384]{1,0:T(8,128)(2,1)} %convolution_convert_fusion.1.k_ref.v_ref, bf16[576,2048]{1,0:T(8,128)(2,1)} %convolution_convert_fusion.qT_ref.vT_ref.kT_ref, ...), custom_call_target="tpu_custom_call" | custom-call | flops 5368709120 | bytes 3145728 | tf_op jit(solution)/shard_map/attend_back_head2/pallas_call | solution.py:144
  211.3 4.2 all-to-all-start.7
  215.5 9.3 %attend_back_head1.1 = (bf16[192,2048]{1,0:T(8,128)(2,1)}, bf16[4,192,512]{2,1,0:T(8,128)(2,1)}) custom-call(bf16[576,2048]{1,0:T(8,128)(2,1)} %convolution_convert_fusion.qT_ref.vT_ref.kT_ref, bf16[2048,384]{1,0:T(8,128)(2,1)} %convolution_convert_fusion.1.k_ref.v_ref, bf16[576,2048]{1,0:T(8,128)(2,1)} %convolution_convert_fusion.qT_ref.vT_ref.kT_ref, ...), custom_call_target="tpu_custom_call" | custom-call | flops 5368709120 | bytes 3145728 | tf_op jit(solution)/shard_map/attend_back_head1/pallas_call | solution.py:144
  227.6 9.5 %attend_back_head0.1 = (bf16[192,2048]{1,0:T(8,128)(2,1)}, bf16[4,192,512]{2,1,0:T(8,128)(2,1)}) custom-call(bf16[576,2048]{1,0:T(8,128)(2,1)} %convolution_convert_fusion.qT_ref.vT_ref.kT_ref, bf16[2048,384]{1,0:T(8,128)(2,1)} %convolution_convert_fusion.1.k_ref.v_ref, bf16[576,2048]{1,0:T(8,128)(2,1)} %convolution_convert_fusion.qT_ref.vT_ref.kT_ref, ...), custom_call_target="tpu_custom_call" | custom-call | flops 5368709120 | bytes 3145728 | tf_op jit(solution)/shard_map/attend_back_head0/pallas_call | solution.py:144
  241.4 6.4 %collective-permute-done.10 = bf16[192,768]{1,0:T(8,128)(2,1)S(1)} collective-permute-done((bf16[192,768]{1,0:T(8,128)(2,1)S(1)}, bf16[192,768]{1,0:T(8,128)(2,1)S(1)}, u32[]{:S(2)}, u32[]{:S(2)}) %collective-permute-start.10) | collective-permute-done | bytes 294944 | tf_op jit(solution)/shard_map/ppermute | solution.py:369
  249.6 24.3 %expert_grads.1 = (bf16[4,2,2,192,768]{4,3,2,1,0:T(8,128)(2,1)}, bf16[4,2,2,192,768]{4,3,2,1,0:T(8,128)(2,1)}, bf16[1024,768]{1,0:T(8,128)(2,1)}) custom-call(s32[2]{0:T(128)} %pad_add_fusion.pick_ref, bf16[1024,768]{1,0:T(8,128)(2,1)} %bitcast.13.x_ref, bf16[1024,768]{1,0:T(8,128)(2,1)} %bitcast.16.dy_ref, f32[1024,128]{1,0:T(8,128)} %get-tuple-element.38.gate_ref, ...), custom_call_target="tpu_custom_call" | custom-call | flops 14495514624 | bytes 31457280 | tf_op jit(solution)/shard_map/expert_grads/pallas_call | solution.py:336
  280.5 4.4 all-to-all-start.5
  285.0 6.1 %collective-permute-done.13 = bf16[96,768]{1,0:T(8,128)(2,1)} collective-permute-done((bf16[96,768]{1,0:T(8,128)(2,1)}, bf16[96,768]{1,0:T(8,128)(2,1)}, u32[]{:S(2)}, u32[]{:S(2)}) %collective-permute-start.13) | collective-permute-done | bytes 147488 | tf_op jit(solution)/shard_map/ppermute | solution.py:374
  300.7 5.3 %collective-permute-done.16 = bf16[96,768]{1,0:T(8,128)(2,1)S(1)} collective-permute-done((bf16[96,768]{1,0:T(8,128)(2,1)S(1)}, bf16[96,768]{1,0:T(8,128)(2,1)S(1)}, u32[]{:S(2)}, u32[]{:S(2)}) %collective-permute-start.16) | collective-permute-done | bytes 147488 | tf_op jit(solution)/shard_map/ppermute | solution.py:374
  313.4 8.6 %collective-permute-done.23 = f32[6,768]{1,0:T(8,128)S(1)} collective-permute-done((f32[6,768]{1,0:T(8,128)S(1)}, f32[6,768]{1,0:T(8,128)S(1)}, u32[]{:S(2)}, u32[]{:S(2)}) %collective-permute-start.23) | collective-permute-done | bytes 18464 | tf_op jit(solution)/shard_map/ppermute | solution.py:369
  322.6 4.0 collective-permute-start.26
  343.8 23.3 %all-to-all-done.8 = bf16[4,192,512]{2,1,0:T(8,128)(2,1)S(1)} async-done(((bf16[4,192,512]{2,1,0:T(8,128)(2,1)}), bf16[4,192,512]{2,1,0:T(8,128)(2,1)S(1)}, u32[]{:S(2)}, u32[]{:S(2)}) %all-to-all-start.8) | async-done | bytes 786464 | tf_op jit(solution)/shard_map/all_to_all | solution.py:568
  383.1 3.7 all-to-all-start.12
  386.8 5.2 %add_convert_fusion = bf16[4,2,2,192,768]{4,3,2,1,0:T(8,128)(2,1)S(1)} fusion(bf16[4,2,2,192,768]{4,3,2,1,0:T(8,128)(2,1)} %collective-permute-done.27, bf16[4,2,2,192,768]{4,3,2,1,0:T(8,128)(2,1)} %get-tuple-element.56), kind=kLoop, calls=%fused_computation | loop fusion | flops 9437184 | bytes 14155776 | tf_op jit(solution)/shard_map/convert_element_type | solution.py:544
  402.1 21.5 %collective-permute-done.28 = bf16[2,2,192,768]{3,2,1,0:T(8,128)(2,1)} collective-permute-done((bf16[2,2,192,768]{3,2,1,0:T(8,128)(2,1)}, bf16[2,2,192,768]{3,2,1,0:T(8,128)(2,1)}, u32[]{:S(2)}, u32[]{:S(2)}) %collective-permute-start.28) | collective-permute-done | bytes 1179680 | tf_op jit(solution)/shard_map/ppermute | solution.py:374
  431.7 22.9 %collective-permute-done.29 = bf16[2,2,192,768]{3,2,1,0:T(8,128)(2,1)S(1)} collective-permute-done((bf16[2,2,192,768]{3,2,1,0:T(8,128)(2,1)S(1)}, bf16[2,2,192,768]{3,2,1,0:T(8,128)(2,1)S(1)}, u32[]{:S(2)}, u32[]{:S(2)}) %collective-permute-start.29) | collective-permute-done | bytes 1179680 | tf_op jit(solution)/shard_map/ppermute | solution.py:374
  460.2 23.3 %collective-permute-done.30 = bf16[2,2,192,768]{3,2,1,0:T(8,128)(2,1)S(1)} collective-permute-done((bf16[2,2,192,768]{3,2,1,0:T(8,128)(2,1)S(1)}, bf16[2,2,192,768]{3,2,1,0:T(8,128)(2,1)S(1)}, u32[]{:S(2)}, u32[]{:S(2)}) %collective-permute-start.30) | collective-permute-done | bytes 1179680 | tf_op jit(solution)/shard_map/ppermute | solution.py:374
  (301 shorter events, 191.5 us)
Async XLA Ops:
  4.0 20.5 %collective-permute-start.1 = (bf16[512,768]{1,0:T(8,128)(2,1)S(1)}, bf16[512,768]{1,0:T(8,128)(2,1)S(1)}, u32[]{:S(2)}, u32[]{:S(2)}) collective-permute-start(bf16[512,768]{1,0:T(8,128)(2,1)S(1)} %fusion.15), channel_id=1, source_target_pairs={{0,4},{4,0},{1,5},{5,1},{2,6},{6,2},{3,7},{7,3},{8,12},{12,8},{9,1... | collective-permute-start | bytes 2359304 | tf_op jit(solution)/shard_map/ppermute | solution.py:369
  7.0 18.1 %collective-permute-start = (bf16[512,768]{1,0:T(8,128)(2,1)S(1)}, bf16[512,768]{1,0:T(8,128)(2,1)}, u32[]{:S(2)}, u32[]{:S(2)}) collective-permute-start(bf16[512,768]{1,0:T(8,128)(2,1)S(1)} %fusion.15), channel_id=1, source_target_pairs={{0,2},{2,0},{1,3},{3,1},{4,6},{6,4},{5,7},{7,5},{8,10},{10,8},{9,1... | collective-permute-start | bytes 2359304 | tf_op jit(solution)/shard_map/ppermute | solution.py:369
  39.6 9.6 %all-to-all-start.2 = ((bf16[4,64,512]{2,1,0:T(8,128)(2,1)}), bf16[4,64,512]{2,1,0:T(8,128)(2,1)S(1)}, u32[]{:S(2)}, u32[]{:S(2)}) async-start(bf16[4,64,512]{2,1,0:T(8,128)(2,1)} %get-tuple-element.37), calls=%async_computation.2 | async-start | bytes 524288 | tf_op jit(solution)/shard_map/all_to_all | solution.py:529
  68.0 23.8 %all-to-all-start.4 = ((bf16[4,256,768]{2,1,0:T(8,128)(2,1)}), bf16[4,256,768]{2,1,0:T(8,128)(2,1)}, u32[]{:S(2)}, u32[]{:S(2)}) async-start(bf16[4,256,768]{2,1,0:T(8,128)(2,1)} %bitcast.15), calls=%async_computation.4 | async-start | bytes 3145728 | tf_op jit(solution)/shard_map/all_to_all | solution.py:501
  91.8 38.0 %all-to-all-start.3 = ((bf16[4,256,768]{2,1,0:T(8,128)(2,1)}), bf16[4,256,768]{2,1,0:T(8,128)(2,1)}, u32[]{:S(2)}, u32[]{:S(2)}) async-start(bf16[4,256,768]{2,1,0:T(8,128)(2,1)} %bitcast.268), calls=%async_computation.3 | async-start | bytes 3145728 | tf_op jit(solution)/shard_map/all_to_all | solution.py:501
  155.8 20.4 %all-to-all-start.6 = ((bf16[4,256,768]{2,1,0:T(8,128)(2,1)}), bf16[4,256,768]{2,1,0:T(8,128)(2,1)}, u32[]{:S(2)}, u32[]{:S(2)}) async-start(bf16[4,256,768]{2,1,0:T(8,128)(2,1)} %bitcast.267), calls=%async_computation.6 | async-start | bytes 3145728 | tf_op jit(solution)/shard_map/all_to_all | solution.py:506
  185.8 9.8 %all-to-all-start.11 = ((bf16[4,64,512]{2,1,0:T(8,128)(2,1)}), bf16[4,64,512]{2,1,0:T(8,128)(2,1)S(1)}, u32[]{:S(2)}, u32[]{:S(2)}) async-start(bf16[4,64,512]{2,1,0:T(8,128)(2,1)} %get-tuple-element.112), calls=%async_computation.11 | async-start | bytes 524288 | tf_op jit(solution)/shard_map/all_to_all | solution.py:566
  192.7 44.4 %collective-permute-start.9 = (bf16[2,192,768]{2,1,0:T(8,128)(2,1)}, bf16[2,192,768]{2,1,0:T(8,128)(2,1)}, u32[]{:S(2)}, u32[]{:S(2)}) collective-permute-start(bf16[2,192,768]{2,1,0:T(8,128)(2,1)} %fusion.49), channel_id=1, source_target_pairs={{0,2},{2,0},{1,3},{3,1},{4,6},{6,4},{5,7},{7,5},{8,10},{10,8},{9,1... | collective-permute-start | bytes 1769480 | tf_op jit(solution)/shard_map/ppermute | solution.py:369
  195.6 15.7 %all-to-all-start.9 = ((bf16[4,64,512]{2,1,0:T(8,128)(2,1)}), bf16[4,64,512]{2,1,0:T(8,128)(2,1)S(1)}, u32[]{:S(2)}, u32[]{:S(2)}) async-start(bf16[4,64,512]{2,1,0:T(8,128)(2,1)} %get-tuple-element.113), calls=%async_computation.9 | async-start | bytes 524288 | tf_op jit(solution)/shard_map/all_to_all | solution.py:566
  211.3 16.3 %all-to-all-start.7 = ((bf16[4,64,512]{2,1,0:T(8,128)(2,1)}), bf16[4,64,512]{2,1,0:T(8,128)(2,1)}, u32[]{:S(2)}, u32[]{:S(2)}) async-start(bf16[4,64,512]{2,1,0:T(8,128)(2,1)} %get-tuple-element.114), calls=%async_computation.7 | async-start | bytes 524288 | tf_op jit(solution)/shard_map/all_to_all | solution.py:566
  248.1 26.9 %collective-permute-start.11 = (bf16[384,768]{1,0:T(8,128)(2,1)S(1)}, bf16[384,768]{1,0:T(8,128)(2,1)S(1)}, u32[]{:S(2)}, u32[]{:S(2)}) collective-permute-start(bf16[384,768]{1,0:T(8,128)(2,1)S(1)} %fusion.47), channel_id=1, source_target_pairs={{0,1},{1,0},{2,3},{3,2},{4,5},{5,4},{6,7},{7,6},{8,9},{9,8},{10,11... | collective-permute-start | bytes 1769480 | tf_op jit(solution)/shard_map/ppermute | solution.py:369
  274.0 112.8 %collective-permute-start.27 = (bf16[4,2,2,192,768]{4,3,2,1,0:T(8,128)(2,1)}, bf16[4,2,2,192,768]{4,3,2,1,0:T(8,128)(2,1)}, u32[]{:S(2)}, u32[]{:S(2)}) collective-permute-start(bf16[4,2,2,192,768]{4,3,2,1,0:T(8,128)(2,1)} %get-tuple-element.57), channel_id=1, source_target_pairs={{0,2},{2,0},{1,3},{3,1},{4,6},{6,4},{5,7},{7,5},{8,10},{10,8},{9,1... | collective-permute-start | bytes 14155784 | tf_op jit(solution)/shard_map/ppermute | solution.py:369
  276.5 14.6 %collective-permute-start.13 = (bf16[96,768]{1,0:T(8,128)(2,1)}, bf16[96,768]{1,0:T(8,128)(2,1)}, u32[]{:S(2)}, u32[]{:S(2)}) collective-permute-start(bf16[96,768]{1,0:T(8,128)(2,1)} %get-tuple-element.102), channel_id=1, source_target_pairs={{0,16},{8,24},{16,0},{24,8},{1,17},{9,25},{17,1},{25,9},{2,18},{10... | collective-permute-start | bytes 442376 | tf_op jit(solution)/shard_map/ppermute | solution.py:374
  276.9 14.2 %collective-permute-start.12 = (bf16[96,768]{1,0:T(8,128)(2,1)}, bf16[96,768]{1,0:T(8,128)(2,1)}, u32[]{:S(2)}, u32[]{:S(2)}) collective-permute-start(bf16[96,768]{1,0:T(8,128)(2,1)} %get-tuple-element.100), channel_id=1, source_target_pairs={{0,8},{8,16},{16,24},{24,0},{1,9},{9,17},{17,25},{25,1},{2,10},{10... | collective-permute-start | bytes 442376 | tf_op jit(solution)/shard_map/ppermute | solution.py:374
  280.5 52.8 %all-to-all-start.5 = ((bf16[4,256,768]{2,1,0:T(8,128)(2,1)}), bf16[4,256,768]{2,1,0:T(8,128)(2,1)}, u32[]{:S(2)}, u32[]{:S(2)}) async-start(bf16[4,256,768]{2,1,0:T(8,128)(2,1)} %bitcast.266), calls=%async_computation.5 | async-start | bytes 3145728 | tf_op jit(solution)/shard_map/all_to_all | solution.py:506
  292.9 13.9 %collective-permute-start.21 = (f32[6,768]{1,0:T(8,128)S(1)}, f32[6,768]{1,0:T(8,128)S(1)}, u32[]{:S(2)}, u32[]{:S(2)}) collective-permute-start(f32[6,768]{1,0:T(8,128)S(1)} %pad_maximum_fusion.6), channel_id=1, source_target_pairs={{0,2},{2,0},{1,3},{3,1},{4,6},{6,4},{5,7},{7,5},{8,10},{10,8},{9,1... | collective-permute-start | bytes 55304 | tf_op jit(solution)/shard_map/ppermute | solution.py:369
  292.9 13.1 %collective-permute-start.16 = (bf16[96,768]{1,0:T(8,128)(2,1)S(1)}, bf16[96,768]{1,0:T(8,128)(2,1)S(1)}, u32[]{:S(2)}, u32[]{:S(2)}) collective-permute-start(bf16[96,768]{1,0:T(8,128)(2,1)S(1)} %get-tuple-element.90), channel_id=1, source_target_pairs={{0,16},{8,24},{16,0},{24,8},{1,17},{9,25},{17,1},{25,9},{2,18},{10... | collective-permute-start | bytes 442376 | tf_op jit(solution)/shard_map/ppermute | solution.py:374
  295.0 11.2 %collective-permute-start.17 = (bf16[96,768]{1,0:T(8,128)(2,1)S(1)}, bf16[96,768]{1,0:T(8,128)(2,1)S(1)}, u32[]{:S(2)}, u32[]{:S(2)}) collective-permute-start(bf16[96,768]{1,0:T(8,128)(2,1)S(1)} %get-tuple-element.90), channel_id=1, source_target_pairs={{0,24},{8,0},{16,8},{24,16},{1,25},{9,1},{17,9},{25,17},{2,26},{10... | collective-permute-start | bytes 442376 | tf_op jit(solution)/shard_map/ppermute | solution.py:374
  306.1 23.7 %collective-permute-start.18 = (bf16[384,768]{1,0:T(8,128)(2,1)S(1)}, bf16[384,768]{1,0:T(8,128)(2,1)}, u32[]{:S(2)}, u32[]{:S(2)}) collective-permute-start(bf16[384,768]{1,0:T(8,128)(2,1)S(1)} %bitcast.264), channel_id=1, source_target_pairs={{0,1},{1,0},{2,3},{3,2},{4,5},{5,4},{6,7},{7,6},{8,9},{9,8},{10,11... | collective-permute-start | bytes 1769480 | tf_op jit(solution)/shard_map/ppermute | solution.py:374
  310.7 11.3 %collective-permute-start.23 = (f32[6,768]{1,0:T(8,128)S(1)}, f32[6,768]{1,0:T(8,128)S(1)}, u32[]{:S(2)}, u32[]{:S(2)}) collective-permute-start(f32[6,768]{1,0:T(8,128)S(1)} %add.368), channel_id=1, source_target_pairs={{0,1},{1,0},{2,3},{3,2},{4,5},{5,4},{6,7},{7,6},{8,9},{9,8},{10,11... | collective-permute-start | bytes 55304 | tf_op jit(solution)/shard_map/ppermute | solution.py:369
  322.6 17.9 %collective-permute-start.26 = (f32[6,768]{1,0:T(8,128)}, f32[6,768]{1,0:T(8,128)}, u32[]{:S(2)}, u32[]{:S(2)}) collective-permute-start(f32[6,768]{1,0:T(8,128)} %add.369), channel_id=1, source_target_pairs={{0,24},{8,0},{16,8},{24,16},{1,25},{9,1},{17,9},{25,17},{2,26},{10... | collective-permute-start | bytes 55304 | tf_op jit(solution)/shard_map/ppermute | solution.py:374
  326.6 14.0 %collective-permute-start.25 = (f32[6,768]{1,0:T(8,128)}, f32[6,768]{1,0:T(8,128)}, u32[]{:S(2)}, u32[]{:S(2)}) collective-permute-start(f32[6,768]{1,0:T(8,128)} %add.369), channel_id=1, source_target_pairs={{0,16},{8,24},{16,0},{24,8},{1,17},{9,25},{17,1},{25,9},{2,18},{10... | collective-permute-start | bytes 55304 | tf_op jit(solution)/shard_map/ppermute | solution.py:374
  327.7 12.8 %collective-permute-start.24 = (f32[6,768]{1,0:T(8,128)}, f32[6,768]{1,0:T(8,128)}, u32[]{:S(2)}, u32[]{:S(2)}) collective-permute-start(f32[6,768]{1,0:T(8,128)} %add.369), channel_id=1, source_target_pairs={{0,8},{8,16},{16,24},{24,0},{1,9},{9,17},{17,25},{25,1},{2,10},{10... | collective-permute-start | bytes 55304 | tf_op jit(solution)/shard_map/ppermute | solution.py:374
  331.8 46.7 %collective-permute-start.19 = (bf16[768,768]{1,0:T(8,128)(2,1)}, bf16[768,768]{1,0:T(8,128)(2,1)}, u32[]{:S(2)}, u32[]{:S(2)}) collective-permute-start(bf16[768,768]{1,0:T(8,128)(2,1)} %bitcast.62), channel_id=1, source_target_pairs={{0,4},{4,0},{1,5},{5,1},{2,6},{6,2},{3,7},{7,3},{8,12},{12,8},{9,1... | collective-permute-start | bytes 3538952 | tf_op jit(solution)/shard_map/ppermute | solution.py:374
  336.9 30.2 %all-to-all-start.8 = ((bf16[4,192,512]{2,1,0:T(8,128)(2,1)}), bf16[4,192,512]{2,1,0:T(8,128)(2,1)S(1)}, u32[]{:S(2)}, u32[]{:S(2)}) async-start(bf16[4,192,512]{2,1,0:T(8,128)(2,1)} %get-tuple-element.45), calls=%async_computation.8 | async-start | bytes 1572864 | tf_op jit(solution)/shard_map/all_to_all | solution.py:568
  367.9 15.1 %all-to-all-start.10 = ((bf16[4,192,512]{2,1,0:T(8,128)(2,1)}), bf16[4,192,512]{2,1,0:T(8,128)(2,1)S(1)}, u32[]{:S(2)}, u32[]{:S(2)}) async-start(bf16[4,192,512]{2,1,0:T(8,128)(2,1)} %get-tuple-element.48), calls=%async_computation.10 | async-start | bytes 1572864 | tf_op jit(solution)/shard_map/all_to_all | solution.py:568
  380.8 48.3 %collective-permute-start.20 = (bf16[2,768,768]{2,1,0:T(8,128)(2,1)}, bf16[2,768,768]{2,1,0:T(8,128)(2,1)}, u32[]{:S(2)}, u32[]{:S(2)}) collective-permute-start(bf16[2,768,768]{2,1,0:T(8,128)(2,1)} %bitcast_dynamic-update-slice_fusion.2), channel_id=1, source_target_pairs={{0,2},{2,0},{1,3},{3,1},{4,6},{6,4},{5,7},{7,5},{8,10},{10,8},{9,1... | collective-permute-start | bytes 7077896 | tf_op jit(solution)/shard_map/ppermute | solution.py:374
  383.1 15.4 %all-to-all-start.12 = ((bf16[4,192,512]{2,1,0:T(8,128)(2,1)}), bf16[4,192,512]{2,1,0:T(8,128)(2,1)S(1)}, u32[]{:S(2)}, u32[]{:S(2)}) async-start(bf16[4,192,512]{2,1,0:T(8,128)(2,1)} %get-tuple-element.51), calls=%async_computation.12 | async-start | bytes 1572864 | tf_op jit(solution)/shard_map/all_to_all | solution.py:568
  393.1 30.5 %collective-permute-start.28 = (bf16[2,2,192,768]{3,2,1,0:T(8,128)(2,1)}, bf16[2,2,192,768]{3,2,1,0:T(8,128)(2,1)}, u32[]{:S(2)}, u32[]{:S(2)}) collective-permute-start(bf16[2,2,192,768]{3,2,1,0:T(8,128)(2,1)} %dynamic-slice_bitcast_fusion), channel_id=1, source_target_pairs={{0,8},{8,16},{16,24},{24,0},{1,9},{9,17},{17,25},{25,1},{2,10},{10... | collective-permute-start | bytes 3538952 | tf_op jit(solution)/shard_map/ppermute | solution.py:374
  425.2 29.4 %collective-permute-start.29 = (bf16[2,2,192,768]{3,2,1,0:T(8,128)(2,1)S(1)}, bf16[2,2,192,768]{3,2,1,0:T(8,128)(2,1)S(1)}, u32[]{:S(2)}, u32[]{:S(2)}) collective-permute-start(bf16[2,2,192,768]{3,2,1,0:T(8,128)(2,1)S(1)} %fusion.1), channel_id=1, source_target_pairs={{0,8},{8,16},{16,24},{24,0},{1,9},{9,17},{17,25},{25,1},{2,10},{10... | collective-permute-start | bytes 3538952 | tf_op jit(solution)/shard_map/ppermute | solution.py:374
  454.9 28.5 %collective-permute-start.30 = (bf16[2,2,192,768]{3,2,1,0:T(8,128)(2,1)S(1)}, bf16[2,2,192,768]{3,2,1,0:T(8,128)(2,1)S(1)}, u32[]{:S(2)}, u32[]{:S(2)}) collective-permute-start(bf16[2,2,192,768]{3,2,1,0:T(8,128)(2,1)S(1)} %fusion), channel_id=1, source_target_pairs={{0,8},{8,16},{16,24},{24,0},{1,9},{9,17},{17,25},{25,1},{2,10},{10... | collective-permute-start | bytes 3538952 | tf_op jit(solution)/shard_map/ppermute | solution.py:374
  484.6 13.4 %collective-permute-start.31 = (bf16[2,192,768]{2,1,0:T(8,128)(2,1)}, bf16[2,192,768]{2,1,0:T(8,128)(2,1)}, u32[]{:S(2)}, u32[]{:S(2)}) collective-permute-start(bf16[2,192,768]{2,1,0:T(8,128)(2,1)} %fusion.48), channel_id=1, source_target_pairs={{0,4},{4,0},{1,5},{5,1},{2,6},{6,2},{3,7},{7,3},{8,12},{12,8},{9,1... | collective-permute-start | bytes 1769480 | tf_op jit(solution)/shard_map/ppermute | solution.py:369
  (70 other events, 627.8 us)

commit v2 on v1

--- a/solution.py
+++ b/solution.py
@@ -26,72 +26,77 @@
     return lax.dot_general(a, b, (((ca,), (cb,)), ((), ())), preferred_element_type=f32)
 
 
-def attend_kernel(lane, blk, qT_ref, k_ref, vT_ref, oT_ref, osend_ref, lse_ref):
+def attend_kernel(heads, blk, qT_ref, k_ref, vT_ref, oT_ref, osend_ref, lse_ref):
     length = qT_ref.shape[1]
-    per = osend_ref.shape[2]
+    per = osend_ref.shape[3]
     c = (HD**-0.5) * LOG2E
     rows = lax.broadcasted_iota(jnp.int32, (blk, blk), 0)
     cols = lax.broadcasted_iota(jnp.int32, (blk, blk), 1)
     keep = rows <= cols
-    for i in range(length // blk):
-        a, b = i * blk, (i + 1) * blk
-        q = qT_ref[:, a:b]
-        sd = dg(k_ref[a:b, lane : lane + HD], q, 1, 0)
-        sd = jnp.where(keep, sd, MASKED)
-        m = jnp.max(sd, axis=0, keepdims=True)
-        if i:
-            s = dg(k_ref[:a, lane : lane + HD], q, 1, 0)
-            m = jnp.maximum(m, jnp.max(s, axis=0, keepdims=True))
-        mc = m * c
-        pd = jnp.exp2(sd * c - mc)
-        total = jnp.sum(pd, axis=0, keepdims=True)
-        o = dg(vT_ref[:, a:b], pd.astype(bf16), 1, 0)
-        if i:
-            p = jnp.exp2(s * c - mc)
-            total = total + jnp.sum(p, axis=0, keepdims=True)
-            o = o + dg(vT_ref[:, :a], p.astype(bf16), 1, 0)
-        o = o / total
-        oT_ref[:, a:b] = o
-        d, off = a // per, a % per
-        osend_ref[d, :, off : off + blk] = o.astype(bf16)
-        lse_ref[:, a:b] = mc + jnp.log2(total)
-
-
-def attend(qkvT, kv, h, dests):
+    for h in range(heads):
+        hs = slice(h * HD, (h + 1) * HD)
+        for i in range(length // blk):
+            a, b = i * blk, (i + 1) * blk
+            q = qT_ref[hs, a:b]
+            sd = dg(k_ref[a:b, hs], q, 1, 0)
+            sd = jnp.where(keep, sd, MASKED)
+            m = jnp.max(sd, axis=0, keepdims=True)
+            if i:
+                s = dg(k_ref[:a, hs], q, 1, 0)
+                m = jnp.maximum(m, jnp.max(s, axis=0, keepdims=True))
+            mc = m * c
+            pd = jnp.exp2(sd * c - mc)
+            total = jnp.sum(pd, axis=0, keepdims=True)
+            o = dg(vT_ref[hs, a:b], pd.astype(bf16), 1, 0)
+            if i:
+                p = jnp.exp2(s * c - mc)
+                total = total + jnp.sum(p, axis=0, keepdims=True)
+                o = o + dg(vT_ref[hs, :a], p.astype(bf16), 1, 0)
+            o = o / total
+            oT_ref[hs, a:b] = o
+            d, off = a // per, a % per
+            osend_ref[d, h, :, off : off + blk] = o.astype(bf16)
+            lse_ref[h, :, a:b] = mc + jnp.log2(total)
+
+
+def attend(qkvT, kv, dests):
     length = kv.shape[0]
-    n = qkvT.shape[0] // (3 * HD)
-    blk = length // dests
+    heads = qkvT.shape[0] // (3 * HD)
+    wide = heads * HD
+    per = length // dests
     return pl.pallas_call(
-        functools.partial(attend_kernel, (h % 2) * HD, blk),
+        functools.partial(attend_kernel, heads, per),
         out_shape=(
-            jax.ShapeDtypeStruct((HD, length), f32),
-            jax.ShapeDtypeStruct((dests, HD, length // dests), bf16),
-            jax.ShapeDtypeStruct((1, length), f32),
+            jax.ShapeDtypeStruct((wide, length), f32),
+            jax.ShapeDtypeStruct((dests, heads, HD, per), bf16),
+            jax.ShapeDtypeStruct((heads, 1, length), f32),
         ),
         grid=(1,),
         in_specs=[
-            pl.BlockSpec((HD, length), lambda i: (h, 0)),
-            pl.BlockSpec((length, 2 * HD), lambda i: (0, h // 2)),
-            pl.BlockSpec((HD, length), lambda i: (2 * n + h, 0)),
+            pl.BlockSpec((wide, length), lambda i: (0, 0)),
+            pl.BlockSpec(kv.shape, lambda i: (0, 0)),
+            pl.BlockSpec((wide, length), lambda i: (2, 0)),
         ],
         out_specs=(
-            pl.BlockSpec((HD, length), lambda i: (0, 0)),
-            pl.BlockSpec((dests, HD, length // dests), lambda i: (0, 0, 0)),
-            pl.BlockSpec((1, length), lambda i: (0, 0)),
+            pl.BlockSpec((wide, length), lambda i: (0, 0)),
+            pl.BlockSpec((dests, heads, HD, per), lambda i: (0, 0, 0, 0)),
+            pl.BlockSpec((heads, 1, length), lambda i: (0, 0, 0)),
         ),
         compiler_params=pltpu.CompilerParams(vmem_limit_bytes=VMEM),
         cost_estimate=pl.CostEstimate(
-            flops=8 * length * length * HD, bytes_accessed=length * HD * 14, transcendentals=length * length // 2
-        ),
-        name=f"attend_head{h}",
+            flops=8 * heads * length * length * HD,
+            bytes_accessed=length * wide * 14,
+            transcendentals=heads * length * length // 2,
+        ),
+        name="attend",
     )(qkvT, kv, qkvT)
 
 
-def attend_back_kernel(
-    lk, lv, blk, qT_ref, k_ref, kT_ref, v_ref, do_ref, oT_ref, lse_ref, dT_ref, dsend_ref, dk_acc, dv_acc
-):
+def attend_back_kernel(lk, lv, blk, *refs):
+    qT_ref, k_ref, kT_ref, v_ref, do_ref, oT_ref, lse_ref = refs[:7]
+    dT_ref, dsend_ref, dk_acc, dv_acc = refs[-4:]
     length = qT_ref.shape[1]
-    per = do_ref.shape[2]
+    per = do_ref.shape[3]
     sc = HD**-0.5
     c = sc * LOG2E
     rows = lax.broadcasted_iota(jnp.int32, (blk, blk), 0)
@@ -102,8 +107,8 @@
         x0, x1 = i * blk, (i + 1) * blk
         d, off = x0 // per, x0 % per
         q = qT_ref[:, x0:x1]
-        do = do_ref[d, :, off : off + blk]
-        lse = lse_ref[:, x0:x1]
+        do = do_ref[d, 0, :, off : off + blk]
+        lse = lse_ref[0, :, x0:x1]
         delta = jnp.sum(do.astype(f32) * oT_ref[:, x0:x1], axis=0, keepdims=True)
         dq = None
         for a, b, diag in ([(0, x0, False)] if i else []) + [(x0, x1, True)]:
@@ -124,50 +129,59 @@
             t = dg(kT_ref[:, a:b], ds, 1, 0)
             dq = t if dq is None else dq + t
         dq = (dq * sc).astype(bf16)
-        dT_ref[0:HD, x0:x1] = dq
-        dsend_ref[d, 0:HD, off : off + blk] = dq
+        dT_ref[0, :, x0:x1] = dq
+        dsend_ref[d, 0, :, off : off + blk] = dq
     for d in range(dsend_ref.shape[0]):
-        dk = (dk_acc[:, d * per : (d + 1) * per] * sc).astype(bf16)
-        dv = dv_acc[:, d * per : (d + 1) * per].astype(bf16)
-        dT_ref[HD : 2 * HD, d * per : (d + 1) * per] = dk
-        dT_ref[2 * HD : 3 * HD, d * per : (d + 1) * per] = dv
-        dsend_ref[d, HD : 2 * HD, :] = dk
-        dsend_ref[d, 2 * HD : 3 * HD, :] = dv
-
-
-def attend_back(qkvT, kv, do, oT, lse, h):
+        at_d = slice(d * per, (d + 1) * per)
+        dk = (dk_acc[:, at_d] * sc).astype(bf16)
+        dv = dv_acc[:, at_d].astype(bf16)
+        dT_ref[1, :, at_d] = dk
+        dT_ref[2, :, at_d] = dv
+        dsend_ref[d, 1] = dk
+        dsend_ref[d, 2] = dv
+
+
+def attend_back(qkvT, kv, do, slot, oT, lse, h, so_far):
     length = kv.shape[0]
     n = qkvT.shape[0] // (3 * HD)
-    dests, _, per = do.shape
+    dests, _, _, per = do.shape
     hv = n + h
     blk = min(256, per)
+    args = [qkvT, kv, qkvT, kv, do, oT, lse]
+    specs = [
+        pl.BlockSpec((HD, length), lambda i: (h, 0)),
+        pl.BlockSpec((length, 2 * HD), lambda i: (0, h // 2)),
+        pl.BlockSpec((HD, length), lambda i: (n + h, 0)),
+        pl.BlockSpec((length, 2 * HD), lambda i: (0, hv // 2)),
+        pl.BlockSpec((dests, 1, HD, per), lambda i: (0, slot, 0, 0)),
+        pl.BlockSpec((HD, length), lambda i: (h, 0)),
+        pl.BlockSpec((1, 1, length), lambda i: (h, 0, 0)),
+    ]
+    alias = {}
+    if so_far is not None:
+        alias = {len(args): 0, len(args) + 1: 1}
+        args += list(so_far)
+        specs += [pl.BlockSpec(memory_space=pl.ANY)] * 2
     return pl.pallas_call(
         functools.partial(attend_back_kernel, (h % 2) * HD, (hv % 2) * HD, blk),
         out_shape=(
-            jax.ShapeDtypeStruct((3 * HD, length), bf16),
-            jax.ShapeDtypeStruct((dests, 3 * HD, per), bf16),
+            jax.ShapeDtypeStruct((3, n * HD, length), bf16),
+            jax.ShapeDtypeStruct((dests, 3, n * HD, per), bf16),
         ),
         grid=(1,),
-        in_specs=[
-            pl.BlockSpec((HD, length), lambda i: (h, 0)),
-            pl.BlockSpec((length, 2 * HD), lambda i: (0, h // 2)),
-            pl.BlockSpec((HD, length), lambda i: (n + h, 0)),
-            pl.BlockSpec((length, 2 * HD), lambda i: (0, hv // 2)),
-            pl.BlockSpec((dests, HD, per), lambda i: (0, 0, 0)),
-            pl.BlockSpec((HD, length), lambda i: (0, 0)),
-            pl.BlockSpec((1, length), lambda i: (0, 0)),
-        ],
+        in_specs=specs,
         out_specs=(
-            pl.BlockSpec((3 * HD, length), lambda i: (0, 0)),
-            pl.BlockSpec((dests, 3 * HD, per), lambda i: (0, 0, 0)),
+            pl.BlockSpec((3, HD, length), lambda i: (0, h, 0)),
+            pl.BlockSpec((dests, 3, HD, per), lambda i: (0, 0, h, 0)),
         ),
         scratch_shapes=[pltpu.VMEM((HD, length), f32)] * 2,
+        input_output_aliases=alias,
         compiler_params=pltpu.CompilerParams(vmem_limit_bytes=VMEM),
         cost_estimate=pl.CostEstimate(
             flops=20 * length * length * HD, bytes_accessed=length * HD * 24, transcendentals=length * length // 2
         ),
         name=f"attend_back_head{h}",
-    )(qkvT, kv, qkvT, kv, do, oT, lse)
+    )(*args)
 
 
 def up_kernel(pick_ref, dy_ref, wo_ref, u_ref):
@@ -392,13 +406,11 @@
 
 
 def sum_all(v):
-    v = v + swap(v, "core")
-    v = v + swap(v, "x")
-    v = v + swap(v, "expert") if lax.axis_size("expert") == 2 else lax.psum(v, "expert")
-    out = v
-    for s in range(1, lax.axis_size("dp")):
-        out = out + shift(v, "dp", s)
-    return out
+    return jnp.sum(lax.all_gather(v, ("dp", "x", "core", "expert")), axis=0)
+
+
+def tie(*arrays):
+    return lax.optimization_barrier(arrays)
 
 
 def scatter_sum(v):
@@ -431,7 +443,7 @@
     return jnp.swapaxes(v, 0, 1)
 
 
-def ring_scatter(parts):
+def ring_steps(parts):
     n = lax.axis_size("dp")
     me = lax.axis_index("dp")
     moving = at(parts, (me - 1) % n)
@@ -440,7 +452,7 @@
         moving = moving.astype(f32) + at(parts, (me - 2 - s) % n).astype(f32)
         if s < n - 2:
             moving = moving.astype(bf16)
-    return moving
+        moving = yield moving
 
 
 def normal_form(v):
@@ -483,11 +495,7 @@
     xh1, rstd1 = normal_form(flat)
     normed = (xh1 * norm1_gain).astype(bf16)
     other = swap(normed, "x")
-    near, far = swap(normed, "core"), swap(other, "core")
-    normed_all = place(
-        [(ctx_i, normed), (ctx_i ^ 1, near), (ctx_i ^ 2, other), (ctx_i ^ 3, far)], ctx
-    ).reshape(length, D)
-
+    near = swap(normed, "core")
     route = routes.reshape(rows)
     hot = (route[:, None] == jnp.arange(experts, dtype=jnp.int32)[None, :]).astype(f32)
     lower = jnp.arange(rows)[:, None] >= jnp.arange(rows)[None, :]
@@ -496,20 +504,25 @@
     slot = ((route % nx) * owners + route // nx) * cap + rank
     spread = (jnp.arange(experts * cap, dtype=jnp.int32)[:, None] == slot[None, :]).astype(bf16)
 
-    def dispatch(v):
-        out = dg(spread, v, 1, 0).astype(bf16).reshape(nx * owners, cap, D)
-        out = lax.all_to_all(out, ("x", "expert"), split_axis=0, concat_axis=0, tiled=True)
-        return out.reshape(-1, D)
-
-    def give_back(v):
-        v = v.reshape(nx * owners, cap, D)
-        v = lax.all_to_all(v, ("x", "expert"), split_axis=0, concat_axis=0, tiled=True)
-        return dg(spread, v.reshape(-1, D), 0, 0)
+    def pack(v):
+        return dg(spread, v, 1, 0).astype(bf16).reshape(nx * owners, cap, D)
+
+    def trade(v):
+        v = lax.all_to_all(v.reshape(nx * owners, cap, D), ("x", "expert"), split_axis=0, concat_axis=0, tiled=True)
+        return v.reshape(-1, D)
+
+    def turn(v):
+        return lax.all_to_all(v, ("x", "core"), split_axis=0, concat_axis=0, tiled=True)
 
     dy_low = cotangent.reshape(rows, D)
     dy = dy_low.astype(f32)
-    dy_rows = dispatch(dy_low)
-    counts = sum_all(jnp.sum(hot, axis=0))
+    other, dy_packed = tie(other, pack(dy_low))
+    dy_rows = trade(dy_packed)
+    far = swap(other, "core")
+    normed_all = place(
+        [(ctx_i, normed), (ctx_i ^ 1, near), (ctx_i ^ 2, other), (ctx_i ^ 3, far)], ctx
+    ).reshape(length, D)
+    counts = sum_all(jnp.zeros((8, 128), f32).at[0, :experts].set(jnp.sum(hot, axis=0)))[0, :experts]
     mean_load = rows * ctx * dp * owners / experts
     load_term = balance_weight * (counts - mean_load) / (mean_load * mean_load)
     expert_id = ei * nx + xi
@@ -522,12 +535,9 @@
     wq, wk, wv = cut(w_query), cut(w_key), cut(w_value)
     qkvT = dg(jnp.concatenate([wq, wk, wv], axis=1), normed_all, 0, 1).astype(bf16)
     kv = dg(normed_all, jnp.concatenate([wk, wv], axis=1), 1, 0).astype(bf16)
-    kept, arrived = [], []
-    for h in range(heads):
-        oT, osend, lse = attend(qkvT, kv, h, ctx)
-        kept.append((oT, lse))
-        arrived.append(lax.all_to_all(osend, ("x", "core"), split_axis=0, concat_axis=0, tiled=True))
-    attT = jnp.stack(arrived, axis=1).reshape(D, rows)
+    oT, osend, lse = attend(qkvT, kv, ctx)
+    osend, dy_rows = tie(osend, dy_rows)
+    attT = turn(osend).reshape(D, rows)
 
     middle = flat + dg(attT, w_output, 0, 0)
     xh2, rstd2 = normal_form(middle)
@@ -535,52 +545,61 @@
     gating = jax.nn.sigmoid(jnp.sum(hot * dg(second, w_router, 1, 0), axis=1))
 
     up = expert_up(pick, dy_rows, w_out)
-    x_rows = dispatch(second)
+    x_rows = trade(pack(second))
     active, grad_hidden, back_rows, router_row, gate = expert_mid(pick, x_rows, up, w_in, wr, load)
-    grad_second = give_back(back_rows)
+    returned = trade(back_rows)
     keep, send, produced = expert_grads(pick, x_rows, dy_rows, gate, active, grad_hidden, w_out, dp, nx)
-    output = (middle + gating[:, None] * give_back(produced)).astype(bf16)
-
+    returned, keep, send, produced = tie(returned, keep, send, produced)
     pair = (keep.astype(f32) + swap(send, "core").astype(f32)).astype(bf16)
-    ringed = ring_scatter(pair)
+
+    grad_second = dg(spread, returned, 0, 0)
+    grad_middle = dy + norm_back(grad_second * norm2_gain, xh2, rstd2)
+    branch = grad_middle.astype(bf16)
+    attT_grad = dg(w_output, branch, 1, 1).astype(bf16).reshape(ctx, heads, HD, rows)
+    do_first, do_later = turn(attT_grad[:, :1]), turn(attT_grad[:, 1:])
+    go = dg(attT, branch, 1, 0)
+    go = go.reshape(nx, 2, mine, D)
+    go_keep = lax.dynamic_index_in_dim(go, ci, 1, keepdims=False)
+    go_send = lax.dynamic_index_in_dim(go, 1 - ci, 1, keepdims=False).astype(bf16)
+    go = go_keep + swap(go_send, "core").astype(f32)
+    go = at(go, xi) + swap(at(go, 1 - xi).astype(bf16), "x").astype(f32)
+
+    do_first, pair = tie(do_first, pair)
+    ring = ring_steps(pair)
+    ringed = next(ring)
+    so_far = attend_back(qkvT, kv, do_first, 0, oT, lse, 0, None)
+    for h in range(1, heads):
+        do_later, ringed, *so_far = tie(do_later, ringed, *so_far)
+        try:
+            ringed = ring.send(ringed)
+        except StopIteration:
+            pass
+        so_far = attend_back(qkvT, kv, do_later, h - 1, oT, lse, h, so_far)
+    dT, dsend = so_far
+    for more in ring:
+        ringed = more
+    got, produced = tie(turn(dsend), produced)
+    grad_normed = 0.0
+    for p, w in enumerate((w_query, w_key, w_value)):
+        grad_normed = grad_normed + dg(got[:, p].reshape(D, rows), w, 0, 1)
+    grad_tokens = grad_middle + norm_back(grad_normed * norm1_gain, xh1, rstd1)
+    output = (middle + gating[:, None] * dg(spread, trade(produced), 0, 0)).astype(bf16)
+
+    weight_rows = dg(dT.reshape(3 * mine, length), normed_all, 1, 0)
+    shared = gather_back(scatter_sum(jnp.concatenate([weight_rows, go], axis=0)).astype(bf16))
+    grads = [shared[:, :, p * mine : (p + 1) * mine].reshape(D, D).astype(f32) for p in range(4)]
+    grads[:3] = [jnp.transpose(g) for g in grads[:3]]
+    grad_norm1 = 0.0
+    for g, w in zip(grads, (w_query, w_key, w_value)):
+        grad_norm1 = grad_norm1 + jnp.sum(g * w.astype(f32), axis=1)
+    grad_norm1 = grad_norm1 / norm1_gain
+
     own = lax.dynamic_index_in_dim(ringed, xi, 1, keepdims=False)
     moved = swap(lax.dynamic_index_in_dim(ringed, 1 - xi, 1, keepdims=False).astype(bf16), "x").astype(f32)
     first, latter = jnp.where(xi == 0, own, moved), jnp.where(xi == 0, moved, own)
     both = jnp.stack([first, latter], axis=1)
     grad_in = jnp.swapaxes(both[0], 1, 2)
     grad_out = both[1]
-
-    grad_middle = dy + norm_back(grad_second * norm2_gain, xh2, rstd2)
-    branch = grad_middle.astype(bf16)
-    go = dg(attT, branch, 1, 0)
-    go = go.reshape(nx, 2, mine, D)
-    go_keep = lax.dynamic_index_in_dim(go, ci, 1, keepdims=False)
-    go_send = lax.dynamic_index_in_dim(go, 1 - ci, 1, keepdims=False).astype(bf16)
-    go = go_keep + swap(go_send, "core").astype(f32)
-    go = at(go, xi) + swap(at(go, 1 - xi).astype(bf16), "x").astype(f32)
-    attT_grad = dg(w_output, branch, 1, 1).astype(bf16).reshape(ctx, heads, HD, rows)
-
-    grad_normed = 0.0
-    weight_rows = []
-    for h in range(heads):
-        do = lax.all_to_all(attT_grad[:, h], ("x", "core"), split_axis=0, concat_axis=0, tiled=True)
-        dT, dsend = attend_back(qkvT, kv, do, kept[h][0], kept[h][1], h)
-        got = lax.all_to_all(dsend, ("x", "core"), split_axis=0, concat_axis=0, tiled=True)
-        wide = jnp.stack([w.reshape(D, ctx, heads, HD)[:, :, h] for w in (w_query, w_key, w_value)], axis=2)
-        grad_normed = grad_normed + dg(got.reshape(-1, rows), wide.reshape(D, -1), 0, 1)
-        weight_rows.append(dg(dT, normed_all, 1, 0))
-    grad_tokens = grad_middle + norm_back(grad_normed * norm1_gain, xh1, rstd1)
-
-    shared = gather_back(scatter_sum(jnp.concatenate(weight_rows + [go], axis=0)).astype(bf16))
-    sides = shared[:, :, : 3 * mine].reshape(nx, 2, heads, 3, HD, D)
-    grads = []
-    for p in range(3):
-        grads.append(jnp.transpose(sides[:, :, :, p].reshape(D, D)).astype(f32))
-    grad_output = shared[:, :, 3 * mine :].reshape(D, D).astype(f32)
-    grad_norm1 = 0.0
-    for g, w in zip(grads, (w_query, w_key, w_value)):
-        grad_norm1 = grad_norm1 + jnp.sum(g * w.astype(f32), axis=1)
-    grad_norm1 = grad_norm1 / norm1_gain
 
     router_rows = (jnp.arange(experts) == expert_id).astype(f32)[:, None] * router_row
     sig = jnp.pad(jnp.sum(hot * gating[:, None], axis=0), (0, D - experts))
@@ -599,7 +618,7 @@
         grads[0],
         grads[1],
         grads[2],
-        grad_output,
+        grads[3],
         grad_norm2,
         grad_router,
         grad_in,

time: 512 us -> 589 us (1.15)
  blocking collectives: 0 us -> 151 us
  waiting for transfers between devices: 178 us -> 107 us
  starting transfers between devices: 86.6 us -> 49.3 us
  local copies, waits for them, and re-layouts: 53.9 us -> 82 us
  other arithmetic: 37.3 us -> 52.6 us
    all_gather x0 -> x2, blocking collectives: none -> 151 us  [sum_all(): return jnp.sum(lax.all_gather(v, ('dp', 'x', 'core', 'expert')), axis=0)]
    all_to_all x13 -> x8, waiting for transfers between devices: 53.1 us -> 12.7 us  [the longest x4 9.76 us: turn(): lax.all_to_all(v, ('x', 'core'), split_axis=0, concat_axis=0, tiled=True)]
    ppermute x18 -> x12, waiting for transfers between devices: 86.3 us -> 62.3 us  [shift(): return lax.ppermute(v, axis, [(i, (i + step) % n) for i in range(n)])]
    all_to_all x13 -> x8, starting transfers between devices: 50.4 us -> 32.9 us  [the longest x4 17.3 us: trade(): lax.all_to_all(v.reshape(nx * owners, cap, D), ('x', 'expert'), split_axi...]
    ppermute x18 -> x12, starting transfers between devices: 22.1 us -> 6.91 us  [shift(): return lax.ppermute(v, axis, [(i, (i + step) % n) for i in range(n)])]
    dynamic_update_slice x12, local copies, waits for them, and re-layouts: 12.7 us -> 24.3 us  [place(): out = lax.dynamic_update_index_in_dim(out, piece, index, 0)]
    ppermute x14 -> x8, waiting for transfers between devices: 38.6 us -> 32.3 us  [swap(): return lax.ppermute(v, axis, [(0, 1), (1, 0)])]
    ppermute x14 -> x8, starting transfers between devices: 14.1 us -> 9.5 us  [swap(): return lax.ppermute(v, axis, [(0, 1), (1, 0)])]
  transfers between devices with their start and end apart: 45 -> 28, of which waited for: 26 -> 12; matrix products, arithmetic and copies ran while one was open for 19% -> 19% of each run, Pallas kernels for 15% -> 12%
where the time goes in v2:
time: 589 us; the launch traced here: 583 us
  blocking collectives  151 us (26%)
  waiting for transfers between devices  107 us (18%)
  Pallas kernels  101 us (17%)
  local copies, waits for them, and re-layouts  82 us (14%)
  other arithmetic  52.6 us (9%)
  starting transfers between devices  49.3 us (8%)
  matrix products  36.6 us (6%)
    all_gather x2, blocking collectives, sum_all(): return jnp.sum(lax.all_gather(v, ('dp', 'x', 'core', 'expert')), axis=0)  151 us
    ppermute x12, waiting for transfers between devices, shift(): return lax.ppermute(v, axis, [(i, (i + step) % n) for i in range(n)])  62.3 us
    dot_general x15, matrix products, dg(): lax.dot_general(a, b, (((ca,), (cb,)), ((), ())), preferred_element_type=...  36.6 us
    ppermute x8, waiting for transfers between devices, swap(): return lax.ppermute(v, axis, [(0, 1), (1, 0)])  32.3 us
    pallas_call x3, Pallas kernels, attend_back(): pl.pallas_call(functools.partial(attend_back_kernel, h % 2 * HD, hv % 2 *...  28 us
    pallas_call x1, Pallas kernels, expert_mid(): pl.pallas_call(mid_kernel, out_shape=(jax.ShapeDtypeStruct((rows, ff), bf...  24.8 us
    unnamed x94, local copies, waits for them, and re-layouts  24.7 us
    dynamic_update_slice x12, local copies, waits for them, and re-layouts, place(): out = lax.dynamic_update_index_in_dim(out, piece, index, 0)  24.3 us
  transfers between devices with their start and end apart: 28, of which 12 were waited for; matrix products, arithmetic and copies ran while one was open for 19% of the time, Pallas kernels for 12%

profile of v2, /device:TPU:0, one launch (start us, length us, event | category | flops | bytes accessed | tf_op | source)
XLA Modules:
  0.0 583.1 jit_solution(17016827135745394930)
XLA Ops:
  14.7 11.6 %collective-permute-done.1 = bf16[512,768]{1,0:T(8,128)(2,1)} collective-permute-done((bf16[512,768]{1,0:T(8,128)(2,1)}, bf16[512,768]{1,0:T(8,128)(2,1)}, u32[]{:S(2)}, u32[]{:S(2)}) %collective-permute-start.1) | collective-permute-done | bytes 786464 | tf_op jit(solution)/shard_map/ppermute | solution.py:383
  29.4 4.1 all-to-all-start
  40.0 5.0 convolution_convert_fusion.1.k_ref.refs_1_.refs_3_
  44.9 5.8 %convolution_convert_fusion.qT_ref.vT_ref.refs_0_.refs_2_ = bf16[576,2048]{1,0:T(8,128)(2,1)} fusion(bf16[2048,768]{1,0:T(8,128)(2,1)} %bitcast.7, bf16[768,192]{1,0:T(8,128)(2,1)S(1)} %copy-done.26, bf16[768,192]{1,0:T(8,128)(2,1)S(1)} %copy-done.27, bf16[768,192]{1,0:T(8,128)(2,1)S(1)} %copy-done.25), kind=kOutput, calls=%fused_computation.1 | convolution fusion | flops 1815773184 | bytes 6389760 | tf_op jit(solution)/shard_map/dot_general | solution.py:26
  50.8 14.2 %attend.1 = (f32[192,2048]{1,0:T(8,128)}, bf16[4,3,64,512]{3,2,1,0:T(8,128)(2,1)}, f32[3,1,2048]{2,1,0:T(1,128)}) custom-call(bf16[576,2048]{1,0:T(8,128)(2,1)} %convolution_convert_fusion.qT_ref.vT_ref.refs_0_.refs_2_, bf16[2048,384]{1,0:T(8,128)(2,1)} %convolution_convert_fusion.1.k_ref.refs_1_.refs_3_, ...), custom_call_target="tpu_custom_call" | custom-call | flops 6442450944 | bytes 5505024 | tf_op jit(solution)/shard_map/attend/pallas_call | solution.py:67
  71.5 9.8 %all-to-all-done.1 = bf16[4,3,64,512]{3,2,1,0:T(8,128)(2,1)S(1)} async-done(((bf16[4,3,64,512]{3,2,1,0:T(8,128)(2,1)}), bf16[4,3,64,512]{3,2,1,0:T(8,128)(2,1)S(1)}, u32[]{:S(2)}, u32[]{:S(2)}) %all-to-all-start.1) | async-done | bytes 786464 | tf_op jit(solution)/shard_map/all_to_all | solution.py:515
  87.4 4.3 all-to-all-start.2
  91.7 10.1 %expert_up.1.u_ref = bf16[1024,3072]{1,0:T(8,128)(2,1)} custom-call(s32[2]{0:T(128)} %pad_add_fusion.pick_ref, bf16[1024,768]{1,0:T(8,128)(2,1)} %bitcast.226, bf16[2,3072,768]{2,1,0:T(8,128)(2,1)} %wo_ref.3), custom_call_target="tpu_custom_call" | custom-call | flops 4831838208 | bytes 12582912 | tf_op jit(solution)/shard_map/expert_up/pallas_call | solution.py:194
  102.9 73.6 %all_gather.13 = f32[32,8,128]{2,1,0:T(8,128)} all-gather(f32[1,8,128]{2,1,0:T(8,128)S(1)} %scatter.4), channel_id=1, replica_groups=mesh['dp'=4,'x'=2,'core'=2,'expert'=2] {'dp','x','core','expert'}, dimensions={0}, use_global_device_ids=true | all-gather | bytes 135168 | tf_op jit(solution)/shard_map/all_gather | solution.py:409
  180.4 24.8 %expert_mid.1 = (bf16[1024,3072]{1,0:T(8,128)(2,1)}, bf16[1024,3072]{1,0:T(8,128)(2,1)}, bf16[1024,768]{1,0:T(8,128)(2,1)}, f32[1,768]{1,0:T(1,128)}, f32[1024,128]{1,0:T(8,128)}) custom-call(s32[2]{0:T(128)} %pad_add_fusion.pick_ref, bf16[1024,768]{1,0:T(8,128)(2,1)} %bitcast.13.x_ref, bf16[1024,3072]{1,0:T(8,128)(2,1)} %expert_up.1.u_ref, ...), custom_call_target="tpu_custom_call" | custom-call | flops 9663676416 | bytes 28311552 | tf_op jit(solution)/shard_map/expert_mid/pallas_call | solution.py:265
  205.3 4.5 all-to-all-start.3
  209.8 24.2 %expert_grads.1 = (bf16[4,2,2,192,768]{4,3,2,1,0:T(8,128)(2,1)}, bf16[4,2,2,192,768]{4,3,2,1,0:T(8,128)(2,1)}, bf16[1024,768]{1,0:T(8,128)(2,1)}) custom-call(s32[2]{0:T(128)} %pad_add_fusion.pick_ref, bf16[1024,768]{1,0:T(8,128)(2,1)} %bitcast.13.x_ref, bf16[1024,768]{1,0:T(8,128)(2,1)} %bitcast.227, f32[1024,128]{1,0:T(8,128)} %get-tuple-element.67.gate_ref, ...), custom_call_target="tpu_custom_call" | custom-call | flops 14495514624 | bytes 31457280 | tf_op jit(solution)/shard_map/expert_grads/pallas_call | solution.py:350
  234.1 3.6 multiply_reduce_fusion.3
  246.9 7.4 %add_convert_fusion = bf16[4,2,2,192,768]{4,3,2,1,0:T(8,128)(2,1)} fusion(bf16[4,2,2,192,768]{4,3,2,1,0:T(8,128)(2,1)} %collective-permute-done.3, bf16[4,2,2,192,768]{4,3,2,1,0:T(8,128)(2,1)} %get-tuple-element.74), kind=kLoop, calls=%fused_computation | loop fusion | flops 9437184 | bytes 14155776 | tf_op jit(solution)/shard_map/convert_element_type | solution.py:553
  258.7 4.1 all-to-all-start.4
  267.0 9.3 %attend_back_head0.1 = (bf16[3,192,2048]{2,1,0:T(8,128)(2,1)}, bf16[4,3,192,512]{3,2,1,0:T(8,128)(2,1)}) custom-call(bf16[576,2048]{1,0:T(8,128)(2,1)} %convolution_convert_fusion.qT_ref.vT_ref.refs_0_.refs_2_, bf16[2048,384]{1,0:T(8,128)(2,1)} %convolution_convert_fusion.1.k_ref.refs_1_.refs_3_, ...), custom_call_target="tpu_custom_call" | custom-call | flops 5368709120 | bytes 3145728 | tf_op jit(solution)/shard_map/attend_back_head0/pallas_call | solution.py:165
  276.3 10.8 %collective-permute-done.4 = bf16[2,2,192,768]{3,2,1,0:T(8,128)(2,1)} collective-permute-done((bf16[2,2,192,768]{3,2,1,0:T(8,128)(2,1)}, bf16[2,2,192,768]{3,2,1,0:T(8,128)(2,1)}, u32[]{:S(2)}, u32[]{:S(2)}) %collective-permute-start.4) | collective-permute-done | bytes 1179680 | tf_op jit(solution)/shard_map/ppermute | solution.py:388
  294.8 7.1 %collective-permute-done.7 = bf16[192,768]{1,0:T(8,128)(2,1)} collective-permute-done((bf16[192,768]{1,0:T(8,128)(2,1)}, bf16[192,768]{1,0:T(8,128)(2,1)}, u32[]{:S(2)}, u32[]{:S(2)}) %collective-permute-start.7) | collective-permute-done | bytes 294944 | tf_op jit(solution)/shard_map/ppermute | solution.py:383
  302.9 9.3 %attend_back_head1.1 = (bf16[3,192,2048]{2,1,0:T(8,128)(2,1)}, bf16[4,3,192,512]{3,2,1,0:T(8,128)(2,1)}) custom-call(bf16[576,2048]{1,0:T(8,128)(2,1)} %convolution_convert_fusion.qT_ref.vT_ref.refs_0_.refs_2_, bf16[2048,384]{1,0:T(8,128)(2,1)} %convolution_convert_fusion.1.k_ref.refs_1_.refs_3_, ...), custom_call_target="tpu_custom_call", output_to_operand_aliasing={{0}: (7, {}), {1}: (8, {})} | custom-call | flops 5368709120 | bytes 3145728 | tf_op jit(solution)/shard_map/attend_back_head1/pallas_call | solution.py:165
  312.3 7.9 %collective-permute-done.5 = bf16[2,2,192,768]{3,2,1,0:T(8,128)(2,1)} collective-permute-done((bf16[2,2,192,768]{3,2,1,0:T(8,128)(2,1)}, bf16[2,2,192,768]{3,2,1,0:T(8,128)(2,1)}, u32[]{:S(2)}, u32[]{:S(2)}) %collective-permute-start.5) | collective-permute-done | bytes 1179680 | tf_op jit(solution)/shard_map/ppermute | solution.py:388
  323.0 9.3 %attend_back_head2.1 = (bf16[3,192,2048]{2,1,0:T(8,128)(2,1)}, bf16[4,3,192,512]{3,2,1,0:T(8,128)(2,1)}) custom-call(bf16[576,2048]{1,0:T(8,128)(2,1)} %convolution_convert_fusion.qT_ref.vT_ref.refs_0_.refs_2_, bf16[2048,384]{1,0:T(8,128)(2,1)} %convolution_convert_fusion.1.k_ref.refs_1_.refs_3_, ...), custom_call_target="tpu_custom_call", output_to_operand_aliasing={{0}: (7, {}), {1}: (8, {})} | custom-call | flops 5368709120 | bytes 3145728 | tf_op jit(solution)/shard_map/attend_back_head2/pallas_call | solution.py:165
  332.4 4.8 fusion.81
  359.5 77.2 %all-gather.1 = f32[32,6,768]{2,1,0:T(8,128)} all-gather(f32[1,6,768]{2,1,0:T(8,128)S(1)} %maximum_bitcast_fusion), channel_id=2, replica_groups=mesh['dp'=4,'x'=2,'core'=2,'expert'=2] {'dp','x','core','expert'}, dimensions={0}, use_global_device_ids=true | all-gather | bytes 608256 | tf_op jit(solution)/shard_map/all_gather | solution.py:409
  442.0 4.5 all-to-all-start.6
  446.5 4.5 collective-permute-start.13
  451.0 20.9 %collective-permute-done.12 = bf16[96,768]{1,0:T(8,128)(2,1)} collective-permute-done((bf16[96,768]{1,0:T(8,128)(2,1)}, bf16[96,768]{1,0:T(8,128)(2,1)}, u32[]{:S(2)}, u32[]{:S(2)}) %collective-permute-start.12) | collective-permute-done | bytes 147488 | tf_op jit(solution)/shard_map/ppermute | solution.py:388
  484.4 7.4 %collective-permute-done.15 = bf16[384,768]{1,0:T(8,128)(2,1)} collective-permute-done((bf16[384,768]{1,0:T(8,128)(2,1)}, bf16[384,768]{1,0:T(8,128)(2,1)}, u32[]{:S(2)}, u32[]{:S(2)}) %collective-permute-start.15) | collective-permute-done | bytes 589856 | tf_op jit(solution)/shard_map/ppermute | solution.py:388
  500.5 4.4 all-to-all-start.7
  509.0 13.9 %collective-permute-done.16 = bf16[768,768]{1,0:T(8,128)(2,1)} collective-permute-done((bf16[768,768]{1,0:T(8,128)(2,1)}, bf16[768,768]{1,0:T(8,128)(2,1)}, u32[]{:S(2)}, u32[]{:S(2)}) %collective-permute-start.16) | collective-permute-done | bytes 1179680 | tf_op jit(solution)/shard_map/ppermute | solution.py:388
  525.3 10.3 %collective-permute-done.19 = bf16[2,192,768]{2,1,0:T(8,128)(2,1)} collective-permute-done((bf16[2,192,768]{2,1,0:T(8,128)(2,1)}, bf16[2,192,768]{2,1,0:T(8,128)(2,1)}, u32[]{:S(2)}, u32[]{:S(2)}) %collective-permute-start.19) | collective-permute-done | bytes 589856 | tf_op jit(solution)/shard_map/ppermute | solution.py:383
  550.6 3.5 fusion.26
  557.4 3.8 fusion.76
  (228 shorter events, 163.8 us)
Async XLA Ops:
  0.6 81.5 %copy-start = (bf16[768,768]{1,0:T(8,128)(2,1)S(1)}, bf16[768,768]{1,0:T(8,128)(2,1)}, u32[]{:S(2)}) copy-start(bf16[768,768]{1,0:T(8,128)(2,1)} %param.21) | copy-start | bytes 3538948
  4.9 28.7 %collective-permute-start = (bf16[512,768]{1,0:T(8,128)(2,1)}, bf16[512,768]{1,0:T(8,128)(2,1)}, u32[]{:S(2)}, u32[]{:S(2)}) collective-permute-start(bf16[512,768]{1,0:T(8,128)(2,1)} %fusion.15), channel_id=1, source_target_pairs={{0,2},{2,0},{1,3},{3,1},{4,6},{6,4},{5,7},{7,5},{8,10},{10,8},{9,1... | collective-permute-start | bytes 2359304 | tf_op jit(solution)/shard_map/ppermute | solution.py:383
  5.3 21.0 %collective-permute-start.1 = (bf16[512,768]{1,0:T(8,128)(2,1)}, bf16[512,768]{1,0:T(8,128)(2,1)}, u32[]{:S(2)}, u32[]{:S(2)}) collective-permute-start(bf16[512,768]{1,0:T(8,128)(2,1)} %fusion.15), channel_id=1, source_target_pairs={{0,4},{4,0},{1,5},{5,1},{2,6},{6,2},{3,7},{7,3},{8,12},{12,8},{9,1... | collective-permute-start | bytes 2359304 | tf_op jit(solution)/shard_map/ppermute | solution.py:383
  26.3 11.5 %collective-permute-start.2 = (bf16[512,768]{1,0:T(8,128)(2,1)}, bf16[512,768]{1,0:T(8,128)(2,1)}, u32[]{:S(2)}, u32[]{:S(2)}) collective-permute-start(bf16[512,768]{1,0:T(8,128)(2,1)} %collective-permute-done.1), channel_id=1, source_target_pairs={{0,2},{2,0},{1,3},{3,1},{4,6},{6,4},{5,7},{7,5},{8,10},{10,8},{9,1... | collective-permute-start | bytes 2359304 | tf_op jit(solution)/shard_map/ppermute | solution.py:383
  29.4 35.5 %all-to-all-start = ((bf16[4,256,768]{2,1,0:T(8,128)(2,1)}), bf16[4,256,768]{2,1,0:T(8,128)(2,1)S(1)}, u32[]{:S(2)}, u32[]{:S(2)}) async-start(bf16[4,256,768]{2,1,0:T(8,128)(2,1)} %bitcast.228), calls=%async_computation | async-start | bytes 3145728 | tf_op jit(solution)/shard_map/all_to_all | solution.py:511
  66.1 15.1 %all-to-all-start.1 = ((bf16[4,3,64,512]{3,2,1,0:T(8,128)(2,1)}), bf16[4,3,64,512]{3,2,1,0:T(8,128)(2,1)S(1)}, u32[]{:S(2)}, u32[]{:S(2)}) async-start(bf16[4,3,64,512]{3,2,1,0:T(8,128)(2,1)} %get-tuple-element.64), calls=%async_computation.1 | async-start | bytes 1572864 | tf_op jit(solution)/shard_map/all_to_all | solution.py:515
  87.4 91.9 %all-to-all-start.2 = ((bf16[4,256,768]{2,1,0:T(8,128)(2,1)}), bf16[4,256,768]{2,1,0:T(8,128)(2,1)}, u32[]{:S(2)}, u32[]{:S(2)}) async-start(bf16[4,256,768]{2,1,0:T(8,128)(2,1)} %bitcast.229), calls=%async_computation.2 | async-start | bytes 3145728 | tf_op jit(solution)/shard_map/all_to_all | solution.py:511
  205.3 28.7 %all-to-all-start.3 = ((bf16[4,256,768]{2,1,0:T(8,128)(2,1)}), bf16[4,256,768]{2,1,0:T(8,128)(2,1)}, u32[]{:S(2)}, u32[]{:S(2)}) async-start(bf16[4,256,768]{2,1,0:T(8,128)(2,1)} %bitcast.230), calls=%async_computation.3 | async-start | bytes 3145728 | tf_op jit(solution)/shard_map/all_to_all | solution.py:511
  234.0 12.9 %collective-permute-start.3 = (bf16[4,2,2,192,768]{4,3,2,1,0:T(8,128)(2,1)}, bf16[4,2,2,192,768]{4,3,2,1,0:T(8,128)(2,1)}, u32[]{:S(2)}, u32[]{:S(2)}) collective-permute-start(bf16[4,2,2,192,768]{4,3,2,1,0:T(8,128)(2,1)} %get-tuple-element.75), channel_id=1, source_target_pairs={{0,2},{2,0},{1,3},{3,1},{4,6},{6,4},{5,7},{7,5},{8,10},{10,8},{9,1... | collective-permute-start | bytes 14155784 | tf_op jit(solution)/shard_map/ppermute | solution.py:383
  242.6 11.6 %copy-start.15 = (bf16[768,512]{1,0:T(8,128)(2,1)}, bf16[768,512]{1,0:T(8,128)(2,1)S(1)}, u32[]{:S(2)}) copy-start(bf16[768,512]{1,0:T(8,128)(2,1)S(1)} %copy.43) | copy-start | bytes 2359300
  243.4 10.8 %all-to-all-start.5 = ((bf16[4,1,64,512]{3,2,1,0:T(8,128)(2,1)}), bf16[4,1,64,512]{3,2,1,0:T(8,128)(2,1)S(1)}, u32[]{:S(2)}, u32[]{:S(2)}) async-start(bf16[4,1,64,512]{3,2,1,0:T(8,128)(2,1)} %slice.77), calls=%async_computation.5 | async-start | bytes 524288 | tf_op jit(solution)/shard_map/all_to_all | solution.py:515
  256.7 30.4 %collective-permute-start.4 = (bf16[2,2,192,768]{3,2,1,0:T(8,128)(2,1)}, bf16[2,2,192,768]{3,2,1,0:T(8,128)(2,1)}, u32[]{:S(2)}, u32[]{:S(2)}) collective-permute-start(bf16[2,2,192,768]{3,2,1,0:T(8,128)(2,1)} %dynamic-slice_bitcast_fusion), channel_id=1, source_target_pairs={{0,8},{8,16},{16,24},{24,0},{1,9},{9,17},{17,25},{25,1},{2,10},{10... | collective-permute-start | bytes 3538952 | tf_op jit(solution)/shard_map/ppermute | solution.py:388
  258.7 31.4 %all-to-all-start.4 = ((bf16[4,2,64,512]{3,2,1,0:T(8,128)(2,1)}), bf16[4,2,64,512]{3,2,1,0:T(8,128)(2,1)}, u32[]{:S(2)}, u32[]{:S(2)}) async-start(bf16[4,2,64,512]{3,2,1,0:T(8,128)(2,1)} %slice.76), calls=%async_computation.4 | async-start | bytes 1048576 | tf_op jit(solution)/shard_map/all_to_all | solution.py:515
  266.5 24.0 %collective-permute-start.6 = (bf16[2,192,768]{2,1,0:T(8,128)(2,1)S(1)}, bf16[2,192,768]{2,1,0:T(8,128)(2,1)}, u32[]{:S(2)}, u32[]{:S(2)}) collective-permute-start(bf16[2,192,768]{2,1,0:T(8,128)(2,1)S(1)} %fusion.49), channel_id=1, source_target_pairs={{0,2},{2,0},{1,3},{3,1},{4,6},{6,4},{5,7},{7,5},{8,10},{10,8},{9,1... | collective-permute-start | bytes 1769480 | tf_op jit(solution)/shard_map/ppermute | solution.py:383
  290.1 30.0 %collective-permute-start.5 = (bf16[2,2,192,768]{3,2,1,0:T(8,128)(2,1)}, bf16[2,2,192,768]{3,2,1,0:T(8,128)(2,1)}, u32[]{:S(2)}, u32[]{:S(2)}) collective-permute-start(bf16[2,2,192,768]{3,2,1,0:T(8,128)(2,1)} %fusion.1), channel_id=1, source_target_pairs={{0,8},{8,16},{16,24},{24,0},{1,9},{9,17},{17,25},{25,1},{2,10},{10... | collective-permute-start | bytes 3538952 | tf_op jit(solution)/shard_map/ppermute | solution.py:388
  292.8 9.1 %collective-permute-start.7 = (bf16[192,768]{1,0:T(8,128)(2,1)}, bf16[192,768]{1,0:T(8,128)(2,1)}, u32[]{:S(2)}, u32[]{:S(2)}) collective-permute-start(bf16[192,768]{1,0:T(8,128)(2,1)} %fusion.55), channel_id=1, source_target_pairs={{0,4},{4,0},{1,5},{5,1},{2,6},{6,2},{3,7},{7,3},{8,12},{12,8},{9,1... | collective-permute-start | bytes 884744 | tf_op jit(solution)/shard_map/ppermute | solution.py:383
  339.6 14.6 %collective-permute-start.8 = (bf16[384,768]{1,0:T(8,128)(2,1)}, bf16[384,768]{1,0:T(8,128)(2,1)}, u32[]{:S(2)}, u32[]{:S(2)}) collective-permute-start(bf16[384,768]{1,0:T(8,128)(2,1)} %fusion.47), channel_id=1, source_target_pairs={{0,1},{1,0},{2,3},{3,2},{4,5},{5,4},{6,7},{7,6},{8,9},{9,8},{10,11... | collective-permute-start | bytes 1769480 | tf_op jit(solution)/shard_map/ppermute | solution.py:383
  357.5 81.1 %collective-permute-start.10 = (bf16[96,768]{1,0:T(8,128)(2,1)}, bf16[96,768]{1,0:T(8,128)(2,1)}, u32[]{:S(2)}, u32[]{:S(2)}) collective-permute-start(bf16[96,768]{1,0:T(8,128)(2,1)} %get-tuple-element.144), channel_id=1, source_target_pairs={{0,16},{8,24},{16,0},{24,8},{1,17},{9,25},{17,1},{25,9},{2,18},{10... | collective-permute-start | bytes 442376 | tf_op jit(solution)/shard_map/ppermute | solution.py:388
  357.5 81.1 %collective-permute-start.11 = (bf16[96,768]{1,0:T(8,128)(2,1)}, bf16[96,768]{1,0:T(8,128)(2,1)}, u32[]{:S(2)}, u32[]{:S(2)}) collective-permute-start(bf16[96,768]{1,0:T(8,128)(2,1)} %get-tuple-element.143), channel_id=1, source_target_pairs={{0,24},{8,0},{16,8},{24,16},{1,25},{9,1},{17,9},{25,17},{2,26},{10... | collective-permute-start | bytes 442376 | tf_op jit(solution)/shard_map/ppermute | solution.py:388
  358.7 79.9 %collective-permute-start.9 = (bf16[96,768]{1,0:T(8,128)(2,1)}, bf16[96,768]{1,0:T(8,128)(2,1)}, u32[]{:S(2)}, u32[]{:S(2)}) collective-permute-start(bf16[96,768]{1,0:T(8,128)(2,1)} %get-tuple-element.142), channel_id=1, source_target_pairs={{0,8},{8,16},{16,24},{24,0},{1,9},{9,17},{17,25},{25,1},{2,10},{10... | collective-permute-start | bytes 442376 | tf_op jit(solution)/shard_map/ppermute | solution.py:388
  438.5 44.0 %collective-permute-start.18 = (bf16[2,2,192,768]{3,2,1,0:T(8,128)(2,1)}, bf16[2,2,192,768]{3,2,1,0:T(8,128)(2,1)}, u32[]{:S(2)}, u32[]{:S(2)}) collective-permute-start(bf16[2,2,192,768]{3,2,1,0:T(8,128)(2,1)} %fusion), channel_id=1, source_target_pairs={{0,8},{8,16},{16,24},{24,0},{1,9},{9,17},{17,25},{25,1},{2,10},{10... | collective-permute-start | bytes 3538952 | tf_op jit(solution)/shard_map/ppermute | solution.py:388
  441.4 30.5 %collective-permute-start.12 = (bf16[96,768]{1,0:T(8,128)(2,1)}, bf16[96,768]{1,0:T(8,128)(2,1)}, u32[]{:S(2)}, u32[]{:S(2)}) collective-permute-start(bf16[96,768]{1,0:T(8,128)(2,1)} %get-tuple-element.130), channel_id=1, source_target_pairs={{0,8},{8,16},{16,24},{24,0},{1,9},{9,17},{17,25},{25,1},{2,10},{10... | collective-permute-start | bytes 442376 | tf_op jit(solution)/shard_map/ppermute | solution.py:388
  442.0 58.6 %all-to-all-start.6 = ((bf16[4,3,192,512]{3,2,1,0:T(8,128)(2,1)}), bf16[4,3,192,512]{3,2,1,0:T(8,128)(2,1)}, u32[]{:S(2)}, u32[]{:S(2)}) async-start(bf16[4,3,192,512]{3,2,1,0:T(8,128)(2,1)} %get-tuple-element.91), calls=%async_computation.6 | async-start | bytes 4718592 | tf_op jit(solution)/shard_map/all_to_all | solution.py:515
  446.5 28.3 %collective-permute-start.13 = (bf16[96,768]{1,0:T(8,128)(2,1)}, bf16[96,768]{1,0:T(8,128)(2,1)S(1)}, u32[]{:S(2)}, u32[]{:S(2)}) collective-permute-start(bf16[96,768]{1,0:T(8,128)(2,1)} %get-tuple-element.130), channel_id=1, source_target_pairs={{0,16},{8,24},{16,0},{24,8},{1,17},{9,25},{17,1},{25,9},{2,18},{10... | collective-permute-start | bytes 442376 | tf_op jit(solution)/shard_map/ppermute | solution.py:388
  451.0 24.5 %collective-permute-start.14 = (bf16[96,768]{1,0:T(8,128)(2,1)}, bf16[96,768]{1,0:T(8,128)(2,1)S(1)}, u32[]{:S(2)}, u32[]{:S(2)}) collective-permute-start(bf16[96,768]{1,0:T(8,128)(2,1)} %get-tuple-element.130), channel_id=1, source_target_pairs={{0,24},{8,0},{16,8},{24,16},{1,25},{9,1},{17,9},{25,17},{2,26},{10... | collective-permute-start | bytes 442376 | tf_op jit(solution)/shard_map/ppermute | solution.py:388
  476.2 15.6 %collective-permute-start.15 = (bf16[384,768]{1,0:T(8,128)(2,1)}, bf16[384,768]{1,0:T(8,128)(2,1)}, u32[]{:S(2)}, u32[]{:S(2)}) collective-permute-start(bf16[384,768]{1,0:T(8,128)(2,1)} %bitcast.52), channel_id=1, source_target_pairs={{0,1},{1,0},{2,3},{3,2},{4,5},{5,4},{6,7},{7,6},{8,9},{9,8},{10,11... | collective-permute-start | bytes 1769480 | tf_op jit(solution)/shard_map/ppermute | solution.py:388
  484.4 13.8 %copy-start.6 = (f32[2,2,192,768]{3,2,1,0:T(8,128)}, f32[2,2,192,768]{3,2,1,0:T(8,128)S(1)}, u32[]{:S(2)}) copy-start(f32[2,2,192,768]{3,2,1,0:T(8,128)S(1)} %convert_add_fusion) | copy-start | bytes 7077892
  493.7 29.2 %collective-permute-start.16 = (bf16[768,768]{1,0:T(8,128)(2,1)}, bf16[768,768]{1,0:T(8,128)(2,1)}, u32[]{:S(2)}, u32[]{:S(2)}) collective-permute-start(bf16[768,768]{1,0:T(8,128)(2,1)} %bitcast.55), channel_id=1, source_target_pairs={{0,4},{4,0},{1,5},{5,1},{2,6},{6,2},{3,7},{7,3},{8,12},{12,8},{9,1... | collective-permute-start | bytes 3538952 | tf_op jit(solution)/shard_map/ppermute | solution.py:388
  494.6 41.0 %collective-permute-start.19 = (bf16[2,192,768]{2,1,0:T(8,128)(2,1)}, bf16[2,192,768]{2,1,0:T(8,128)(2,1)}, u32[]{:S(2)}, u32[]{:S(2)}) collective-permute-start(bf16[2,192,768]{2,1,0:T(8,128)(2,1)} %fusion.48), channel_id=1, source_target_pairs={{0,4},{4,0},{1,5},{5,1},{2,6},{6,2},{3,7},{7,3},{8,12},{12,8},{9,1... | collective-permute-start | bytes 1769480 | tf_op jit(solution)/shard_map/ppermute | solution.py:383
  500.5 50.1 %all-to-all-start.7 = ((bf16[4,256,768]{2,1,0:T(8,128)(2,1)}), bf16[4,256,768]{2,1,0:T(8,128)(2,1)}, u32[]{:S(2)}, u32[]{:S(2)}) async-start(bf16[4,256,768]{2,1,0:T(8,128)(2,1)} %bitcast.225), calls=%async_computation.7 | async-start | bytes 3145728 | tf_op jit(solution)/shard_map/all_to_all | solution.py:511
  509.0 26.6 %copy-start.7 = (f32[2,2,192,768]{3,2,1,0:T(8,128)S(1)}, f32[2,2,192,768]{3,2,1,0:T(8,128)}, u32[]{:S(2)}) copy-start(f32[2,2,192,768]{3,2,1,0:T(8,128)} %copy-done.6) | copy-start | bytes 7077892
  525.3 28.8 %collective-permute-start.17 = (bf16[2,768,768]{2,1,0:T(8,128)(2,1)}, bf16[2,768,768]{2,1,0:T(8,128)(2,1)}, u32[]{:S(2)}, u32[]{:S(2)}) collective-permute-start(bf16[2,768,768]{2,1,0:T(8,128)(2,1)} %bitcast_dynamic-update-slice_fusion.2), channel_id=1, source_target_pairs={{0,2},{2,0},{1,3},{3,1},{4,6},{6,4},{5,7},{7,5},{8,10},{10,8},{9,1... | collective-permute-start | bytes 7077896 | tf_op jit(solution)/shard_map/ppermute | solution.py:388
  (40 other events, 138.9 us)

commit v3 on v2

--- a/solution.py
+++ b/solution.py
@@ -24,6 +24,54 @@
 
 def dg(a, b, ca, cb):
     return lax.dot_general(a, b, (((ca,), (cb,)), ((), ())), preferred_element_type=f32)
+
+
+def project_kernel(place_ref, tok_ref, gain_ref, w_ref, *refs):
+    normed_ref, qkvT_ref, kv_ref = refs[-3:]
+    x = tok_ref[...].astype(f32)
+    centred = x - jnp.mean(x, axis=1, keepdims=True)
+    rstd = lax.rsqrt(jnp.mean(centred * centred, axis=1, keepdims=True) + norm_eps)
+    normed = (centred * rstd * gain_ref[...]).astype(bf16)
+    normed_ref[...] = normed
+    qkv = dg(normed, w_ref[...], 1, 0).astype(bf16)
+    kv_ref[...] = qkv[:, qkv.shape[1] - kv_ref.shape[1] :]
+    qkvT_ref[...] = qkv.T
+
+
+def project(place, tok, gain, w, ctx, so_far):
+    rows = tok.shape[0]
+    wide = w.shape[1]
+    args = [tok, gain, w]
+    specs = [pl.BlockSpec(a.shape, lambda i, p: (0, 0)) for a in args]
+    alias = {}
+    if so_far is not None:
+        alias = {4: 0, 5: 1, 6: 2}
+        args += list(so_far)
+        specs += [pl.BlockSpec(memory_space=pl.ANY)] * 3
+    return pl.pallas_call(
+        project_kernel,
+        out_shape=(
+            jax.ShapeDtypeStruct((ctx * rows, D), bf16),
+            jax.ShapeDtypeStruct((wide, ctx * rows), bf16),
+            jax.ShapeDtypeStruct((ctx * rows, 2 * wide // 3), bf16),
+        ),
+        grid_spec=pltpu.PrefetchScalarGridSpec(
+            num_scalar_prefetch=1,
+            grid=(1,),
+            in_specs=specs,
+            out_specs=(
+                pl.BlockSpec((rows, D), lambda i, p: (p[0], 0)),
+                pl.BlockSpec((wide, rows), lambda i, p: (0, p[0])),
+                pl.BlockSpec((rows, 2 * wide // 3), lambda i, p: (p[0], 0)),
+            ),
+        ),
+        input_output_aliases=alias,
+        compiler_params=pltpu.CompilerParams(vmem_limit_bytes=VMEM),
+        cost_estimate=pl.CostEstimate(
+            flops=4 * rows * D * wide, bytes_accessed=4 * rows * D + 8 * rows * wide, transcendentals=0
+        ),
+        name="project",
+    )(place.astype(jnp.int32).reshape(1), *args)
 
 
 def attend_kernel(heads, blk, qT_ref, k_ref, vT_ref, oT_ref, osend_ref, lse_ref):
@@ -379,6 +427,113 @@
     )(pick, x, dy, gate, act, gh, w_out)
 
 
+def weight_rows_kernel(half_ref, dT_ref, normed_ref, go_ref, small_ref, keep_ref, send_ref, acc):
+    n = dT_ref.shape[0]
+    half = keep_ref.shape[0]
+    acc[:n] = dg(dT_ref[...], normed_ref[...], 1, 0)
+    acc[n:] = go_ref[...]
+    a = pl.multiple_of(half_ref[0] * half, half)
+    b = pl.multiple_of((1 - half_ref[0]) * half, half)
+    keep_ref[...] = acc[pl.ds(a, half)]
+    send_ref[:half] = acc[pl.ds(b, half)].astype(bf16)
+    send_ref[half:] = small_ref[...]
+
+
+def weight_rows(half, dT, normed, go, small):
+    rows = dT.shape[0] + go.shape[0]
+    extra = small.shape[0]
+    args = (dT, normed, go, small)
+    return pl.pallas_call(
+        weight_rows_kernel,
+        out_shape=(
+            jax.ShapeDtypeStruct((rows // 2, D), f32),
+            jax.ShapeDtypeStruct((rows // 2 + extra, D), bf16),
+        ),
+        grid_spec=pltpu.PrefetchScalarGridSpec(
+            num_scalar_prefetch=1,
+            grid=(1,),
+            in_specs=[pl.BlockSpec(a.shape, lambda i, p: (0, 0)) for a in args],
+            out_specs=(
+                pl.BlockSpec((rows // 2, D), lambda i, p: (0, 0)),
+                pl.BlockSpec((rows // 2 + extra, D), lambda i, p: (0, 0)),
+            ),
+            scratch_shapes=[pltpu.VMEM((rows, D), f32)],
+        ),
+        compiler_params=pltpu.CompilerParams(vmem_limit_bytes=VMEM),
+        cost_estimate=pl.CostEstimate(
+            flops=2 * dT.size * D, bytes_accessed=2 * dT.size + 2 * normed.size + 6 * rows * D, transcendentals=0
+        ),
+        name="weight_rows",
+    )(half.astype(jnp.int32).reshape(1), *args)
+
+
+def finish_kernel(dp, me_ref, *refs):
+    pieces = refs[:8]
+    weights = refs[8:11]
+    outs = refs[11:15]
+    gain_ref = refs[15]
+    got, wide, in_sem, out_sem = refs[16:]
+    z, xi, ci, yi = me_ref[0], me_ref[1], me_ref[2], me_ref[3]
+    rows = pieces[0].shape[0] // dp
+    per = 4 * 2 // dp
+    copies = []
+    for n in range(8):
+        c, x, y = (n // 4) ^ ci, ((n // 2) % 2) ^ xi, (n % 2) ^ yi
+        for r in range(dp):
+            j = y * dp + lax.rem(z + dp - r, dp)
+            p = lax.div(j * 4, 2 * dp)
+            first = (x * 2 + c) * (D // 4) + lax.rem(j, 2 * dp // 4) * rows
+            copy = pltpu.make_async_copy(
+                pieces[n].at[pl.ds(r * rows, rows)],
+                got.at[p, pl.ds(pl.multiple_of(first, rows), rows)],
+                in_sem.at[n, r],
+            )
+            copy.start()
+            copies.append(copy)
+    for copy in copies:
+        copy.wait()
+    del per
+    gain = jnp.zeros((D, 1), f32)
+    backs = []
+    for p in range(4):
+        if p < 3:
+            g = got[p].T.astype(f32)
+            gain = gain + jnp.sum(g * weights[p][...].astype(f32), axis=1, keepdims=True)
+        else:
+            g = got[p].astype(f32)
+        wide[p] = g
+        back = pltpu.make_async_copy(wide.at[p], outs[p], out_sem.at[p])
+        back.start()
+        backs.append(back)
+    gain_ref[...] = gain
+    for back in backs:
+        back.wait()
+
+
+def finish(me, pieces, weights, dp):
+    whole = jax.ShapeDtypeStruct((D, D), f32)
+    anywhere = pl.BlockSpec(memory_space=pl.ANY)
+    return pl.pallas_call(
+        functools.partial(finish_kernel, dp),
+        out_shape=(whole,) * 4 + (jax.ShapeDtypeStruct((D, 1), f32),),
+        grid_spec=pltpu.PrefetchScalarGridSpec(
+            num_scalar_prefetch=1,
+            grid=(1,),
+            in_specs=[anywhere] * 8 + [pl.BlockSpec((D, D), lambda i, p: (0, 0))] * 3,
+            out_specs=(anywhere,) * 4 + (pl.BlockSpec((D, 1), lambda i, p: (0, 0)),),
+            scratch_shapes=[
+                pltpu.VMEM((4, D, D), bf16),
+                pltpu.VMEM((4, D, D), f32),
+                pltpu.SemaphoreType.DMA((8, dp)),
+                pltpu.SemaphoreType.DMA((4,)),
+            ],
+        ),
+        compiler_params=pltpu.CompilerParams(vmem_limit_bytes=VMEM),
+        cost_estimate=pl.CostEstimate(flops=8 * D * D, bytes_accessed=32 * D * D, transcendentals=0),
+        name="finish",
+    )(me, *pieces, *weights)
+
+
 def swap(v, axis):
     return lax.ppermute(v, axis, [(0, 1), (1, 0)])
 
@@ -392,67 +547,30 @@
     return lax.dynamic_index_in_dim(v, index, 0, keepdims=False)
 
 
-def place(pieces, n):
-    out = jnp.zeros((n,) + pieces[0][1].shape, pieces[0][1].dtype)
-    for index, piece in pieces:
-        out = lax.dynamic_update_index_in_dim(out, piece, index, 0)
+def two(v):
+    high = lax.reduce_precision(v, 8, 7)
+    return jnp.concatenate([high, v - high], axis=0).astype(bf16)
+
+
+def one(v):
+    v = v.astype(f32)
+    n = v.shape[0] // 2
+    return v[:n] + v[n:]
+
+
+def add_pair(v):
+    return v + (swap(v, "expert") if lax.axis_size("expert") == 2 else lax.psum(v, "expert") - v)
+
+
+def add_shifts(v):
+    out = v
+    for s in range(1, lax.axis_size("dp")):
+        out = out + shift(v, "dp", s)
     return out
-
-
-def gather_shifts(v, axis):
-    n = lax.axis_size(axis)
-    me = lax.axis_index(axis)
-    return place([(me, v)] + [((me - s) % n, shift(v, axis, s)) for s in range(1, n)], n)
-
-
-def sum_all(v):
-    return jnp.sum(lax.all_gather(v, ("dp", "x", "core", "expert")), axis=0)
 
 
 def tie(*arrays):
     return lax.optimization_barrier(arrays)
-
-
-def scatter_sum(v):
-    e = lax.axis_size("expert")
-    if e == 2:
-        me = lax.axis_index("expert")
-        halves = v.reshape(2, -1, D)
-        v = at(halves, me) + swap(at(halves, 1 - me).astype(bf16), "expert").astype(f32)
-    else:
-        v = lax.psum_scatter(v.astype(bf16), "expert", scatter_dimension=0, tiled=True).astype(f32)
-    n = lax.axis_size("dp")
-    me = lax.axis_index("dp")
-    parts = v.reshape(n, -1, D)
-    out = at(parts, me)
-    for s in range(1, n):
-        out = out + shift(at(parts, (me + s) % n).astype(bf16), "dp", s).astype(f32)
-    return out
-
-
-def gather_back(v):
-    v = gather_shifts(v, "dp")
-    v = v.reshape((-1,) + v.shape[2:])
-    if lax.axis_size("expert") == 2:
-        v = gather_shifts(v, "expert")
-    else:
-        v = lax.all_gather(v, "expert")
-    v = v.reshape((-1,) + v.shape[2:])
-    v = gather_shifts(v, "x")
-    v = gather_shifts(v, "core")
-    return jnp.swapaxes(v, 0, 1)
-
-
-def ring_steps(parts):
-    n = lax.axis_size("dp")
-    me = lax.axis_index("dp")
-    moving = at(parts, (me - 1) % n)
-    for s in range(n - 1):
-        moving = shift(moving, "dp", 1)
-        moving = moving.astype(f32) + at(parts, (me - 2 - s) % n).astype(f32)
-        if s < n - 2:
-            moving = moving.astype(bf16)
-        moving = yield moving
 
 
 def normal_form(v):
@@ -491,11 +609,10 @@
     heads = mine // HD
     pick = jnp.stack([xi, ci]).astype(jnp.int32)
 
-    flat = tokens.reshape(rows, D).astype(f32)
-    xh1, rstd1 = normal_form(flat)
-    normed = (xh1 * norm1_gain).astype(bf16)
-    other = swap(normed, "x")
-    near = swap(normed, "core")
+    tok = tokens.reshape(rows, D)
+    other = swap(tok, "x")
+    near = swap(tok, "core")
+
     route = routes.reshape(rows)
     hot = (route[:, None] == jnp.arange(experts, dtype=jnp.int32)[None, :]).astype(f32)
     lower = jnp.arange(rows)[:, None] >= jnp.arange(rows)[None, :]
@@ -514,31 +631,37 @@
     def turn(v):
         return lax.all_to_all(v, ("x", "core"), split_axis=0, concat_axis=0, tiled=True)
 
+    def cut(w):
+        return lax.dynamic_slice(w, (0, ctx_i * mine), (D, mine))
+
+    w_own = jnp.concatenate([cut(w_query), cut(w_key), cut(w_value)], axis=1)
+    gain1 = norm1_gain.reshape(1, D)
     dy_low = cotangent.reshape(rows, D)
     dy = dy_low.astype(f32)
-    other, dy_packed = tie(other, pack(dy_low))
+    counts = jnp.sum(hot, axis=0)
+    counts = counts + swap(counts, "core")
+    counts = counts + swap(counts, "x")
+    so_far = project(ctx_i, tok, gain1, w_own, ctx, None)
+    so_far = project(ctx_i ^ 1, near, gain1, w_own, ctx, so_far)
+    other, dy_packed, counts, *so_far = tie(other, pack(dy_low), counts, *so_far)
+    far = swap(other, "core")
     dy_rows = trade(dy_packed)
-    far = swap(other, "core")
-    normed_all = place(
-        [(ctx_i, normed), (ctx_i ^ 1, near), (ctx_i ^ 2, other), (ctx_i ^ 3, far)], ctx
-    ).reshape(length, D)
-    counts = sum_all(jnp.zeros((8, 128), f32).at[0, :experts].set(jnp.sum(hot, axis=0)))[0, :experts]
+    counts = add_pair(counts)
+    so_far = project(ctx_i ^ 2, other, gain1, w_own, ctx, so_far)
+    so_far = project(ctx_i ^ 3, far, gain1, w_own, ctx, so_far)
+    counts, normed_all, qkvT, kv = tie(counts, *so_far)
+    counts = add_shifts(counts)
+    oT, osend, lse = attend(qkvT, kv, ctx)
+    osend, dy_rows, counts = tie(osend, dy_rows, counts)
+    attT = turn(osend).reshape(D, rows)
+
     mean_load = rows * ctx * dp * owners / experts
     load_term = balance_weight * (counts - mean_load) / (mean_load * mean_load)
     expert_id = ei * nx + xi
     load = jnp.broadcast_to(lax.dynamic_slice(load_term, (expert_id,), (1,)).reshape(1, 1), (1, 128))
     wr = lax.dynamic_slice(w_router, (0, expert_id), (D, 1)).astype(f32).reshape(1, D)
 
-    def cut(w):
-        return lax.dynamic_slice(w, (0, ctx_i * mine), (D, mine))
-
-    wq, wk, wv = cut(w_query), cut(w_key), cut(w_value)
-    qkvT = dg(jnp.concatenate([wq, wk, wv], axis=1), normed_all, 0, 1).astype(bf16)
-    kv = dg(normed_all, jnp.concatenate([wk, wv], axis=1), 1, 0).astype(bf16)
-    oT, osend, lse = attend(qkvT, kv, ctx)
-    osend, dy_rows = tie(osend, dy_rows)
-    attT = turn(osend).reshape(D, rows)
-
+    flat = tok.astype(f32)
     middle = flat + dg(attT, w_output, 0, 0)
     xh2, rstd2 = normal_form(middle)
     second = (xh2 * norm2_gain).astype(bf16)
@@ -550,62 +673,100 @@
     returned = trade(back_rows)
     keep, send, produced = expert_grads(pick, x_rows, dy_rows, gate, active, grad_hidden, w_out, dp, nx)
     returned, keep, send, produced = tie(returned, keep, send, produced)
-    pair = (keep.astype(f32) + swap(send, "core").astype(f32)).astype(bf16)
+    taken = swap(send, "core")
+    zi = lax.axis_index("dp")
+
+    def chunk(i):
+        return at(keep, (i + dp) % dp).astype(f32) + at(taken, (i + dp) % dp).astype(f32)
+
+    def ring(moving, step):
+        moving = shift(moving, "dp", 1).astype(f32) + chunk(zi - 2 - step)
+        return moving if step == dp - 2 else moving.astype(bf16)
 
     grad_second = dg(spread, returned, 0, 0)
     grad_middle = dy + norm_back(grad_second * norm2_gain, xh2, rstd2)
     branch = grad_middle.astype(bf16)
     attT_grad = dg(w_output, branch, 1, 1).astype(bf16).reshape(ctx, heads, HD, rows)
     do_first, do_later = turn(attT_grad[:, :1]), turn(attT_grad[:, 1:])
-    go = dg(attT, branch, 1, 0)
-    go = go.reshape(nx, 2, mine, D)
+
+    go = dg(attT, branch, 1, 0).reshape(nx, 2, mine, D)
+    router_rows = (jnp.arange(experts) == expert_id).astype(f32)[:, None] * router_row
+    sig = jnp.pad(jnp.sum(hot * gating[:, None], axis=0), (0, D - experts))
+    small = jnp.concatenate([router_rows, jnp.sum(grad_second * xh2, axis=0)[None], sig[None]], axis=0)
+    small = jnp.pad(small, ((0, -small.shape[0] % 8), (0, 0)))
+    go_send = lax.dynamic_index_in_dim(go, 1 - ci, 1, keepdims=False).astype(bf16).reshape(-1, D)
+    go_send = jnp.concatenate([go_send, two(small)], axis=0)
     go_keep = lax.dynamic_index_in_dim(go, ci, 1, keepdims=False)
-    go_send = lax.dynamic_index_in_dim(go, 1 - ci, 1, keepdims=False).astype(bf16)
-    go = go_keep + swap(go_send, "core").astype(f32)
-    go = at(go, xi) + swap(at(go, 1 - xi).astype(bf16), "x").astype(f32)
-
-    do_first, pair = tie(do_first, pair)
-    ring = ring_steps(pair)
-    ringed = next(ring)
+
+    moving = chunk(zi - 1).astype(bf16)
+    do_first, moving, go_send = tie(do_first, moving, go_send)
+    moving = ring(moving, 0)
+    go_got = swap(go_send, "core")
     so_far = attend_back(qkvT, kv, do_first, 0, oT, lse, 0, None)
-    for h in range(1, heads):
-        do_later, ringed, *so_far = tie(do_later, ringed, *so_far)
-        try:
-            ringed = ring.send(ringed)
-        except StopIteration:
-            pass
+    do_later, go_got, produced, *so_far = tie(do_later, go_got, produced, *so_far)
+    go = go_keep + go_got[: nx * mine].astype(f32).reshape(nx, mine, D)
+    small = small + one(go_got[nx * mine :])
+    go_got = swap(jnp.concatenate([at(go, 1 - xi).astype(bf16), two(small)], axis=0), "x")
+    went_back = trade(produced)
+    so_far = attend_back(qkvT, kv, do_later, 0, oT, lse, 1, so_far)
+    go_got, moving, *so_far = tie(go_got, moving, *so_far)
+    go = at(go, xi) + go_got[:mine].astype(f32)
+    small = small + one(go_got[mine:])
+    moving = ring(moving, 1)
+    for h in range(2, heads):
         so_far = attend_back(qkvT, kv, do_later, h - 1, oT, lse, h, so_far)
-    dT, dsend = so_far
-    for more in ring:
-        ringed = more
-    got, produced = tie(turn(dsend), produced)
+    went_back, dT, dsend = tie(went_back, *so_far)
+    output = (middle + gating[:, None] * dg(spread, went_back, 0, 0)).astype(bf16)
+    got = turn(dsend)
+
+    ei2 = ei if owners == 2 else jnp.zeros_like(ei)
+    half, send = weight_rows(ei2, dT.reshape(3 * mine, length), normed_all, go, two(small))
+    cut_at = half.shape[0]
+    if owners == 2:
+        gift = swap(send, "expert")
+        gift, moving = tie(gift, moving)
+        halves = [half + gift[:cut_at].astype(f32)]
+        small = small + one(gift[cut_at:])
+    else:
+        halves = [lax.psum(half, "expert"), lax.psum(send[:cut_at].astype(f32), "expert")]
+        small = lax.psum(small, "expert")
+    pieces = []
+    for part in halves:
+        part = part.reshape(dp, -1, D)
+        share = at(part, zi)
+        more = small
+        for step in range(1, dp):
+            gift = jnp.concatenate([at(part, (zi + step) % dp).astype(bf16), two(small)], axis=0)
+            gift = shift(gift, "dp", step)
+            share = share + gift[: share.shape[0]].astype(f32)
+            more = more + one(gift[share.shape[0] :])
+        share = share.astype(bf16)
+        pieces.append(jnp.concatenate([share] + [shift(share, "dp", step) for step in range(1, dp)], axis=0))
+    small = more
+    for step in range(2, dp - 1):
+        moving = ring(moving, step)
+
+    if owners == 2:
+        pieces.append(swap(pieces[0], "expert"))
+    pieces += [swap(piece, "x") for piece in pieces]
+    pieces += [swap(piece, "core") for piece in pieces]
+    me = jnp.stack([zi, xi, ci, ei2]).astype(jnp.int32)
+    *grads, grad_norm1 = finish(me, pieces, (w_query, w_key, w_value), dp)
+    grad_norm1 = grad_norm1.reshape(D) / norm1_gain
+
     grad_normed = 0.0
     for p, w in enumerate((w_query, w_key, w_value)):
         grad_normed = grad_normed + dg(got[:, p].reshape(D, rows), w, 0, 1)
+    xh1, rstd1 = normal_form(flat)
     grad_tokens = grad_middle + norm_back(grad_normed * norm1_gain, xh1, rstd1)
-    output = (middle + gating[:, None] * dg(spread, trade(produced), 0, 0)).astype(bf16)
-
-    weight_rows = dg(dT.reshape(3 * mine, length), normed_all, 1, 0)
-    shared = gather_back(scatter_sum(jnp.concatenate([weight_rows, go], axis=0)).astype(bf16))
-    grads = [shared[:, :, p * mine : (p + 1) * mine].reshape(D, D).astype(f32) for p in range(4)]
-    grads[:3] = [jnp.transpose(g) for g in grads[:3]]
-    grad_norm1 = 0.0
-    for g, w in zip(grads, (w_query, w_key, w_value)):
-        grad_norm1 = grad_norm1 + jnp.sum(g * w.astype(f32), axis=1)
-    grad_norm1 = grad_norm1 / norm1_gain
-
-    own = lax.dynamic_index_in_dim(ringed, xi, 1, keepdims=False)
-    moved = swap(lax.dynamic_index_in_dim(ringed, 1 - xi, 1, keepdims=False).astype(bf16), "x").astype(f32)
+
+    own = lax.dynamic_index_in_dim(moving, xi, 1, keepdims=False)
+    moved = swap(lax.dynamic_index_in_dim(moving, 1 - xi, 1, keepdims=False).astype(bf16), "x").astype(f32)
     first, latter = jnp.where(xi == 0, own, moved), jnp.where(xi == 0, moved, own)
     both = jnp.stack([first, latter], axis=1)
     grad_in = jnp.swapaxes(both[0], 1, 2)
     grad_out = both[1]
 
-    router_rows = (jnp.arange(experts) == expert_id).astype(f32)[:, None] * router_row
-    sig = jnp.pad(jnp.sum(hot * gating[:, None], axis=0), (0, D - experts))
-    small = sum_all(
-        jnp.concatenate([router_rows, jnp.sum(grad_second * xh2, axis=0)[None], sig[None]], axis=0)
-    )
     grad_router = jnp.transpose(small[:experts])
     grad_norm2 = small[experts]
     total_sig = small[experts + 1, :experts]

time: 589 us -> 414 us (0.70)
  blocking collectives: 151 us -> 15.6 us
  local copies, waits for them, and re-layouts: 82 us -> 24.5 us
  Pallas kernels: 101 us -> 132 us
  other arithmetic: 52.6 us -> 36.3 us
  matrix products: 36.6 us -> 20.4 us
  starting transfers between devices: 49.3 us -> 62.8 us
    all_gather x2 -> x0, blocking collectives: 151 us -> none  [sum_all(): return jnp.sum(lax.all_gather(v, ('dp', 'x', 'core', 'expert')), axis=0)]
    pallas_call x0 -> x6, Pallas kernels: none -> 31.4 us  [the longest x4 15.1 us: project(): pl.pallas_call(project_kernel, out_shape=(jax.ShapeDtypeStruct((ctx * row...]
    dynamic_update_slice x12 -> x0, local copies, waits for them, and re-layouts: 24.3 us -> none  [place(): out = lax.dynamic_update_index_in_dim(out, piece, index, 0)]
    ppermute x8 -> x18, waiting for transfers between devices: 32.3 us -> 56.1 us  [swap(): return lax.ppermute(v, axis, [(0, 1), (1, 0)])]
    unnamed x94 -> x90, local copies, waits for them, and re-layouts: 24.7 us -> 7.47 us
    dot_general x15 -> x12, matrix products: 36.6 us -> 20.4 us  [dg(): lax.dot_general(a, b, (((ca,), (cb,)), ((), ())), preferred_element_type=...]
    all_to_all x0 -> x1, blocking collectives: none -> 15.6 us  [turn(): lax.all_to_all(v, ('x', 'core'), split_axis=0, concat_axis=0, tiled=True)]
    ppermute x12, waiting for transfers between devices: 62.3 us -> 47.7 us  [shift(): return lax.ppermute(v, axis, [(i, (i + step) % n) for i in range(n)])]
  transfers between devices with their start and end apart: 28 -> 37, of which waited for: 12 -> 12; matrix products, arithmetic and copies ran while one was open for 19% -> 17% of each run, Pallas kernels for 12% -> 24%
where the time goes in v3:
time: 414 us; the launch traced here: 406 us
  Pallas kernels  132 us (32%)
  waiting for transfers between devices  111 us (27%)
  starting transfers between devices  62.8 us (15%)
  other arithmetic  36.3 us (9%)
  local copies, waits for them, and re-layouts  24.5 us (6%)
  matrix products  20.4 us (5%)
  blocking collectives  15.6 us (4%)
    ppermute x18, waiting for transfers between devices, swap(): return lax.ppermute(v, axis, [(0, 1), (1, 0)])  56.1 us
    ppermute x12, waiting for transfers between devices, shift(): return lax.ppermute(v, axis, [(i, (i + step) % n) for i in range(n)])  47.7 us
    pallas_call x3, Pallas kernels, attend_back(): pl.pallas_call(functools.partial(attend_back_kernel, h % 2 * HD, hv % 2 *...  28 us
    pallas_call x1, Pallas kernels, expert_mid(): pl.pallas_call(mid_kernel, out_shape=(jax.ShapeDtypeStruct((rows, ff), bf...  24.8 us
    pallas_call x1, Pallas kernels, expert_grads(): pl.pallas_call(grads_kernel, out_shape=(part, part, jax.ShapeDtypeStruct(...  24.1 us
    dot_general x12, matrix products, dg(): lax.dot_general(a, b, (((ca,), (cb,)), ((), ())), preferred_element_type=...  20.4 us
    ppermute x12, starting transfers between devices, shift(): return lax.ppermute(v, axis, [(i, (i + step) % n) for i in range(n)])  19.7 us
    all_to_all x4, starting transfers between devices, trade(): lax.all_to_all(v.reshape(nx * owners, cap, D), ('x', 'expert'), split_axi...  17.6 us
  transfers between devices with their start and end apart: 37, of which 12 were waited for; matrix products, arithmetic and copies ran while one was open for 17% of the time, Pallas kernels for 24%

profile of v3, /device:TPU:0, one launch (start us, length us, event | category | flops | bytes accessed | tf_op | source)
XLA Modules:
  0.0 405.8 jit_solution(10496438136759803287)
XLA Ops:
  10.2 3.8 project.4
  16.8 5.4 %collective-permute-done.2 = f32[4]{0:T(128)S(1)} collective-permute-done((f32[4]{0:T(128)S(1)}, f32[4]{0:T(128)S(1)}, u32[]{:S(2)}, u32[]{:S(2)}) %collective-permute-start.2) | collective-permute-done | bytes 48 | tf_op jit(solution)/shard_map/ppermute | solution.py:538
  23.1 3.8 project.5
  26.9 4.0 all-to-all-start
  32.9 3.8 project.6
  36.6 14.2 %collective-permute-done.4 = f32[4]{0:T(128)S(1)} collective-permute-done((f32[4]{0:T(128)S(1)}, f32[4]{0:T(128)S(1)}, u32[]{:S(2)}, u32[]{:S(2)}) %collective-permute-start.4) | collective-permute-done | bytes 48 | tf_op jit(solution)/shard_map/ppermute | solution.py:538
  51.7 3.8 project.7
  55.4 3.7 collective-permute-start.8
  60.4 13.8 %attend.1 = (f32[192,2048]{1,0:T(8,128)}, bf16[4,3,64,512]{3,2,1,0:T(8,128)(2,1)}, f32[3,1,2048]{2,1,0:T(1,128)}) custom-call(bf16[576,2048]{1,0:T(8,128)(2,1)} %get-tuple-element.99.qT_ref.vT_ref.refs_0_.refs_2_, bf16[2048,384]{1,0:T(8,128)(2,1)} %get-tuple-element.100.k_ref.refs_1_.refs_3_, bf16[576,2048]{1,0:T(8,128)(2,1)} %get-tuple-element.99.qT_ref.vT_ref.refs_0_.refs_2_), custom_call_target="tpu_custom_call" | custom-call | flops 6442450944 | bytes 5505024 | tf_op jit(solution)/shard_map/attend/pallas_call | solution.py:115
  74.7 15.6 %all_to_all.40 = bf16[4,3,64,512]{3,2,1,0:T(8,128)(2,1)S(1)} all-to-all(bf16[4,3,64,512]{3,2,1,0:T(8,128)(2,1)} %get-tuple-element.104), channel_id=1, replica_groups=mesh['dp'=4,'x'=2,'core'=2,'expert'=2] {'x','core'}, dimensions={0} | all-to-all | bytes 1572864 | tf_op jit(solution)/shard_map/all_to_all | solution.py:632
  94.5 4.5 %all-to-all-start.2 = ((bf16[4,256,768]{2,1,0:T(8,128)(2,1)}), bf16[4,256,768]{2,1,0:T(8,128)(2,1)}, u32[]{:S(2)}, u32[]{:S(2)}) async-start(bf16[4,256,768]{2,1,0:T(8,128)(2,1)} %bitcast.141), calls=%async_computation.2 | async-start | bytes 3145728 | tf_op jit(solution)/shard_map/all_to_all | solution.py:628
  101.3 9.9 %expert_up.1.u_ref = bf16[1024,3072]{1,0:T(8,128)(2,1)} custom-call(s32[2]{0:T(128)} %pad_add_fusion.pick_ref, bf16[1024,768]{1,0:T(8,128)(2,1)} %bitcast.138, bf16[2,3072,768]{2,1,0:T(8,128)(2,1)} %wo_ref.3), custom_call_target="tpu_custom_call" | custom-call | flops 4831838208 | bytes 12582912 | tf_op jit(solution)/shard_map/expert_up/pallas_call | solution.py:242
  111.2 7.0 %all-to-all-done.2 = bf16[4,256,768]{2,1,0:T(8,128)(2,1)} async-done(((bf16[4,256,768]{2,1,0:T(8,128)(2,1)}), bf16[4,256,768]{2,1,0:T(8,128)(2,1)}, u32[]{:S(2)}, u32[]{:S(2)}) %all-to-all-start.2) | async-done | bytes 1572896 | tf_op jit(solution)/shard_map/all_to_all | solution.py:628
  119.4 24.8 %expert_mid.1 = (bf16[1024,3072]{1,0:T(8,128)(2,1)}, bf16[1024,3072]{1,0:T(8,128)(2,1)}, bf16[1024,768]{1,0:T(8,128)(2,1)}, f32[1,768]{1,0:T(1,128)}, f32[1024,128]{1,0:T(8,128)}) custom-call(s32[2]{0:T(128)} %pad_add_fusion.pick_ref, bf16[1024,768]{1,0:T(8,128)(2,1)} %bitcast.13.x_ref, bf16[1024,3072]{1,0:T(8,128)(2,1)} %expert_up.1.u_ref, ...), custom_call_target="tpu_custom_call" | custom-call | flops 9663676416 | bytes 28311552 | tf_op jit(solution)/shard_map/expert_mid/pallas_call | solution.py:313
  144.2 4.5 %all-to-all-start.3 = ((bf16[4,256,768]{2,1,0:T(8,128)(2,1)}), bf16[4,256,768]{2,1,0:T(8,128)(2,1)}, u32[]{:S(2)}, u32[]{:S(2)}) async-start(bf16[4,256,768]{2,1,0:T(8,128)(2,1)} %bitcast.142), calls=%async_computation.3 | async-start | bytes 3145728 | tf_op jit(solution)/shard_map/all_to_all | solution.py:628
  148.7 24.1 %expert_grads.1 = (bf16[4,2,2,192,768]{4,3,2,1,0:T(8,128)(2,1)}, bf16[4,2,2,192,768]{4,3,2,1,0:T(8,128)(2,1)}, bf16[1024,768]{1,0:T(8,128)(2,1)}) custom-call(s32[2]{0:T(128)} %pad_add_fusion.pick_ref, bf16[1024,768]{1,0:T(8,128)(2,1)} %bitcast.13.x_ref, bf16[1024,768]{1,0:T(8,128)(2,1)} %bitcast.139, f32[1024,128]{1,0:T(8,128)} %get-tuple-element.108.gate_ref, ...), custom_call_target="tpu_custom_call" | custom-call | flops 14495514624 | bytes 31457280 | tf_op jit(solution)/shard_map/expert_grads/pallas_call | solution.py:398
  209.2 9.3 %attend_back_head0.1 = (bf16[3,192,2048]{2,1,0:T(8,128)(2,1)}, bf16[4,3,192,512]{3,2,1,0:T(8,128)(2,1)}) custom-call(bf16[576,2048]{1,0:T(8,128)(2,1)} %get-tuple-element.99.qT_ref.vT_ref.refs_0_.refs_2_, bf16[2048,384]{1,0:T(8,128)(2,1)} %get-tuple-element.100.k_ref.refs_1_.refs_3_, bf16[576,2048]{1,0:T(8,128)(2,1)} %get-tuple-element.99.qT_ref.vT_ref.refs_0_.refs_2_, ...), custom_call_target="tpu_custom_call" | custom-call | flops 5368709120 | bytes 3145728 | tf_op jit(solution)/shard_map/attend_back_head0/pallas_call | solution.py:213
  221.9 4.6 %all-to-all-start.6 = ((bf16[4,256,768]{2,1,0:T(8,128)(2,1)}), bf16[4,256,768]{2,1,0:T(8,128)(2,1)}, u32[]{:S(2)}, u32[]{:S(2)}) async-start(bf16[4,256,768]{2,1,0:T(8,128)(2,1)} %bitcast.137), calls=%async_computation.6 | async-start | bytes 3145728 | tf_op jit(solution)/shard_map/all_to_all | solution.py:628
  230.2 9.3 %attend_back_head1.1 = (bf16[3,192,2048]{2,1,0:T(8,128)(2,1)}, bf16[4,3,192,512]{3,2,1,0:T(8,128)(2,1)}) custom-call(bf16[576,2048]{1,0:T(8,128)(2,1)} %get-tuple-element.99.qT_ref.vT_ref.refs_0_.refs_2_, bf16[2048,384]{1,0:T(8,128)(2,1)} %get-tuple-element.100.k_ref.refs_1_.refs_3_, ...), custom_call_target="tpu_custom_call", output_to_operand_aliasing={{0}: (7, {}), {1}: (8, {})} | custom-call | flops 5368709120 | bytes 3145728 | tf_op jit(solution)/shard_map/attend_back_head1/pallas_call | solution.py:213
  243.0 9.8 %collective-permute-done.11 = bf16[208,768]{1,0:T(8,128)(2,1)S(1)} collective-permute-done((bf16[208,768]{1,0:T(8,128)(2,1)S(1)}, bf16[208,768]{1,0:T(8,128)(2,1)S(1)}, u32[]{:S(2)}, u32[]{:S(2)}) %collective-permute-start.11) | collective-permute-done | bytes 319520 | tf_op jit(solution)/shard_map/ppermute | solution.py:538
  255.1 9.3 %attend_back_head2.1 = (bf16[3,192,2048]{2,1,0:T(8,128)(2,1)}, bf16[4,3,192,512]{3,2,1,0:T(8,128)(2,1)}) custom-call(bf16[576,2048]{1,0:T(8,128)(2,1)} %get-tuple-element.99.qT_ref.vT_ref.refs_0_.refs_2_, bf16[2048,384]{1,0:T(8,128)(2,1)} %get-tuple-element.100.k_ref.refs_1_.refs_3_, ...), custom_call_target="tpu_custom_call", output_to_operand_aliasing={{0}: (7, {}), {1}: (8, {})} | custom-call | flops 5368709120 | bytes 3145728 | tf_op jit(solution)/shard_map/attend_back_head2/pallas_call | solution.py:213
  264.4 6.0 %weight_rows.1 = (f32[384,768]{1,0:T(8,128)}, bf16[400,768]{1,0:T(8,128)(2,1)}) custom-call(s32[1]{0:T(128)} %bitcast.37.half_ref, bf16[576,2048]{1,0:T(8,128)(2,1)} %bitcast.150, bf16[2048,768]{1,0:T(8,128)(2,1)} %get-tuple-element.140.normed_ref, f32[192,768]{1,0:T(8,128)} %bitcast_add_fusion.3.go_ref, bf16[16,768]{1,0:T(8,128)(2,1)} %pad_maximum_fusion.11.small_ref), custom_call_target="tpu_custom_call" | custom-call | flops 1811939328 | bytes 9043968 | tf_op jit(solution)/shard_map/weight_rows/pallas_call | solution.py:446
  272.9 4.5 %all-to-all-start.7 = ((bf16[4,3,192,512]{3,2,1,0:T(8,128)(2,1)}), bf16[4,3,192,512]{3,2,1,0:T(8,128)(2,1)}, u32[]{:S(2)}, u32[]{:S(2)}) async-start(bf16[4,3,192,512]{3,2,1,0:T(8,128)(2,1)} %get-tuple-element.138), calls=%async_computation.7 | async-start | bytes 4718592 | tf_op jit(solution)/shard_map/all_to_all | solution.py:632
  277.4 4.8 %collective-permute-done.14 = bf16[2,2,192,768]{3,2,1,0:T(8,128)(2,1)} collective-permute-done((bf16[2,2,192,768]{3,2,1,0:T(8,128)(2,1)}, bf16[2,2,192,768]{3,2,1,0:T(8,128)(2,1)}, u32[]{:S(2)}, u32[]{:S(2)}) %collective-permute-start.14) | collective-permute-done | bytes 1179680 | tf_op jit(solution)/shard_map/ppermute | solution.py:543
  292.3 3.5 fusion.19
  297.4 30.3 %collective-permute-done.16 = bf16[112,768]{1,0:T(8,128)(2,1)S(1)} collective-permute-done((bf16[112,768]{1,0:T(8,128)(2,1)S(1)}, bf16[112,768]{1,0:T(8,128)(2,1)S(1)}, u32[]{:S(2)}, u32[]{:S(2)}) %collective-permute-start.16) | collective-permute-done | bytes 172064 | tf_op jit(solution)/shard_map/ppermute | solution.py:543
  327.8 5.2 %collective-permute-start.19 = (bf16[96,768]{1,0:T(8,128)(2,1)S(1)}, bf16[96,768]{1,0:T(8,128)(2,1)S(1)}, u32[]{:S(2)}, u32[]{:S(2)}) collective-permute-start(bf16[96,768]{1,0:T(8,128)(2,1)S(1)} %fusion.41), channel_id=1, source_target_pairs={{0,16},{8,24},{16,0},{24,8},{1,17},{9,25},{17,1},{25,9},{2,18},{10... | collective-permute-start | bytes 442376 | tf_op jit(solution)/shard_map/ppermute | solution.py:543
  335.1 10.7 %collective-permute-done.19 = bf16[96,768]{1,0:T(8,128)(2,1)S(1)} collective-permute-done((bf16[96,768]{1,0:T(8,128)(2,1)S(1)}, bf16[96,768]{1,0:T(8,128)(2,1)S(1)}, u32[]{:S(2)}, u32[]{:S(2)}) %collective-permute-start.19) | collective-permute-done | bytes 147488 | tf_op jit(solution)/shard_map/ppermute | solution.py:543
  350.8 10.3 %collective-permute-done.21.refs_1_ = bf16[384,768]{1,0:T(8,128)(2,1)} collective-permute-done((bf16[384,768]{1,0:T(8,128)(2,1)}, bf16[384,768]{1,0:T(8,128)(2,1)}, u32[]{:S(2)}, u32[]{:S(2)}) %collective-permute-start.21) | collective-permute-done | bytes 589856 | tf_op jit(solution)/shard_map/ppermute | solution.py:538
  371.8 5.8 %collective-permute-done.23.refs_3_ = bf16[384,768]{1,0:T(8,128)(2,1)} collective-permute-done((bf16[384,768]{1,0:T(8,128)(2,1)}, bf16[384,768]{1,0:T(8,128)(2,1)}, u32[]{:S(2)}, u32[]{:S(2)}) %collective-permute-start.23) | collective-permute-done | bytes 589856 | tf_op jit(solution)/shard_map/ppermute | solution.py:538
  379.2 10.5 %collective-permute-done.29 = bf16[2,192,768]{2,1,0:T(8,128)(2,1)S(1)} collective-permute-done((bf16[2,192,768]{2,1,0:T(8,128)(2,1)S(1)}, bf16[2,192,768]{2,1,0:T(8,128)(2,1)S(1)}, u32[]{:S(2)}, u32[]{:S(2)}) %collective-permute-start.29) | collective-permute-done | bytes 589856 | tf_op jit(solution)/shard_map/ppermute | solution.py:538
  392.4 10.3 %finish.1 = (f32[768,768]{1,0:T(8,128)}, f32[768,768]{1,0:T(8,128)}, f32[768,768]{1,0:T(8,128)}, f32[768,768]{1,0:T(8,128)}, f32[768,1]{1,0:T(8,128)}) custom-call(s32[4]{0:T(128)} %pad_add_fusion.1.me_ref, bf16[384,768]{1,0:T(8,128)(2,1)} %pad_maximum_fusion.3.refs_0_, bf16[384,768]{1,0:T(8,128)(2,1)} %collective-permute-done.21.refs_1_, ...), custom_call_target="tpu_custom_call" | custom-call | flops 4718592 | bytes 18874368 | tf_op jit(solution)/shard_map/finish/pallas_call | solution.py:516
  (239 shorter events, 111.7 us)
Async XLA Ops:
  0.7 21.5 %collective-permute-start.3 = (bf16[512,768]{1,0:T(8,128)(2,1)}, bf16[512,768]{1,0:T(8,128)(2,1)S(1)}, u32[]{:S(2)}, u32[]{:S(2)}) collective-permute-start(bf16[512,768]{1,0:T(8,128)(2,1)} %bitcast.125), channel_id=1, source_target_pairs={{0,2},{2,0},{1,3},{3,1},{4,6},{6,4},{5,7},{7,5},{8,10},{10,8},{9,1... | collective-permute-start | bytes 2359304 | tf_op jit(solution)/shard_map/ppermute | solution.py:538
  1.2 25.7 %collective-permute-start = (bf16[512,768]{1,0:T(8,128)(2,1)}, bf16[512,768]{1,0:T(8,128)(2,1)}, u32[]{:S(2)}, u32[]{:S(2)}) collective-permute-start(bf16[512,768]{1,0:T(8,128)(2,1)} %bitcast.126), channel_id=1, source_target_pairs={{0,4},{4,0},{1,5},{5,1},{2,6},{6,2},{3,7},{7,3},{8,12},{12,8},{9,1... | collective-permute-start | bytes 2359304 | tf_op jit(solution)/shard_map/ppermute | solution.py:538
  26.8 23.9 %collective-permute-start.5 = (bf16[512,768]{1,0:T(8,128)(2,1)}, bf16[512,768]{1,0:T(8,128)(2,1)S(1)}, u32[]{:S(2)}, u32[]{:S(2)}) collective-permute-start(bf16[512,768]{1,0:T(8,128)(2,1)} %collective-permute-done.tok_ref), channel_id=1, source_target_pairs={{0,2},{2,0},{1,3},{3,1},{4,6},{6,4},{5,7},{7,5},{8,10},{10,8},{9,1... | collective-permute-start | bytes 2359304 | tf_op jit(solution)/shard_map/ppermute | solution.py:538
  26.9 47.9 %all-to-all-start = ((bf16[4,256,768]{2,1,0:T(8,128)(2,1)}), bf16[4,256,768]{2,1,0:T(8,128)(2,1)S(1)}, u32[]{:S(2)}, u32[]{:S(2)}) async-start(bf16[4,256,768]{2,1,0:T(8,128)(2,1)} %bitcast.140), calls=%async_computation | async-start | bytes 3145728 | tf_op jit(solution)/shard_map/all_to_all | solution.py:628
  30.8 19.9 %collective-permute-start.4 = (f32[4]{0:T(128)S(1)}, f32[4]{0:T(128)S(1)}, u32[]{:S(2)}, u32[]{:S(2)}) collective-permute-start(f32[4]{0:T(128)S(1)} %add.297), channel_id=1, source_target_pairs={{0,1},{1,0},{2,3},{3,2},{4,5},{5,4},{6,7},{7,6},{8,9},{9,8},{10,11... | collective-permute-start | bytes 56 | tf_op jit(solution)/shard_map/ppermute | solution.py:538
  55.4 18.8 %collective-permute-start.8 = (f32[4]{0:T(128)S(1)}, f32[4]{0:T(128)S(1)}, u32[]{:S(2)}, u32[]{:S(2)}) collective-permute-start(f32[4]{0:T(128)S(1)} %add.300), channel_id=1, source_target_pairs={{0,24},{8,0},{16,8},{24,16},{1,25},{9,1},{17,9},{25,17},{2,26},{10... | collective-permute-start | bytes 56 | tf_op jit(solution)/shard_map/ppermute | solution.py:543
  59.1 15.1 %collective-permute-start.7 = (f32[4]{0:T(128)S(1)}, f32[4]{0:T(128)S(1)}, u32[]{:S(2)}, u32[]{:S(2)}) collective-permute-start(f32[4]{0:T(128)S(1)} %add.300), channel_id=1, source_target_pairs={{0,16},{8,24},{16,0},{24,8},{1,17},{9,25},{17,1},{25,9},{2,18},{10... | collective-permute-start | bytes 56 | tf_op jit(solution)/shard_map/ppermute | solution.py:543
  59.1 15.1 %collective-permute-start.6 = (f32[4]{0:T(128)S(1)}, f32[4]{0:T(128)S(1)}, u32[]{:S(2)}, u32[]{:S(2)}) collective-permute-start(f32[4]{0:T(128)S(1)} %add.300), channel_id=1, source_target_pairs={{0,8},{8,16},{16,24},{24,0},{1,9},{9,17},{17,25},{25,1},{2,10},{10... | collective-permute-start | bytes 56 | tf_op jit(solution)/shard_map/ppermute | solution.py:543
  94.5 23.7 %all-to-all-start.2 = ((bf16[4,256,768]{2,1,0:T(8,128)(2,1)}), bf16[4,256,768]{2,1,0:T(8,128)(2,1)}, u32[]{:S(2)}, u32[]{:S(2)}) async-start(bf16[4,256,768]{2,1,0:T(8,128)(2,1)} %bitcast.141), calls=%async_computation.2 | async-start | bytes 3145728 | tf_op jit(solution)/shard_map/all_to_all | solution.py:628
  144.2 28.6 %all-to-all-start.3 = ((bf16[4,256,768]{2,1,0:T(8,128)(2,1)}), bf16[4,256,768]{2,1,0:T(8,128)(2,1)}, u32[]{:S(2)}, u32[]{:S(2)}) async-start(bf16[4,256,768]{2,1,0:T(8,128)(2,1)} %bitcast.142), calls=%async_computation.3 | async-start | bytes 3145728 | tf_op jit(solution)/shard_map/all_to_all | solution.py:628
  172.8 24.9 %collective-permute-start.9 = (bf16[4,2,2,192,768]{4,3,2,1,0:T(8,128)(2,1)}, bf16[4,2,2,192,768]{4,3,2,1,0:T(8,128)(2,1)}, u32[]{:S(2)}, u32[]{:S(2)}) collective-permute-start(bf16[4,2,2,192,768]{4,3,2,1,0:T(8,128)(2,1)} %get-tuple-element.116), channel_id=1, source_target_pairs={{0,2},{2,0},{1,3},{3,1},{4,6},{6,4},{5,7},{7,5},{8,10},{10,8},{9,1... | collective-permute-start | bytes 14155784 | tf_op jit(solution)/shard_map/ppermute | solution.py:538
  200.7 17.8 %collective-permute-start.10 = (bf16[400,768]{1,0:T(8,128)(2,1)}, bf16[400,768]{1,0:T(8,128)(2,1)}, u32[]{:S(2)}, u32[]{:S(2)}) collective-permute-start(bf16[400,768]{1,0:T(8,128)(2,1)} %pad_maximum_fusion.2), channel_id=1, source_target_pairs={{0,2},{2,0},{1,3},{3,1},{4,6},{6,4},{5,7},{7,5},{8,10},{10,8},{9,1... | collective-permute-start | bytes 1843208 | tf_op jit(solution)/shard_map/ppermute | solution.py:538
  203.0 15.6 %all-to-all-start.4 = ((bf16[4,2,64,512]{3,2,1,0:T(8,128)(2,1)}), bf16[4,2,64,512]{3,2,1,0:T(8,128)(2,1)S(1)}, u32[]{:S(2)}, u32[]{:S(2)}) async-start(bf16[4,2,64,512]{3,2,1,0:T(8,128)(2,1)} %slice.136), calls=%async_computation.4 | async-start | bytes 1048576 | tf_op jit(solution)/shard_map/all_to_all | solution.py:632
  206.5 33.1 %collective-permute-start.12 = (bf16[2,2,192,768]{3,2,1,0:T(8,128)(2,1)}, bf16[2,2,192,768]{3,2,1,0:T(8,128)(2,1)}, u32[]{:S(2)}, u32[]{:S(2)}) collective-permute-start(bf16[2,2,192,768]{3,2,1,0:T(8,128)(2,1)} %fusion.22), channel_id=1, source_target_pairs={{0,8},{8,16},{16,24},{24,0},{1,9},{9,17},{17,25},{25,1},{2,10},{10... | collective-permute-start | bytes 3538952 | tf_op jit(solution)/shard_map/ppermute | solution.py:543
  221.9 42.5 %all-to-all-start.6 = ((bf16[4,256,768]{2,1,0:T(8,128)(2,1)}), bf16[4,256,768]{2,1,0:T(8,128)(2,1)}, u32[]{:S(2)}, u32[]{:S(2)}) async-start(bf16[4,256,768]{2,1,0:T(8,128)(2,1)} %bitcast.137), calls=%async_computation.6 | async-start | bytes 3145728 | tf_op jit(solution)/shard_map/all_to_all | solution.py:628
  228.2 24.6 %collective-permute-start.11 = (bf16[208,768]{1,0:T(8,128)(2,1)S(1)}, bf16[208,768]{1,0:T(8,128)(2,1)S(1)}, u32[]{:S(2)}, u32[]{:S(2)}) collective-permute-start(bf16[208,768]{1,0:T(8,128)(2,1)S(1)} %pad_maximum_fusion.4), channel_id=1, source_target_pairs={{0,4},{4,0},{1,5},{5,1},{2,6},{6,2},{3,7},{7,3},{8,12},{12,8},{9,1... | collective-permute-start | bytes 958472 | tf_op jit(solution)/shard_map/ppermute | solution.py:538
  252.8 29.4 %collective-permute-start.14 = (bf16[2,2,192,768]{3,2,1,0:T(8,128)(2,1)}, bf16[2,2,192,768]{3,2,1,0:T(8,128)(2,1)}, u32[]{:S(2)}, u32[]{:S(2)}) collective-permute-start(bf16[2,2,192,768]{3,2,1,0:T(8,128)(2,1)} %fusion.1), channel_id=1, source_target_pairs={{0,8},{8,16},{16,24},{24,0},{1,9},{9,17},{17,25},{25,1},{2,10},{10... | collective-permute-start | bytes 3538952 | tf_op jit(solution)/shard_map/ppermute | solution.py:543
  270.4 15.5 %collective-permute-start.13 = (bf16[400,768]{1,0:T(8,128)(2,1)}, bf16[400,768]{1,0:T(8,128)(2,1)S(1)}, u32[]{:S(2)}, u32[]{:S(2)}) collective-permute-start(bf16[400,768]{1,0:T(8,128)(2,1)} %get-tuple-element.143), channel_id=1, source_target_pairs={{0,1},{1,0},{2,3},{3,2},{4,5},{5,4},{6,7},{7,6},{8,9},{9,8},{10,11... | collective-permute-start | bytes 1843208 | tf_op jit(solution)/shard_map/ppermute | solution.py:538
  272.9 90.2 %all-to-all-start.7 = ((bf16[4,3,192,512]{3,2,1,0:T(8,128)(2,1)}), bf16[4,3,192,512]{3,2,1,0:T(8,128)(2,1)}, u32[]{:S(2)}, u32[]{:S(2)}) async-start(bf16[4,3,192,512]{3,2,1,0:T(8,128)(2,1)} %get-tuple-element.138), calls=%async_computation.7 | async-start | bytes 4718592 | tf_op jit(solution)/shard_map/all_to_all | solution.py:632
  288.9 38.7 %collective-permute-start.16 = (bf16[112,768]{1,0:T(8,128)(2,1)S(1)}, bf16[112,768]{1,0:T(8,128)(2,1)S(1)}, u32[]{:S(2)}, u32[]{:S(2)}) collective-permute-start(bf16[112,768]{1,0:T(8,128)(2,1)S(1)} %get-tuple-element.174), channel_id=1, source_target_pairs={{0,16},{8,24},{16,0},{24,8},{1,17},{9,25},{17,1},{25,9},{2,18},{10... | collective-permute-start | bytes 516104 | tf_op jit(solution)/shard_map/ppermute | solution.py:543
  291.9 35.8 %collective-permute-start.17 = (bf16[112,768]{1,0:T(8,128)(2,1)S(1)}, bf16[112,768]{1,0:T(8,128)(2,1)S(1)}, u32[]{:S(2)}, u32[]{:S(2)}) collective-permute-start(bf16[112,768]{1,0:T(8,128)(2,1)S(1)} %get-tuple-element.175), channel_id=1, source_target_pairs={{0,24},{8,0},{16,8},{24,16},{1,25},{9,1},{17,9},{25,17},{2,26},{10... | collective-permute-start | bytes 516104 | tf_op jit(solution)/shard_map/ppermute | solution.py:543
  295.9 73.0 %collective-permute-start.28 = (bf16[2,2,192,768]{3,2,1,0:T(8,128)(2,1)}, bf16[2,2,192,768]{3,2,1,0:T(8,128)(2,1)}, u32[]{:S(2)}, u32[]{:S(2)}) collective-permute-start(bf16[2,2,192,768]{3,2,1,0:T(8,128)(2,1)} %fusion), channel_id=1, source_target_pairs={{0,8},{8,16},{16,24},{24,0},{1,9},{9,17},{17,25},{25,1},{2,10},{10... | collective-permute-start | bytes 3538952 | tf_op jit(solution)/shard_map/ppermute | solution.py:543
  327.8 17.9 %collective-permute-start.19 = (bf16[96,768]{1,0:T(8,128)(2,1)S(1)}, bf16[96,768]{1,0:T(8,128)(2,1)S(1)}, u32[]{:S(2)}, u32[]{:S(2)}) collective-permute-start(bf16[96,768]{1,0:T(8,128)(2,1)S(1)} %fusion.41), channel_id=1, source_target_pairs={{0,16},{8,24},{16,0},{24,8},{1,17},{9,25},{17,1},{25,9},{2,18},{10... | collective-permute-start | bytes 442376 | tf_op jit(solution)/shard_map/ppermute | solution.py:543
  333.0 12.8 %collective-permute-start.18 = (bf16[96,768]{1,0:T(8,128)(2,1)S(1)}, bf16[96,768]{1,0:T(8,128)(2,1)S(1)}, u32[]{:S(2)}, u32[]{:S(2)}) collective-permute-start(bf16[96,768]{1,0:T(8,128)(2,1)S(1)} %fusion.41), channel_id=1, source_target_pairs={{0,8},{8,16},{16,24},{24,0},{1,9},{9,17},{17,25},{25,1},{2,10},{10... | collective-permute-start | bytes 442376 | tf_op jit(solution)/shard_map/ppermute | solution.py:543
  346.7 16.2 %collective-permute-start.22 = (bf16[384,768]{1,0:T(8,128)(2,1)}, bf16[384,768]{1,0:T(8,128)(2,1)}, u32[]{:S(2)}, u32[]{:S(2)}) collective-permute-start(bf16[384,768]{1,0:T(8,128)(2,1)} %pad_maximum_fusion.3.refs_0_), channel_id=1, source_target_pairs={{0,4},{4,0},{1,5},{5,1},{2,6},{6,2},{3,7},{7,3},{8,12},{12,8},{9,1... | collective-permute-start | bytes 1769480 | tf_op jit(solution)/shard_map/ppermute | solution.py:538
  346.8 14.3 %collective-permute-start.21 = (bf16[384,768]{1,0:T(8,128)(2,1)}, bf16[384,768]{1,0:T(8,128)(2,1)}, u32[]{:S(2)}, u32[]{:S(2)}) collective-permute-start(bf16[384,768]{1,0:T(8,128)(2,1)} %pad_maximum_fusion.3.refs_0_), channel_id=1, source_target_pairs={{0,1},{1,0},{2,3},{3,2},{4,5},{5,4},{6,7},{7,6},{8,9},{9,8},{10,11... | collective-permute-start | bytes 1769480 | tf_op jit(solution)/shard_map/ppermute | solution.py:538
  350.8 40.7 %collective-permute-start.24 = (bf16[384,768]{1,0:T(8,128)(2,1)}, bf16[384,768]{1,0:T(8,128)(2,1)}, u32[]{:S(2)}, u32[]{:S(2)}) collective-permute-start(bf16[384,768]{1,0:T(8,128)(2,1)} %pad_maximum_fusion.3.refs_0_), channel_id=1, source_target_pairs={{0,2},{2,0},{1,3},{3,1},{4,6},{6,4},{5,7},{7,5},{8,10},{10,8},{9,1... | collective-permute-start | bytes 1769480 | tf_op jit(solution)/shard_map/ppermute | solution.py:538
  361.1 30.4 %collective-permute-start.25 = (bf16[384,768]{1,0:T(8,128)(2,1)}, bf16[384,768]{1,0:T(8,128)(2,1)}, u32[]{:S(2)}, u32[]{:S(2)}) collective-permute-start(bf16[384,768]{1,0:T(8,128)(2,1)} %collective-permute-done.21.refs_1_), channel_id=1, source_target_pairs={{0,2},{2,0},{1,3},{3,1},{4,6},{6,4},{5,7},{7,5},{8,10},{10,8},{9,1... | collective-permute-start | bytes 1769480 | tf_op jit(solution)/shard_map/ppermute | solution.py:538
  361.1 16.4 %collective-permute-start.23 = (bf16[384,768]{1,0:T(8,128)(2,1)}, bf16[384,768]{1,0:T(8,128)(2,1)}, u32[]{:S(2)}, u32[]{:S(2)}) collective-permute-start(bf16[384,768]{1,0:T(8,128)(2,1)} %collective-permute-done.21.refs_1_), channel_id=1, source_target_pairs={{0,4},{4,0},{1,5},{5,1},{2,6},{6,2},{3,7},{7,3},{8,12},{12,8},{9,1... | collective-permute-start | bytes 1769480 | tf_op jit(solution)/shard_map/ppermute | solution.py:538
  362.9 28.6 %collective-permute-start.26 = (bf16[384,768]{1,0:T(8,128)(2,1)}, bf16[384,768]{1,0:T(8,128)(2,1)}, u32[]{:S(2)}, u32[]{:S(2)}) collective-permute-start(bf16[384,768]{1,0:T(8,128)(2,1)} %collective-permute-done.22.refs_2_), channel_id=1, source_target_pairs={{0,2},{2,0},{1,3},{3,1},{4,6},{6,4},{5,7},{7,5},{8,10},{10,8},{9,1... | collective-permute-start | bytes 1769480 | tf_op jit(solution)/shard_map/ppermute | solution.py:538
  371.4 18.3 %collective-permute-start.29 = (bf16[2,192,768]{2,1,0:T(8,128)(2,1)S(1)}, bf16[2,192,768]{2,1,0:T(8,128)(2,1)S(1)}, u32[]{:S(2)}, u32[]{:S(2)}) collective-permute-start(bf16[2,192,768]{2,1,0:T(8,128)(2,1)S(1)} %fusion.35), channel_id=1, source_target_pairs={{0,4},{4,0},{1,5},{5,1},{2,6},{6,2},{3,7},{7,3},{8,12},{12,8},{9,1... | collective-permute-start | bytes 1769480 | tf_op jit(solution)/shard_map/ppermute | solution.py:538
  377.6 13.9 %collective-permute-start.27 = (bf16[384,768]{1,0:T(8,128)(2,1)}, bf16[384,768]{1,0:T(8,128)(2,1)S(1)}, u32[]{:S(2)}, u32[]{:S(2)}) collective-permute-start(bf16[384,768]{1,0:T(8,128)(2,1)} %collective-permute-done.23.refs_3_), channel_id=1, source_target_pairs={{0,2},{2,0},{1,3},{3,1},{4,6},{6,4},{5,7},{7,5},{8,10},{10,8},{9,1... | collective-permute-start | bytes 1769480 | tf_op jit(solution)/shard_map/ppermute | solution.py:538
  (50 other events, 375.6 us)

commit v4 on v3

--- a/solution.py
+++ b/solution.py
@@ -427,44 +427,178 @@
     )(pick, x, dy, gate, act, gh, w_out)
 
 
-def weight_rows_kernel(half_ref, dT_ref, normed_ref, go_ref, small_ref, keep_ref, send_ref, acc):
+def one_hot_slots(slot, slots):
+    return (lax.broadcasted_iota(jnp.int32, (slots, slot.shape[1]), 0) == slot).astype(f32).astype(bf16)
+
+
+def halves_of(v):
+    high = v.astype(bf16)
+    return jnp.concatenate([high, (v - high.astype(f32)).astype(bf16)], axis=0)
+
+
+def sum_halves(v):
+    v = v.astype(f32)
+    n = v.shape[0] // 2
+    return v[:n] + v[n:]
+
+
+def branch_kernel(
+    norm_row,
+    me_ref,
+    back_ref,
+    slot_ref,
+    dy_ref,
+    middle_ref,
+    gain_ref,
+    w_ref,
+    att_ref,
+    early_ref,
+    grad_ref,
+    heads_ref,
+    keep_ref,
+    send_ref,
+    small_ref,
+    acc,
+):
+    g = dg(one_hot_slots(slot_ref[...], back_ref.shape[0]), back_ref[...], 0, 0)
+    v = middle_ref[...]
+    centred = v - jnp.mean(v, axis=1, keepdims=True)
+    rstd = lax.rsqrt(jnp.mean(centred * centred, axis=1, keepdims=True) + norm_eps)
+    xh = centred * rstd
+    dn = g * gain_ref[...]
+    grad = rstd * (dn - jnp.mean(dn, axis=1, keepdims=True) - xh * jnp.mean(dn * xh, axis=1, keepdims=True))
+    grad = dy_ref[...].astype(f32) + grad
+    grad_ref[...] = grad
+    low = grad.astype(bf16)
+    heads_ref[...] = dg(w_ref[...], low, 1, 1).astype(bf16).reshape(heads_ref.shape)
+    row = lax.broadcasted_iota(jnp.int32, small_ref.shape, 0)
+    small = early_ref[...] + jnp.where(row == norm_row, jnp.sum(g * xh, axis=0, keepdims=True), 0.0)
+    small_ref[...] = small
+    acc[...] = dg(att_ref[...], low, 1, 0)
+    nx, w, _ = keep_ref.shape
+    for x in range(nx):
+        keep_ref[x] = acc[pl.ds(pl.multiple_of((2 * x + me_ref[0]) * w, w), w)]
+        send_ref[x * w : (x + 1) * w] = acc[pl.ds(pl.multiple_of((2 * x + 1 - me_ref[0]) * w, w), w)].astype(bf16)
+    send_ref[nx * w :] = halves_of(small)
+
+
+def whole_block(shape):
+    return pl.BlockSpec(shape, lambda i, p: (0,) * len(shape))
+
+
+def one_step(kernel, name, outs, args, scratch, flops):
+    return pl.pallas_call(
+        kernel,
+        out_shape=tuple(jax.ShapeDtypeStruct(shape, dtype) for shape, dtype in outs),
+        grid_spec=pltpu.PrefetchScalarGridSpec(
+            num_scalar_prefetch=1,
+            grid=(1,),
+            in_specs=[whole_block(a.shape) for a in args[1:]],
+            out_specs=tuple(whole_block(shape) for shape, _ in outs),
+            scratch_shapes=scratch,
+        ),
+        compiler_params=pltpu.CompilerParams(vmem_limit_bytes=VMEM),
+        cost_estimate=pl.CostEstimate(
+            flops=flops, bytes_accessed=4 * sum(a.size for a in args), transcendentals=0
+        ),
+        name=name,
+    )(*args)
+
+
+def branch_back(ci, back, slot, dy, middle, gain, w, attT, early, norm_row, ctx):
+    rows = dy.shape[0]
+    mine = D // ctx
+    outs = (
+        ((rows, D), f32),
+        ((ctx, HEADS // ctx, HD, rows), bf16),
+        ((ctx // 2, mine, D), f32),
+        ((ctx // 2 * mine + 2 * early.shape[0], D), bf16),
+        (early.shape, f32),
+    )
+    return one_step(
+        functools.partial(branch_kernel, norm_row),
+        "branch_back",
+        outs,
+        (ci, back, slot, dy, middle, gain, w, attT, early),
+        [pltpu.VMEM((D, D), f32)],
+        2 * rows * D * (back.shape[0] + 2 * D),
+    )
+
+
+def go_kernel(me_ref, keep_ref, got_ref, small_ref, own_ref, send_ref, sum_ref, acc):
+    nx, w, _ = keep_ref.shape
+    for x in range(nx):
+        acc[x] = keep_ref[x] + got_ref[x * w : (x + 1) * w].astype(f32)
+    small = small_ref[...] + sum_halves(got_ref[nx * w :])
+    sum_ref[...] = small
+    own_ref[...] = acc[me_ref[0]]
+    send_ref[:w] = acc[1 - me_ref[0]].astype(bf16)
+    send_ref[w:] = halves_of(small)
+
+
+def go_step(xi, keep, got, small):
+    w = keep.shape[1]
+    outs = (((w, D), f32), ((w + 2 * small.shape[0], D), bf16), (small.shape, f32))
+    return one_step(go_kernel, "go_step", outs, (xi, keep, got, small), [pltpu.VMEM(keep.shape, f32)], 0)
+
+
+def weight_rows_kernel(half_ref, dT_ref, normed_ref, go_ref, got_ref, early_ref, keep_ref, send_ref, small_ref, acc):
     n = dT_ref.shape[0]
+    w = go_ref.shape[0]
     half = keep_ref.shape[0]
     acc[:n] = dg(dT_ref[...], normed_ref[...], 1, 0)
-    acc[n:] = go_ref[...]
+    acc[n:] = go_ref[...] + got_ref[:w].astype(f32)
+    small = early_ref[...] + sum_halves(got_ref[w:])
+    small_ref[...] = small
     a = pl.multiple_of(half_ref[0] * half, half)
     b = pl.multiple_of((1 - half_ref[0]) * half, half)
     keep_ref[...] = acc[pl.ds(a, half)]
     send_ref[:half] = acc[pl.ds(b, half)].astype(bf16)
-    send_ref[half:] = small_ref[...]
-
-
-def weight_rows(half, dT, normed, go, small):
+    send_ref[half:] = halves_of(small)
+
+
+def weight_rows(half, dT, normed, go, got, small):
     rows = dT.shape[0] + go.shape[0]
-    extra = small.shape[0]
-    args = (dT, normed, go, small)
-    return pl.pallas_call(
+    outs = (((rows // 2, D), f32), ((rows // 2 + 2 * small.shape[0], D), bf16), (small.shape, f32))
+    return one_step(
         weight_rows_kernel,
-        out_shape=(
-            jax.ShapeDtypeStruct((rows // 2, D), f32),
-            jax.ShapeDtypeStruct((rows // 2 + extra, D), bf16),
-        ),
-        grid_spec=pltpu.PrefetchScalarGridSpec(
-            num_scalar_prefetch=1,
-            grid=(1,),
-            in_specs=[pl.BlockSpec(a.shape, lambda i, p: (0, 0)) for a in args],
-            out_specs=(
-                pl.BlockSpec((rows // 2, D), lambda i, p: (0, 0)),
-                pl.BlockSpec((rows // 2 + extra, D), lambda i, p: (0, 0)),
-            ),
-            scratch_shapes=[pltpu.VMEM((rows, D), f32)],
-        ),
-        compiler_params=pltpu.CompilerParams(vmem_limit_bytes=VMEM),
-        cost_estimate=pl.CostEstimate(
-            flops=2 * dT.size * D, bytes_accessed=2 * dT.size + 2 * normed.size + 6 * rows * D, transcendentals=0
-        ),
-        name="weight_rows",
-    )(half.astype(jnp.int32).reshape(1), *args)
+        "weight_rows",
+        outs,
+        (half, dT, normed, go, got, small),
+        [pltpu.VMEM((rows, D), f32)],
+        2 * dT.size * D,
+    )
+
+
+def share_kernel(me_ref, half_ref, got_ref, early_ref, own_ref, *refs):
+    dp = len(refs) - 1
+    sends, small_ref, acc = refs[: dp - 1], refs[dp - 1], refs[dp]
+    half = half_ref.shape[0]
+    w = half // dp
+    acc[...] = half_ref[...] + got_ref[:half].astype(f32)
+    small = early_ref[...] + sum_halves(got_ref[half:])
+    small_ref[...] = small
+
+    def share(step):
+        return acc[pl.ds(pl.multiple_of(lax.rem(me_ref[0] + step, dp) * w, w), w)]
+
+    own_ref[...] = share(0)
+    for step in range(1, dp):
+        sends[step - 1][:w] = share(step).astype(bf16)
+        sends[step - 1][w:] = halves_of(small)
+
+
+def share_step(zi, half, got, small, dp):
+    w = half.shape[0] // dp
+    outs = (((w, D), f32),) + (((w + 2 * small.shape[0], D), bf16),) * (dp - 1) + ((small.shape, f32),)
+    return one_step(
+        functools.partial(share_kernel),
+        "share_step",
+        outs,
+        (zi, half, got, small),
+        [pltpu.VMEM(half.shape, f32)],
+        0,
+    )
 
 
 def finish_kernel(dp, me_ref, *refs):
@@ -547,11 +681,6 @@
     return lax.dynamic_index_in_dim(v, index, 0, keepdims=False)
 
 
-def two(v):
-    high = lax.reduce_precision(v, 8, 7)
-    return jnp.concatenate([high, v - high], axis=0).astype(bf16)
-
-
 def one(v):
     v = v.astype(f32)
     n = v.shape[0] // 2
@@ -567,6 +696,10 @@
     for s in range(1, lax.axis_size("dp")):
         out = out + shift(v, "dp", s)
     return out
+
+
+def index(i):
+    return i.astype(jnp.int32).reshape(1)
 
 
 def tie(*arrays):
@@ -639,18 +772,17 @@
     dy_low = cotangent.reshape(rows, D)
     dy = dy_low.astype(f32)
     counts = jnp.sum(hot, axis=0)
+    counts = add_shifts(add_pair(counts))
     counts = counts + swap(counts, "core")
-    counts = counts + swap(counts, "x")
     so_far = project(ctx_i, tok, gain1, w_own, ctx, None)
     so_far = project(ctx_i ^ 1, near, gain1, w_own, ctx, so_far)
-    other, dy_packed, counts, *so_far = tie(other, pack(dy_low), counts, *so_far)
+    dy_packed, counts, *so_far = tie(pack(dy_low), counts, *so_far)
+    dy_rows = trade(dy_packed)
+    other, *so_far = tie(other, *so_far)
     far = swap(other, "core")
-    dy_rows = trade(dy_packed)
-    counts = add_pair(counts)
+    counts = counts + swap(tie(counts, other)[0], "x")
     so_far = project(ctx_i ^ 2, other, gain1, w_own, ctx, so_far)
-    so_far = project(ctx_i ^ 3, far, gain1, w_own, ctx, so_far)
-    counts, normed_all, qkvT, kv = tie(counts, *so_far)
-    counts = add_shifts(counts)
+    normed_all, qkvT, kv = project(ctx_i ^ 3, far, gain1, w_own, ctx, so_far)
     oT, osend, lse = attend(qkvT, kv, ctx)
     osend, dy_rows, counts = tie(osend, dy_rows, counts)
     attT = turn(osend).reshape(D, rows)
@@ -668,7 +800,9 @@
     gating = jax.nn.sigmoid(jnp.sum(hot * dg(second, w_router, 1, 0), axis=1))
 
     up = expert_up(pick, dy_rows, w_out)
+    sig = jnp.pad(jnp.sum(hot * gating[:, None], axis=0), (0, D - experts))
     x_rows = trade(pack(second))
+    x_rows, gating, sig = tie(x_rows, gating, sig)
     active, grad_hidden, back_rows, router_row, gate = expert_mid(pick, x_rows, up, w_in, wr, load)
     returned = trade(back_rows)
     keep, send, produced = expert_grads(pick, x_rows, dy_rows, gate, active, grad_hidden, w_out, dp, nx)
@@ -683,66 +817,55 @@
         moving = shift(moving, "dp", 1).astype(f32) + chunk(zi - 2 - step)
         return moving if step == dp - 2 else moving.astype(bf16)
 
-    grad_second = dg(spread, returned, 0, 0)
-    grad_middle = dy + norm_back(grad_second * norm2_gain, xh2, rstd2)
-    branch = grad_middle.astype(bf16)
-    attT_grad = dg(w_output, branch, 1, 1).astype(bf16).reshape(ctx, heads, HD, rows)
-    do_first, do_later = turn(attT_grad[:, :1]), turn(attT_grad[:, 1:])
-
-    go = dg(attT, branch, 1, 0).reshape(nx, 2, mine, D)
     router_rows = (jnp.arange(experts) == expert_id).astype(f32)[:, None] * router_row
-    sig = jnp.pad(jnp.sum(hot * gating[:, None], axis=0), (0, D - experts))
-    small = jnp.concatenate([router_rows, jnp.sum(grad_second * xh2, axis=0)[None], sig[None]], axis=0)
+    small = jnp.concatenate([router_rows, jnp.zeros((1, D), f32), sig[None]], axis=0)
     small = jnp.pad(small, ((0, -small.shape[0] % 8), (0, 0)))
-    go_send = lax.dynamic_index_in_dim(go, 1 - ci, 1, keepdims=False).astype(bf16).reshape(-1, D)
-    go_send = jnp.concatenate([go_send, two(small)], axis=0)
-    go_keep = lax.dynamic_index_in_dim(go, ci, 1, keepdims=False)
-
+    grad_middle, heads_grad, go, go_send, small = branch_back(
+        index(ci), returned, slot[None], dy_low, middle, norm2_gain.reshape(1, D), w_output, attT, small, experts, ctx
+    )
+    do = turn(heads_grad)
+
+    go_got = swap(go_send, "core")
     moving = chunk(zi - 1).astype(bf16)
-    do_first, moving, go_send = tie(do_first, moving, go_send)
+    go, go_send, small = go_step(index(xi), go, go_got, small)
+    do, moving, go_send = tie(do, moving, go_send)
     moving = ring(moving, 0)
-    go_got = swap(go_send, "core")
-    so_far = attend_back(qkvT, kv, do_first, 0, oT, lse, 0, None)
-    do_later, go_got, produced, *so_far = tie(do_later, go_got, produced, *so_far)
-    go = go_keep + go_got[: nx * mine].astype(f32).reshape(nx, mine, D)
-    small = small + one(go_got[nx * mine :])
-    go_got = swap(jnp.concatenate([at(go, 1 - xi).astype(bf16), two(small)], axis=0), "x")
+    go_got = swap(go_send, "x")
+
+    so_far = attend_back(qkvT, kv, do, 0, oT, lse, 0, None)
+    go_got, produced, *so_far = tie(go_got, produced, *so_far)
     went_back = trade(produced)
-    so_far = attend_back(qkvT, kv, do_later, 0, oT, lse, 1, so_far)
-    go_got, moving, *so_far = tie(go_got, moving, *so_far)
-    go = at(go, xi) + go_got[:mine].astype(f32)
-    small = small + one(go_got[mine:])
+    so_far = attend_back(qkvT, kv, do, 1, oT, lse, 1, so_far)
+    moving, *so_far = tie(moving, *so_far)
     moving = ring(moving, 1)
     for h in range(2, heads):
-        so_far = attend_back(qkvT, kv, do_later, h - 1, oT, lse, h, so_far)
+        so_far = attend_back(qkvT, kv, do, h, oT, lse, h, so_far)
     went_back, dT, dsend = tie(went_back, *so_far)
     output = (middle + gating[:, None] * dg(spread, went_back, 0, 0)).astype(bf16)
     got = turn(dsend)
 
     ei2 = ei if owners == 2 else jnp.zeros_like(ei)
-    half, send = weight_rows(ei2, dT.reshape(3 * mine, length), normed_all, go, two(small))
-    cut_at = half.shape[0]
+    half, send, small = weight_rows(index(ei2), dT.reshape(3 * mine, length), normed_all, go, go_got, small)
     if owners == 2:
         gift = swap(send, "expert")
         gift, moving = tie(gift, moving)
-        halves = [half + gift[:cut_at].astype(f32)]
-        small = small + one(gift[cut_at:])
+        halves = [(half, gift)]
     else:
-        halves = [lax.psum(half, "expert"), lax.psum(send[:cut_at].astype(f32), "expert")]
+        cut_at = half.shape[0]
         small = lax.psum(small, "expert")
+        nothing = jnp.zeros_like(send)
+        halves = [(lax.psum(half, "expert"), nothing), (lax.psum(send[:cut_at].astype(f32), "expert"), nothing)]
     pieces = []
-    for part in halves:
-        part = part.reshape(dp, -1, D)
-        share = at(part, zi)
-        more = small
-        for step in range(1, dp):
-            gift = jnp.concatenate([at(part, (zi + step) % dp).astype(bf16), two(small)], axis=0)
-            gift = shift(gift, "dp", step)
+    for part, gift in halves:
+        share, *gifts, more = share_step(index(zi), part, gift, small, dp)
+        gifts = [shift(gift, "dp", step + 1) for step, gift in enumerate(gifts)]
+        for gift in gifts:
+            more = more + one(gift[share.shape[0] :])
             share = share + gift[: share.shape[0]].astype(f32)
-            more = more + one(gift[share.shape[0] :])
         share = share.astype(bf16)
         pieces.append(jnp.concatenate([share] + [shift(share, "dp", step) for step in range(1, dp)], axis=0))
     small = more
+    moving, *pieces = tie(moving, *pieces)
     for step in range(2, dp - 1):
         moving = ring(moving, step)
 

time: 414 us -> 364 us (0.88)
  blocking collectives: 15.6 us -> 0 us
  Pallas kernels: 132 us -> 146 us
  waiting for transfers between devices: 111 us -> 99 us
  other arithmetic: 36.3 us -> 25.7 us
  starting transfers between devices: 62.8 us -> 53.9 us
  local copies, waits for them, and re-layouts: 24.5 us -> 17.1 us
  matrix products: 20.4 us -> 13.3 us
    ppermute x18, waiting for transfers between devices: 56.1 us -> 31 us  [swap(): return lax.ppermute(v, axis, [(0, 1), (1, 0)])]
    all_to_all x3, waiting for transfers between devices: 0.01 us -> 16.1 us  [turn(): lax.all_to_all(v, ('x', 'core'), split_axis=0, concat_axis=0, tiled=True)]
    all_to_all x1 -> x0, blocking collectives: 15.6 us -> none  [turn(): lax.all_to_all(v, ('x', 'core'), split_axis=0, concat_axis=0, tiled=True)]
    pallas_call x1 -> x4, Pallas kernels: 6 us -> 19.1 us  [one_step(): pl.pallas_call(kernel, out_shape=tuple((jax.ShapeDtypeStruct(shape, dtype...]
    dot_general x12 -> x9, matrix products: 20.4 us -> 13.3 us  [dg(): lax.dot_general(a, b, (((ca,), (cb,)), ((), ())), preferred_element_type=...]
    ppermute x12, starting transfers between devices: 19.7 us -> 13.7 us  [shift(): return lax.ppermute(v, axis, [(i, (i + step) % n) for i in range(n)])]
    slice x3 -> x0, local copies, waits for them, and re-layouts: 4.41 us -> none  [the longest x2 2.5 us: per_device(): do_first, do_later = (turn(attT_grad[:, :1]), turn(attT_grad[:, 1:]))]
    add x5 -> x1, other arithmetic: 4.23 us -> 0.01 us  [per_device(): counts = counts + swap(tie(counts, other)[0], 'x')]
  transfers between devices with their start and end apart: 37 -> 37, of which waited for: 12 -> 18; matrix products, arithmetic and copies ran while one was open for 17% -> 11% of each run, Pallas kernels for 24% -> 34%
where the time goes in v4:
time: 364 us; the launch traced here: 358 us
  Pallas kernels  146 us (40%)
  waiting for transfers between devices  99 us (27%)
  starting transfers between devices  53.9 us (15%)
  other arithmetic  25.7 us (7%)
  local copies, waits for them, and re-layouts  17.1 us (5%)
  matrix products  13.3 us (4%)
    ppermute x12, waiting for transfers between devices, shift(): return lax.ppermute(v, axis, [(i, (i + step) % n) for i in range(n)])  44.2 us
    ppermute x18, waiting for transfers between devices, swap(): return lax.ppermute(v, axis, [(0, 1), (1, 0)])  31 us
    pallas_call x3, Pallas kernels, attend_back(): pl.pallas_call(functools.partial(attend_back_kernel, h % 2 * HD, hv % 2 *...  28 us
    pallas_call x1, Pallas kernels, expert_mid(): pl.pallas_call(mid_kernel, out_shape=(jax.ShapeDtypeStruct((rows, ff), bf...  24.8 us
    pallas_call x1, Pallas kernels, expert_grads(): pl.pallas_call(grads_kernel, out_shape=(part, part, jax.ShapeDtypeStruct(...  24.2 us
    pallas_call x4, Pallas kernels, one_step(): pl.pallas_call(kernel, out_shape=tuple((jax.ShapeDtypeStruct(shape, dtype...  19.1 us
    all_to_all x3, waiting for transfers between devices, turn(): lax.all_to_all(v, ('x', 'core'), split_axis=0, concat_axis=0, tiled=True)  16.1 us
    all_to_all x4, starting transfers between devices, trade(): lax.all_to_all(v.reshape(nx * owners, cap, D), ('x', 'expert'), split_axi...  15.3 us
  transfers between devices with their start and end apart: 37, of which 18 were waited for; matrix products, arithmetic and copies ran while one was open for 11% of the time, Pallas kernels for 34%

profile of v4, /device:TPU:0, one launch (start us, length us, event | category | flops | bytes accessed | tf_op | source)
XLA Modules:
  0.0 357.7 jit_solution(18160283095686067801)
XLA Ops:
  12.5 3.8 %project.4 = (bf16[2048,768]{1,0:T(8,128)(2,1)}, bf16[576,2048]{1,0:T(8,128)(2,1)}, bf16[2048,384]{1,0:T(8,128)(2,1)}) custom-call(s32[1]{0:T(128)} %bitcast.6.place_ref, bf16[512,768]{1,0:T(8,128)(2,1)} %bitcast.107, f32[1,768]{1,0:T(1,128)} %reshape.299.gain_ref, bf16[768,576]{1,0:T(8,128)(2,1)} %pad_maximum_fusion.1.w_ref), custom_call_target="tpu_custom_call" | custom-call | flops 905969664 | bytes 3932160 | tf_op jit(solution)/shard_map/project/pallas_call | solution.py:51
  18.5 3.6 %collective-permute-start.4 = (f32[4]{0:T(128)S(1)}, f32[4]{0:T(128)S(1)}, u32[]{:S(2)}, u32[]{:S(2)}) collective-permute-start(f32[4]{0:T(128)S(1)} %add.271), channel_id=1, source_target_pairs={{0,24},{8,0},{16,8},{24,16},{1,25},{9,1},{17,9},{25,17},{2,26},{10... | collective-permute-start | bytes 56 | tf_op jit(solution)/shard_map/ppermute | solution.py:677
  29.5 3.8 %project.5 = (bf16[2048,768]{1,0:T(8,128)(2,1)}, bf16[576,2048]{1,0:T(8,128)(2,1)}, bf16[2048,384]{1,0:T(8,128)(2,1)}) custom-call(s32[1]{0:T(128)} %bitcast.5.place_ref, bf16[512,768]{1,0:T(8,128)(2,1)} %copy-done.15, f32[1,768]{1,0:T(1,128)} %reshape.299.gain_ref, ...), custom_call_target="tpu_custom_call", output_to_operand_aliasing={{0}: (4, {}), {1}: (5, {}), {2}: (6, {})} | custom-call | flops 905969664 | bytes 3932160 | tf_op jit(solution)/shard_map/project/pallas_call | solution.py:51
  34.1 3.9 %all-to-all-start = ((bf16[4,256,768]{2,1,0:T(8,128)(2,1)}), bf16[4,256,768]{2,1,0:T(8,128)(2,1)S(1)}, u32[]{:S(2)}, u32[]{:S(2)}) async-start(bf16[4,256,768]{2,1,0:T(8,128)(2,1)} %bitcast.111), calls=%async_computation | async-start | bytes 3145728 | tf_op jit(solution)/shard_map/all_to_all | solution.py:761
  40.0 3.8 %project.6 = (bf16[2048,768]{1,0:T(8,128)(2,1)}, bf16[576,2048]{1,0:T(8,128)(2,1)}, bf16[2048,384]{1,0:T(8,128)(2,1)}) custom-call(s32[1]{0:T(128)} %bitcast.7.place_ref, bf16[512,768]{1,0:T(8,128)(2,1)} %copy-done.14, f32[1,768]{1,0:T(1,128)} %reshape.299.gain_ref, ...), custom_call_target="tpu_custom_call", output_to_operand_aliasing={{0}: (4, {}), {1}: (5, {}), {2}: (6, {})} | custom-call | flops 905969664 | bytes 3932160 | tf_op jit(solution)/shard_map/project/pallas_call | solution.py:51
  43.8 13.8 %collective-permute-done.8 = f32[4]{0:T(128)S(1)} collective-permute-done((f32[4]{0:T(128)S(1)}, f32[4]{0:T(128)S(1)}, u32[]{:S(2)}, u32[]{:S(2)}) %collective-permute-start.8) | collective-permute-done | bytes 48 | tf_op jit(solution)/shard_map/ppermute | solution.py:672
  58.5 3.8 %project.7 = (bf16[2048,768]{1,0:T(8,128)(2,1)}, bf16[576,2048]{1,0:T(8,128)(2,1)}, bf16[2048,384]{1,0:T(8,128)(2,1)}) custom-call(s32[1]{0:T(128)} %bitcast.1.place_ref, bf16[512,768]{1,0:T(8,128)(2,1)} %copy-done.16, f32[1,768]{1,0:T(1,128)} %reshape.299.gain_ref, ...), custom_call_target="tpu_custom_call", output_to_operand_aliasing={{0}: (4, {}), {1}: (5, {}), {2}: (6, {})} | custom-call | flops 905969664 | bytes 3932160 | tf_op jit(solution)/shard_map/project/pallas_call | solution.py:51
  62.3 14.3 %attend.1 = (f32[192,2048]{1,0:T(8,128)}, bf16[4,3,64,512]{3,2,1,0:T(8,128)(2,1)}, f32[3,1,2048]{2,1,0:T(1,128)}) custom-call(bf16[576,2048]{1,0:T(8,128)(2,1)} %get-tuple-element.115.qT_ref.vT_ref.refs_0_.refs_2_, bf16[2048,384]{1,0:T(8,128)(2,1)} %get-tuple-element.116.k_ref.refs_1_.refs_3_, bf16[576,2048]{1,0:T(8,128)(2,1)} %get-tuple-element.115.qT_ref.vT_ref.refs_0_.refs_2_), custom_call_target="tpu_custom_call" | custom-call | flops 6442450944 | bytes 5505024 | tf_op jit(solution)/shard_map/attend/pallas_call | solution.py:115
  76.6 3.6 %all-to-all-start.1 = ((bf16[4,3,64,512]{3,2,1,0:T(8,128)(2,1)}), bf16[4,3,64,512]{3,2,1,0:T(8,128)(2,1)S(1)}, u32[]{:S(2)}, u32[]{:S(2)}) async-start(bf16[4,3,64,512]{3,2,1,0:T(8,128)(2,1)} %get-tuple-element.121), calls=%async_computation.1 | async-start | bytes 1572864 | tf_op jit(solution)/shard_map/all_to_all | solution.py:765
  80.8 11.0 %all-to-all-done.1 = bf16[4,3,64,512]{3,2,1,0:T(8,128)(2,1)S(1)} async-done(((bf16[4,3,64,512]{3,2,1,0:T(8,128)(2,1)}), bf16[4,3,64,512]{3,2,1,0:T(8,128)(2,1)S(1)}, u32[]{:S(2)}, u32[]{:S(2)}) %all-to-all-start.1) | async-done | bytes 786464 | tf_op jit(solution)/shard_map/all_to_all | solution.py:765
  97.7 3.6 all-to-all-start.2
  102.4 9.9 %expert_up.1.u_ref = bf16[1024,3072]{1,0:T(8,128)(2,1)} custom-call(s32[2]{0:T(128)} %pad_add_fusion.pick_ref, bf16[1024,768]{1,0:T(8,128)(2,1)} %bitcast.109, bf16[2,3072,768]{2,1,0:T(8,128)(2,1)} %wo_ref.3), custom_call_target="tpu_custom_call" | custom-call | flops 4831838208 | bytes 12582912 | tf_op jit(solution)/shard_map/expert_up/pallas_call | solution.py:242
  112.8 7.7 %all-to-all-done.2 = bf16[4,256,768]{2,1,0:T(8,128)(2,1)S(1)} async-done(((bf16[4,256,768]{2,1,0:T(8,128)(2,1)}), bf16[4,256,768]{2,1,0:T(8,128)(2,1)S(1)}, u32[]{:S(2)}, u32[]{:S(2)}) %all-to-all-start.2) | async-done | bytes 1572896 | tf_op jit(solution)/shard_map/all_to_all | solution.py:761
  121.7 24.8 %expert_mid.1 = (bf16[1024,3072]{1,0:T(8,128)(2,1)}, bf16[1024,3072]{1,0:T(8,128)(2,1)}, bf16[1024,768]{1,0:T(8,128)(2,1)}, f32[1,768]{1,0:T(1,128)}, f32[1024,128]{1,0:T(8,128)}) custom-call(s32[2]{0:T(128)} %pad_add_fusion.pick_ref, bf16[1024,768]{1,0:T(8,128)(2,1)} %bitcast.114, bf16[1024,3072]{1,0:T(8,128)(2,1)} %expert_up.1.u_ref, ...), custom_call_target="tpu_custom_call" | custom-call | flops 9663676416 | bytes 28311552 | tf_op jit(solution)/shard_map/expert_mid/pallas_call | solution.py:313
  146.5 3.7 %all-to-all-start.3 = ((bf16[4,256,768]{2,1,0:T(8,128)(2,1)}), bf16[4,256,768]{2,1,0:T(8,128)(2,1)S(1)}, u32[]{:S(2)}, u32[]{:S(2)}) async-start(bf16[4,256,768]{2,1,0:T(8,128)(2,1)} %bitcast.116), calls=%async_computation.3 | async-start | bytes 3145728 | tf_op jit(solution)/shard_map/all_to_all | solution.py:761
  150.3 24.2 %expert_grads.1 = (bf16[4,2,2,192,768]{4,3,2,1,0:T(8,128)(2,1)}, bf16[4,2,2,192,768]{4,3,2,1,0:T(8,128)(2,1)}, bf16[1024,768]{1,0:T(8,128)(2,1)}) custom-call(s32[2]{0:T(128)} %pad_add_fusion.pick_ref, bf16[1024,768]{1,0:T(8,128)(2,1)} %bitcast.115, bf16[1024,768]{1,0:T(8,128)(2,1)} %bitcast.110, f32[1024,128]{1,0:T(8,128)} %get-tuple-element.127.gate_ref, ...), custom_call_target="tpu_custom_call" | custom-call | flops 14495514624 | bytes 31457280 | tf_op jit(solution)/shard_map/expert_grads/pallas_call | solution.py:398
  176.7 7.3 %branch_back.1 = (f32[512,768]{1,0:T(8,128)}, bf16[4,3,64,512]{3,2,1,0:T(8,128)(2,1)}, f32[2,192,768]{2,1,0:T(8,128)}, bf16[400,768]{1,0:T(8,128)(2,1)}, f32[8,768]{1,0:T(8,128)}) custom-call(s32[1]{0:T(128)} %bitcast.12.me_ref, bf16[1024,768]{1,0:T(8,128)(2,1)} %bitcast.113, s32[1,512]{1,0:T(1,128)} %multiply_add_fusion.slot_ref, ...), custom_call_target="tpu_custom_call" | custom-call | flops 2013265920 | bytes 10253316 | tf_op jit(solution)/shard_map/branch_back/pallas_call | solution.py:490
  194.4 5.1 %all-to-all-done.4.refs_4_ = bf16[4,3,64,512]{3,2,1,0:T(8,128)(2,1)S(1)} async-done(((bf16[4,3,64,512]{3,2,1,0:T(8,128)(2,1)}), bf16[4,3,64,512]{3,2,1,0:T(8,128)(2,1)S(1)}, u32[]{:S(2)}, u32[]{:S(2)}) %all-to-all-start.4) | async-done | bytes 786464 | tf_op jit(solution)/shard_map/all_to_all | solution.py:765
  200.4 9.3 %attend_back_head0.1 = (bf16[3,192,2048]{2,1,0:T(8,128)(2,1)}, bf16[4,3,192,512]{3,2,1,0:T(8,128)(2,1)}) custom-call(bf16[576,2048]{1,0:T(8,128)(2,1)} %get-tuple-element.115.qT_ref.vT_ref.refs_0_.refs_2_, bf16[2048,384]{1,0:T(8,128)(2,1)} %get-tuple-element.116.k_ref.refs_1_.refs_3_, bf16[576,2048]{1,0:T(8,128)(2,1)} %get-tuple-element.115.qT_ref.vT_ref.refs_0_.refs_2_, ...), custom_call_target="tpu_custom_call" | custom-call | flops 5368709120 | bytes 3145728 | tf_op jit(solution)/shard_map/attend_back_head0/pallas_call | solution.py:213
  210.4 4.1 %all-to-all-start.5 = ((bf16[4,256,768]{2,1,0:T(8,128)(2,1)}), bf16[4,256,768]{2,1,0:T(8,128)(2,1)S(1)}, u32[]{:S(2)}, u32[]{:S(2)}) async-start(bf16[4,256,768]{2,1,0:T(8,128)(2,1)} %bitcast.21), calls=%async_computation.5 | async-start | bytes 3145728 | tf_op jit(solution)/shard_map/all_to_all | solution.py:761
  214.5 9.3 %attend_back_head1.1 = (bf16[3,192,2048]{2,1,0:T(8,128)(2,1)}, bf16[4,3,192,512]{3,2,1,0:T(8,128)(2,1)}) custom-call(bf16[576,2048]{1,0:T(8,128)(2,1)} %get-tuple-element.115.qT_ref.vT_ref.refs_0_.refs_2_, bf16[2048,384]{1,0:T(8,128)(2,1)} %get-tuple-element.116.k_ref.refs_1_.refs_3_, ...), custom_call_target="tpu_custom_call", output_to_operand_aliasing={{0}: (7, {}), {1}: (8, {})} | custom-call | flops 5368709120 | bytes 3145728 | tf_op jit(solution)/shard_map/attend_back_head1/pallas_call | solution.py:213
  223.9 5.3 %collective-permute-done.12 = bf16[2,2,192,768]{3,2,1,0:T(8,128)(2,1)S(1)} collective-permute-done((bf16[2,2,192,768]{3,2,1,0:T(8,128)(2,1)}, bf16[2,2,192,768]{3,2,1,0:T(8,128)(2,1)S(1)}, u32[]{:S(2)}, u32[]{:S(2)}) %collective-permute-start.12) | collective-permute-done | bytes 1179680 | tf_op jit(solution)/shard_map/ppermute | solution.py:677
  233.0 9.3 %attend_back_head2.1 = (bf16[3,192,2048]{2,1,0:T(8,128)(2,1)}, bf16[4,3,192,512]{3,2,1,0:T(8,128)(2,1)}) custom-call(bf16[576,2048]{1,0:T(8,128)(2,1)} %get-tuple-element.115.qT_ref.vT_ref.refs_0_.refs_2_, bf16[2048,384]{1,0:T(8,128)(2,1)} %get-tuple-element.116.k_ref.refs_1_.refs_3_, ...), custom_call_target="tpu_custom_call", output_to_operand_aliasing={{0}: (7, {}), {1}: (8, {})} | custom-call | flops 5368709120 | bytes 3145728 | tf_op jit(solution)/shard_map/attend_back_head2/pallas_call | solution.py:213
  242.4 6.7 %weight_rows.1 = (f32[384,768]{1,0:T(8,128)}, bf16[400,768]{1,0:T(8,128)(2,1)}, f32[8,768]{1,0:T(8,128)}) custom-call(s32[1]{0:T(128)} %bitcast.30.half_ref, bf16[576,2048]{1,0:T(8,128)(2,1)} %bitcast.129, bf16[2048,768]{1,0:T(8,128)(2,1)} %get-tuple-element.164.normed_ref, f32[192,768]{1,0:T(8,128)} %get-tuple-element.165.go_ref, ...), custom_call_target="tpu_custom_call" | custom-call | flops 1811939328 | bytes 12263428 | tf_op jit(solution)/shard_map/weight_rows/pallas_call | solution.py:490
  251.6 3.6 %all-to-all-start.6 = ((bf16[4,3,192,512]{3,2,1,0:T(8,128)(2,1)}), bf16[4,3,192,512]{3,2,1,0:T(8,128)(2,1)S(1)}, u32[]{:S(2)}, u32[]{:S(2)}) async-start(bf16[4,3,192,512]{3,2,1,0:T(8,128)(2,1)} %get-tuple-element.162), calls=%async_computation.6 | async-start | bytes 4718592 | tf_op jit(solution)/shard_map/all_to_all | solution.py:765
  255.3 6.1 %collective-permute-done.14 = bf16[2,2,192,768]{3,2,1,0:T(8,128)(2,1)} collective-permute-done((bf16[2,2,192,768]{3,2,1,0:T(8,128)(2,1)}, bf16[2,2,192,768]{3,2,1,0:T(8,128)(2,1)}, u32[]{:S(2)}, u32[]{:S(2)}) %collective-permute-start.14) | collective-permute-done | bytes 1179680 | tf_op jit(solution)/shard_map/ppermute | solution.py:677
  275.3 7.2 %collective-permute-done.16 = bf16[112,768]{1,0:T(8,128)(2,1)S(1)} collective-permute-done((bf16[112,768]{1,0:T(8,128)(2,1)}, bf16[112,768]{1,0:T(8,128)(2,1)S(1)}, u32[]{:S(2)}, u32[]{:S(2)}) %collective-permute-start.16) | collective-permute-done | bytes 172064 | tf_op jit(solution)/shard_map/ppermute | solution.py:677
  288.4 9.8 %collective-permute-done.19 = bf16[96,768]{1,0:T(8,128)(2,1)S(1)} collective-permute-done((bf16[96,768]{1,0:T(8,128)(2,1)S(1)}, bf16[96,768]{1,0:T(8,128)(2,1)S(1)}, u32[]{:S(2)}, u32[]{:S(2)}) %collective-permute-start.19) | collective-permute-done | bytes 147488 | tf_op jit(solution)/shard_map/ppermute | solution.py:677
  304.4 8.3 %collective-permute-done.21.refs_1_ = bf16[384,768]{1,0:T(8,128)(2,1)} collective-permute-done((bf16[384,768]{1,0:T(8,128)(2,1)}, bf16[384,768]{1,0:T(8,128)(2,1)}, u32[]{:S(2)}, u32[]{:S(2)}) %collective-permute-start.21) | collective-permute-done | bytes 589856 | tf_op jit(solution)/shard_map/ppermute | solution.py:672
  320.2 6.4 %collective-permute-done.23.refs_3_ = bf16[384,768]{1,0:T(8,128)(2,1)} collective-permute-done((bf16[384,768]{1,0:T(8,128)(2,1)}, bf16[384,768]{1,0:T(8,128)(2,1)}, u32[]{:S(2)}, u32[]{:S(2)}) %collective-permute-start.23) | collective-permute-done | bytes 589856 | tf_op jit(solution)/shard_map/ppermute | solution.py:672
  326.6 8.3 %collective-permute-done.28 = bf16[2,2,192,768]{3,2,1,0:T(8,128)(2,1)} collective-permute-done((bf16[2,2,192,768]{3,2,1,0:T(8,128)(2,1)}, bf16[2,2,192,768]{3,2,1,0:T(8,128)(2,1)}, u32[]{:S(2)}, u32[]{:S(2)}) %collective-permute-start.28) | collective-permute-done | bytes 1179680 | tf_op jit(solution)/shard_map/ppermute | solution.py:677
  341.6 10.2 %finish.1 = (f32[768,768]{1,0:T(8,128)}, f32[768,768]{1,0:T(8,128)}, f32[768,768]{1,0:T(8,128)}, f32[768,768]{1,0:T(8,128)}, f32[768,1]{1,0:T(8,128)}) custom-call(s32[4]{0:T(128)} %pad_add_fusion.1.me_ref, bf16[384,768]{1,0:T(8,128)(2,1)} %pad_maximum_fusion.2.refs_0_, bf16[384,768]{1,0:T(8,128)(2,1)} %collective-permute-done.21.refs_1_, ...), custom_call_target="tpu_custom_call" | custom-call | flops 4718592 | bytes 18874368 | tf_op jit(solution)/shard_map/finish/pallas_call | solution.py:650
  (182 shorter events, 99.0 us)
Async XLA Ops:
  0.6 32.6 %collective-permute-start = (bf16[512,768]{1,0:T(8,128)(2,1)}, bf16[512,768]{1,0:T(8,128)(2,1)S(1)}, u32[]{:S(2)}, u32[]{:S(2)}) collective-permute-start(bf16[512,768]{1,0:T(8,128)(2,1)} %bitcast.105), channel_id=1, source_target_pairs={{0,4},{4,0},{1,5},{5,1},{2,6},{6,2},{3,7},{7,3},{8,12},{12,8},{9,1... | collective-permute-start | bytes 2359304 | tf_op jit(solution)/shard_map/ppermute | solution.py:672
  3.6 24.9 %collective-permute-start.6 = (bf16[512,768]{1,0:T(8,128)(2,1)}, bf16[512,768]{1,0:T(8,128)(2,1)S(1)}, u32[]{:S(2)}, u32[]{:S(2)}) collective-permute-start(bf16[512,768]{1,0:T(8,128)(2,1)} %bitcast.106), channel_id=1, source_target_pairs={{0,2},{2,0},{1,3},{3,1},{4,6},{6,4},{5,7},{7,5},{8,10},{10,8},{9,1... | collective-permute-start | bytes 2359304 | tf_op jit(solution)/shard_map/ppermute | solution.py:672
  4.4 14.0 %collective-permute-start.1 = (f32[4]{0:T(128)S(1)}, f32[4]{0:T(128)S(1)}, u32[]{:S(2)}, u32[]{:S(2)}) collective-permute-start(f32[4]{0:T(128)S(1)} %convert_reduce_fusion.1), channel_id=1, source_target_pairs={{0,1},{1,0},{2,3},{3,2},{4,5},{5,4},{6,7},{7,6},{8,9},{9,8},{10,11... | collective-permute-start | bytes 56 | tf_op jit(solution)/shard_map/ppermute | solution.py:672
  33.2 24.4 %collective-permute-start.7 = (bf16[512,768]{1,0:T(8,128)(2,1)S(1)}, bf16[512,768]{1,0:T(8,128)(2,1)S(1)}, u32[]{:S(2)}, u32[]{:S(2)}) collective-permute-start(bf16[512,768]{1,0:T(8,128)(2,1)S(1)} %collective-permute-done.tok_ref), channel_id=1, source_target_pairs={{0,2},{2,0},{1,3},{3,1},{4,6},{6,4},{5,7},{7,5},{8,10},{10,8},{9,1... | collective-permute-start | bytes 2359304 | tf_op jit(solution)/shard_map/ppermute | solution.py:672
  34.1 42.5 %all-to-all-start = ((bf16[4,256,768]{2,1,0:T(8,128)(2,1)}), bf16[4,256,768]{2,1,0:T(8,128)(2,1)S(1)}, u32[]{:S(2)}, u32[]{:S(2)}) async-start(bf16[4,256,768]{2,1,0:T(8,128)(2,1)} %bitcast.111), calls=%async_computation | async-start | bytes 3145728 | tf_op jit(solution)/shard_map/all_to_all | solution.py:761
  38.0 19.6 %collective-permute-start.8 = (f32[4]{0:T(128)S(1)}, f32[4]{0:T(128)S(1)}, u32[]{:S(2)}, u32[]{:S(2)}) collective-permute-start(f32[4]{0:T(128)S(1)} %add.275), channel_id=1, source_target_pairs={{0,4},{4,0},{1,5},{5,1},{2,6},{6,2},{3,7},{7,3},{8,12},{12,8},{9,1... | collective-permute-start | bytes 56 | tf_op jit(solution)/shard_map/ppermute | solution.py:672
  76.6 15.3 %all-to-all-start.1 = ((bf16[4,3,64,512]{3,2,1,0:T(8,128)(2,1)}), bf16[4,3,64,512]{3,2,1,0:T(8,128)(2,1)S(1)}, u32[]{:S(2)}, u32[]{:S(2)}) async-start(bf16[4,3,64,512]{3,2,1,0:T(8,128)(2,1)} %get-tuple-element.121), calls=%async_computation.1 | async-start | bytes 1572864 | tf_op jit(solution)/shard_map/all_to_all | solution.py:765
  97.7 22.9 %all-to-all-start.2 = ((bf16[4,256,768]{2,1,0:T(8,128)(2,1)}), bf16[4,256,768]{2,1,0:T(8,128)(2,1)S(1)}, u32[]{:S(2)}, u32[]{:S(2)}) async-start(bf16[4,256,768]{2,1,0:T(8,128)(2,1)} %bitcast.117), calls=%async_computation.2 | async-start | bytes 3145728 | tf_op jit(solution)/shard_map/all_to_all | solution.py:761
  146.5 27.9 %all-to-all-start.3 = ((bf16[4,256,768]{2,1,0:T(8,128)(2,1)}), bf16[4,256,768]{2,1,0:T(8,128)(2,1)S(1)}, u32[]{:S(2)}, u32[]{:S(2)}) async-start(bf16[4,256,768]{2,1,0:T(8,128)(2,1)} %bitcast.116), calls=%async_computation.3 | async-start | bytes 3145728 | tf_op jit(solution)/shard_map/all_to_all | solution.py:761
  174.5 17.0 %collective-permute-start.9 = (bf16[4,2,2,192,768]{4,3,2,1,0:T(8,128)(2,1)}, bf16[4,2,2,192,768]{4,3,2,1,0:T(8,128)(2,1)}, u32[]{:S(2)}, u32[]{:S(2)}) collective-permute-start(bf16[4,2,2,192,768]{4,3,2,1,0:T(8,128)(2,1)} %get-tuple-element.138), channel_id=1, source_target_pairs={{0,2},{2,0},{1,3},{3,1},{4,6},{6,4},{5,7},{7,5},{8,10},{10,8},{9,1... | collective-permute-start | bytes 14155784 | tf_op jit(solution)/shard_map/ppermute | solution.py:672
  184.4 15.1 %all-to-all-start.4 = ((bf16[4,3,64,512]{3,2,1,0:T(8,128)(2,1)}), bf16[4,3,64,512]{3,2,1,0:T(8,128)(2,1)S(1)}, u32[]{:S(2)}, u32[]{:S(2)}) async-start(bf16[4,3,64,512]{3,2,1,0:T(8,128)(2,1)} %get-tuple-element.136), calls=%async_computation.4 | async-start | bytes 1572864 | tf_op jit(solution)/shard_map/all_to_all | solution.py:765
  199.5 29.7 %collective-permute-start.12 = (bf16[2,2,192,768]{3,2,1,0:T(8,128)(2,1)}, bf16[2,2,192,768]{3,2,1,0:T(8,128)(2,1)S(1)}, u32[]{:S(2)}, u32[]{:S(2)}) collective-permute-start(bf16[2,2,192,768]{3,2,1,0:T(8,128)(2,1)} %fusion.20), channel_id=1, source_target_pairs={{0,8},{8,16},{16,24},{24,0},{1,9},{9,17},{17,25},{25,1},{2,10},{10... | collective-permute-start | bytes 3538952 | tf_op jit(solution)/shard_map/ppermute | solution.py:677
  199.7 10.0 %collective-permute-start.11 = (bf16[208,768]{1,0:T(8,128)(2,1)}, bf16[208,768]{1,0:T(8,128)(2,1)S(1)}, u32[]{:S(2)}, u32[]{:S(2)}) collective-permute-start(bf16[208,768]{1,0:T(8,128)(2,1)} %get-tuple-element.143), channel_id=1, source_target_pairs={{0,4},{4,0},{1,5},{5,1},{2,6},{6,2},{3,7},{7,3},{8,12},{12,8},{9,1... | collective-permute-start | bytes 958472 | tf_op jit(solution)/shard_map/ppermute | solution.py:672
  210.4 31.9 %all-to-all-start.5 = ((bf16[4,256,768]{2,1,0:T(8,128)(2,1)}), bf16[4,256,768]{2,1,0:T(8,128)(2,1)S(1)}, u32[]{:S(2)}, u32[]{:S(2)}) async-start(bf16[4,256,768]{2,1,0:T(8,128)(2,1)} %bitcast.21), calls=%async_computation.5 | async-start | bytes 3145728 | tf_op jit(solution)/shard_map/all_to_all | solution.py:761
  232.3 29.1 %collective-permute-start.14 = (bf16[2,2,192,768]{3,2,1,0:T(8,128)(2,1)}, bf16[2,2,192,768]{3,2,1,0:T(8,128)(2,1)}, u32[]{:S(2)}, u32[]{:S(2)}) collective-permute-start(bf16[2,2,192,768]{3,2,1,0:T(8,128)(2,1)} %fusion.1), channel_id=1, source_target_pairs={{0,8},{8,16},{16,24},{24,0},{1,9},{9,17},{17,25},{25,1},{2,10},{10... | collective-permute-start | bytes 3538952 | tf_op jit(solution)/shard_map/ppermute | solution.py:677
  249.0 15.9 %collective-permute-start.13 = (bf16[400,768]{1,0:T(8,128)(2,1)}, bf16[400,768]{1,0:T(8,128)(2,1)}, u32[]{:S(2)}, u32[]{:S(2)}) collective-permute-start(bf16[400,768]{1,0:T(8,128)(2,1)} %get-tuple-element.168), channel_id=1, source_target_pairs={{0,1},{1,0},{2,3},{3,2},{4,5},{5,4},{6,7},{7,6},{8,9},{9,8},{10,11... | collective-permute-start | bytes 1843208 | tf_op jit(solution)/shard_map/ppermute | solution.py:672
  251.6 63.4 %all-to-all-start.6 = ((bf16[4,3,192,512]{3,2,1,0:T(8,128)(2,1)}), bf16[4,3,192,512]{3,2,1,0:T(8,128)(2,1)S(1)}, u32[]{:S(2)}, u32[]{:S(2)}) async-start(bf16[4,3,192,512]{3,2,1,0:T(8,128)(2,1)} %get-tuple-element.162), calls=%async_computation.6 | async-start | bytes 4718592 | tf_op jit(solution)/shard_map/all_to_all | solution.py:765
  267.6 7.7 %collective-permute-start.17 = (bf16[112,768]{1,0:T(8,128)(2,1)}, bf16[112,768]{1,0:T(8,128)(2,1)S(1)}, u32[]{:S(2)}, u32[]{:S(2)}) collective-permute-start(bf16[112,768]{1,0:T(8,128)(2,1)} %get-tuple-element.177), channel_id=1, source_target_pairs={{0,24},{8,0},{16,8},{24,16},{1,25},{9,1},{17,9},{25,17},{2,26},{10... | collective-permute-start | bytes 516104 | tf_op jit(solution)/shard_map/ppermute | solution.py:677
  270.1 12.3 %collective-permute-start.16 = (bf16[112,768]{1,0:T(8,128)(2,1)}, bf16[112,768]{1,0:T(8,128)(2,1)S(1)}, u32[]{:S(2)}, u32[]{:S(2)}) collective-permute-start(bf16[112,768]{1,0:T(8,128)(2,1)} %get-tuple-element.176), channel_id=1, source_target_pairs={{0,16},{8,24},{16,0},{24,8},{1,17},{9,25},{17,1},{25,9},{2,18},{10... | collective-permute-start | bytes 516104 | tf_op jit(solution)/shard_map/ppermute | solution.py:677
  270.1 12.3 %collective-permute-start.15 = (bf16[112,768]{1,0:T(8,128)(2,1)}, bf16[112,768]{1,0:T(8,128)(2,1)S(1)}, u32[]{:S(2)}, u32[]{:S(2)}) collective-permute-start(bf16[112,768]{1,0:T(8,128)(2,1)} %get-tuple-element.175), channel_id=1, source_target_pairs={{0,8},{8,16},{16,24},{24,0},{1,9},{9,17},{17,25},{25,1},{2,10},{10... | collective-permute-start | bytes 516104 | tf_op jit(solution)/shard_map/ppermute | solution.py:677
  282.5 5.9 %collective-permute-start.20 = (bf16[96,768]{1,0:T(8,128)(2,1)S(1)}, bf16[96,768]{1,0:T(8,128)(2,1)S(1)}, u32[]{:S(2)}, u32[]{:S(2)}) collective-permute-start(bf16[96,768]{1,0:T(8,128)(2,1)S(1)} %add_convert_fusion.2), channel_id=1, source_target_pairs={{0,24},{8,0},{16,8},{24,16},{1,25},{9,1},{17,9},{25,17},{2,26},{10... | collective-permute-start | bytes 442376 | tf_op jit(solution)/shard_map/ppermute | solution.py:677
  283.9 14.3 %collective-permute-start.19 = (bf16[96,768]{1,0:T(8,128)(2,1)S(1)}, bf16[96,768]{1,0:T(8,128)(2,1)S(1)}, u32[]{:S(2)}, u32[]{:S(2)}) collective-permute-start(bf16[96,768]{1,0:T(8,128)(2,1)S(1)} %add_convert_fusion.2), channel_id=1, source_target_pairs={{0,16},{8,24},{16,0},{24,8},{1,17},{9,25},{17,1},{25,9},{2,18},{10... | collective-permute-start | bytes 442376 | tf_op jit(solution)/shard_map/ppermute | solution.py:677
  285.8 12.5 %collective-permute-start.18 = (bf16[96,768]{1,0:T(8,128)(2,1)S(1)}, bf16[96,768]{1,0:T(8,128)(2,1)S(1)}, u32[]{:S(2)}, u32[]{:S(2)}) collective-permute-start(bf16[96,768]{1,0:T(8,128)(2,1)S(1)} %add_convert_fusion.2), channel_id=1, source_target_pairs={{0,8},{8,16},{16,24},{24,0},{1,9},{9,17},{17,25},{25,1},{2,10},{10... | collective-permute-start | bytes 442376 | tf_op jit(solution)/shard_map/ppermute | solution.py:677
  299.1 13.7 %collective-permute-start.21 = (bf16[384,768]{1,0:T(8,128)(2,1)}, bf16[384,768]{1,0:T(8,128)(2,1)}, u32[]{:S(2)}, u32[]{:S(2)}) collective-permute-start(bf16[384,768]{1,0:T(8,128)(2,1)} %pad_maximum_fusion.2.refs_0_), channel_id=1, source_target_pairs={{0,1},{1,0},{2,3},{3,2},{4,5},{5,4},{6,7},{7,6},{8,9},{9,8},{10,11... | collective-permute-start | bytes 1769480 | tf_op jit(solution)/shard_map/ppermute | solution.py:672
  300.6 14.4 %collective-permute-start.22 = (bf16[384,768]{1,0:T(8,128)(2,1)}, bf16[384,768]{1,0:T(8,128)(2,1)}, u32[]{:S(2)}, u32[]{:S(2)}) collective-permute-start(bf16[384,768]{1,0:T(8,128)(2,1)} %pad_maximum_fusion.2.refs_0_), channel_id=1, source_target_pairs={{0,4},{4,0},{1,5},{5,1},{2,6},{6,2},{3,7},{7,3},{8,12},{12,8},{9,1... | collective-permute-start | bytes 1769480 | tf_op jit(solution)/shard_map/ppermute | solution.py:672
  304.3 36.5 %collective-permute-start.24 = (bf16[384,768]{1,0:T(8,128)(2,1)}, bf16[384,768]{1,0:T(8,128)(2,1)}, u32[]{:S(2)}, u32[]{:S(2)}) collective-permute-start(bf16[384,768]{1,0:T(8,128)(2,1)} %pad_maximum_fusion.2.refs_0_), channel_id=1, source_target_pairs={{0,2},{2,0},{1,3},{3,1},{4,6},{6,4},{5,7},{7,5},{8,10},{10,8},{9,1... | collective-permute-start | bytes 1769480 | tf_op jit(solution)/shard_map/ppermute | solution.py:672
  304.3 30.6 %collective-permute-start.28 = (bf16[2,2,192,768]{3,2,1,0:T(8,128)(2,1)}, bf16[2,2,192,768]{3,2,1,0:T(8,128)(2,1)}, u32[]{:S(2)}, u32[]{:S(2)}) collective-permute-start(bf16[2,2,192,768]{3,2,1,0:T(8,128)(2,1)} %fusion), channel_id=1, source_target_pairs={{0,8},{8,16},{16,24},{24,0},{1,9},{9,17},{17,25},{25,1},{2,10},{10... | collective-permute-start | bytes 3538952 | tf_op jit(solution)/shard_map/ppermute | solution.py:677
  312.7 13.9 %collective-permute-start.23 = (bf16[384,768]{1,0:T(8,128)(2,1)}, bf16[384,768]{1,0:T(8,128)(2,1)}, u32[]{:S(2)}, u32[]{:S(2)}) collective-permute-start(bf16[384,768]{1,0:T(8,128)(2,1)} %collective-permute-done.21.refs_1_), channel_id=1, source_target_pairs={{0,4},{4,0},{1,5},{5,1},{2,6},{6,2},{3,7},{7,3},{8,12},{12,8},{9,1... | collective-permute-start | bytes 1769480 | tf_op jit(solution)/shard_map/ppermute | solution.py:672
  313.7 27.0 %collective-permute-start.25 = (bf16[384,768]{1,0:T(8,128)(2,1)}, bf16[384,768]{1,0:T(8,128)(2,1)}, u32[]{:S(2)}, u32[]{:S(2)}) collective-permute-start(bf16[384,768]{1,0:T(8,128)(2,1)} %collective-permute-done.21.refs_1_), channel_id=1, source_target_pairs={{0,2},{2,0},{1,3},{3,1},{4,6},{6,4},{5,7},{7,5},{8,10},{10,8},{9,1... | collective-permute-start | bytes 1769480 | tf_op jit(solution)/shard_map/ppermute | solution.py:672
  315.0 25.8 %collective-permute-start.26 = (bf16[384,768]{1,0:T(8,128)(2,1)}, bf16[384,768]{1,0:T(8,128)(2,1)}, u32[]{:S(2)}, u32[]{:S(2)}) collective-permute-start(bf16[384,768]{1,0:T(8,128)(2,1)} %collective-permute-done.22.refs_2_), channel_id=1, source_target_pairs={{0,2},{2,0},{1,3},{3,1},{4,6},{6,4},{5,7},{7,5},{8,10},{10,8},{9,1... | collective-permute-start | bytes 1769480 | tf_op jit(solution)/shard_map/ppermute | solution.py:672
  326.6 14.2 %collective-permute-start.27 = (bf16[384,768]{1,0:T(8,128)(2,1)}, bf16[384,768]{1,0:T(8,128)(2,1)S(1)}, u32[]{:S(2)}, u32[]{:S(2)}) collective-permute-start(bf16[384,768]{1,0:T(8,128)(2,1)} %collective-permute-done.23.refs_3_), channel_id=1, source_target_pairs={{0,2},{2,0},{1,3},{3,1},{4,6},{6,4},{5,7},{7,5},{8,10},{10,8},{9,1... | collective-permute-start | bytes 1769480 | tf_op jit(solution)/shard_map/ppermute | solution.py:672
  338.3 15.3 %collective-permute-start.29 = (bf16[2,192,768]{2,1,0:T(8,128)(2,1)}, bf16[2,192,768]{2,1,0:T(8,128)(2,1)}, u32[]{:S(2)}, u32[]{:S(2)}) collective-permute-start(bf16[2,192,768]{2,1,0:T(8,128)(2,1)} %fusion.29), channel_id=1, source_target_pairs={{0,4},{4,0},{1,5},{5,1},{2,6},{6,2},{3,7},{7,3},{8,12},{12,8},{9,1... | collective-permute-start | bytes 1769480 | tf_op jit(solution)/shard_map/ppermute | solution.py:672
  (33 other events, 176.0 us)

commit v5 on v4

--- a/solution.py
+++ b/solution.py
@@ -269,34 +269,36 @@
     def _():
         logit = jnp.sum(x_ref[...].astype(f32) * wr_ref[...], axis=1, keepdims=True)
         gate[...] = jnp.broadcast_to(jax.nn.sigmoid(logit), gate.shape)
-
-    h = dg(x_ref[...], wi_ref[0], 1, 0)
-    h2 = h * h
-    t = jnp.tanh(h * (GELU_A + (GELU_A * GELU_B) * h2))
-    hp = 0.5 + 0.5 * t
-    dgelu = hp + (0.5 * h) * (1.0 - t * t) * (GELU_A + (3.0 * GELU_A * GELU_B) * h2)
-    u = u_ref[...].astype(f32)
-    act = (h * hp).astype(bf16)
-    act_ref[...] = act
-    g1 = jnp.sum(act.astype(f32) * u, axis=1, keepdims=True)
-    gh = (gate[:, :1] * u * dgelu).astype(bf16)
-    gh_ref[...] = gh
-    part = dg(gh, wi_ref[0], 1, 1)
-
-    @pl.when(f == 0)
-    def _():
-        acc[...] = part
-        gg[...] = jnp.broadcast_to(g1, gg.shape)
-
-    @pl.when(f > 0)
-    def _():
-        acc[...] += part
-        gg[...] += g1
+        acc[...] = jnp.zeros_like(acc)
+        gg[...] = jnp.zeros_like(gg)
+
+    step = 256
+    for r in range(0, x_ref.shape[0], step):
+        rs = slice(r, r + step)
+        for c in range(0, wi_ref.shape[2], step):
+            cs = slice(c, c + step)
+            h = dg(x_ref[rs], wi_ref[0, :, cs], 1, 0)
+            h2 = h * h
+            t = jnp.tanh(h * (GELU_A + (GELU_A * GELU_B) * h2))
+            hp = 0.5 + 0.5 * t
+            dgelu = hp + (h * (hp - hp * hp)) * (2.0 * GELU_A + (6.0 * GELU_A * GELU_B) * h2)
+            u = u_ref[rs, cs].astype(f32)
+            active = h * hp
+            act_ref[rs, cs] = active.astype(bf16)
+            au = active * u
+            lanes = au[:, :128]
+            for j in range(128, step, 128):
+                lanes = lanes + au[:, j : j + 128]
+            gg[rs] += lanes
+            gh = (gate[rs, :1] * (u * dgelu)).astype(bf16)
+            gh_ref[rs, cs] = gh
+            acc[rs] += dg(gh, wi_ref[0, :, cs], 1, 1)
 
     @pl.when(f == n - 1)
     def _():
         g = gate[:, :1]
-        sel = (g * (1.0 - g) * (gg[:, :1] + load_ref[:, :1])).astype(bf16).astype(f32)
+        got = jnp.sum(gg[...], axis=1, keepdims=True)
+        sel = (g * (1.0 - g) * (got + load_ref[:, :1])).astype(bf16).astype(f32)
         rows_ref[...] = (acc[...] + sel * wr_ref[...]).astype(bf16)
         router_ref[...] = jnp.sum(x_ref[...].astype(f32) * sel, axis=0, keepdims=True)
         gate_ref[...] = gate[...]
@@ -347,10 +349,9 @@
 
 
 def grads_kernel(
-    pick_ref, x_ref, dy_ref, gate_ref, act_ref, gh_ref, wo_ref, keep_ref, send_ref, prod_ref, acc, go, gi, gexp
+    pick_ref, x_ref, dy_ref, gate_ref, act_ref, gh_ref, keep_ref, send_ref, go, gi, gexp
 ):
     f = pl.program_id(0)
-    n = pl.num_programs(0)
 
     @pl.when(f == 0)
     def _():
@@ -358,16 +359,6 @@
 
     go[...] = dg(act_ref[...], gexp[...], 0, 0).astype(bf16)
     gi[...] = dg(gh_ref[...], x_ref[...], 0, 0).astype(bf16)
-    part = dg(act_ref[...], wo_ref[0], 1, 0)
-
-    @pl.when(f == 0)
-    def _():
-        acc[...] = part
-
-    @pl.when(f > 0)
-    def _():
-        acc[...] += part
-
     w = keep_ref.shape[3]
     me = pick_ref[1]
     for xx in range(keep_ref.shape[2]):
@@ -378,14 +369,10 @@
         send_ref[0, 0, xx] = gi[pl.ds(b, w)]
         send_ref[0, 1, xx] = go[pl.ds(b, w)]
 
-    @pl.when(f == n - 1)
-    def _():
-        prod_ref[...] = acc[...].astype(bf16)
-
-
-def expert_grads(pick, x, dy, gate, act, gh, w_out, dp, nx):
+
+def expert_grads(pick, x, dy, gate, act, gh, dp, nx):
     rows = x.shape[0]
-    ff = w_out.shape[1]
+    ff = act.shape[1]
     fc = ff // dp
     w = fc // (2 * nx)
 
@@ -397,21 +384,13 @@
     part_spec = pl.BlockSpec((1, 2, nx, w, D), lambda f, p: (f, 0, 0, 0, 0))
     return pl.pallas_call(
         grads_kernel,
-        out_shape=(part, part, jax.ShapeDtypeStruct((rows, D), bf16)),
+        out_shape=(part, part),
         grid_spec=pltpu.PrefetchScalarGridSpec(
             num_scalar_prefetch=1,
             grid=(dp,),
-            in_specs=[
-                full((rows, D)),
-                full((rows, D)),
-                full((rows, 128)),
-                wide,
-                wide,
-                pl.BlockSpec((1, fc, D), lambda f, p: (p[0], f, 0)),
-            ],
-            out_specs=(part_spec, part_spec, full((rows, D))),
+            in_specs=[full((rows, D)), full((rows, D)), full((rows, 128)), wide, wide],
+            out_specs=(part_spec, part_spec),
             scratch_shapes=[
-                pltpu.VMEM((rows, D), f32),
                 pltpu.VMEM((fc, D), bf16),
                 pltpu.VMEM((fc, D), bf16),
                 pltpu.VMEM((rows, D), bf16),
@@ -419,12 +398,52 @@
         ),
         compiler_params=pltpu.CompilerParams(vmem_limit_bytes=VMEM),
         cost_estimate=pl.CostEstimate(
-            flops=6 * rows * D * ff,
-            bytes_accessed=2 * (3 * rows * D + 3 * ff * D + 2 * rows * ff),
+            flops=4 * rows * D * ff,
+            bytes_accessed=2 * (2 * rows * D + 2 * ff * D + 2 * rows * ff),
             transcendentals=0,
         ),
         name="expert_grads",
-    )(pick, x, dy, gate, act, gh, w_out)
+    )(pick, x, dy, gate, act, gh)
+
+
+def out_kernel(pick_ref, act_ref, wo_ref, out_ref, acc):
+    f = pl.program_id(0)
+    part = dg(act_ref[...], wo_ref[0], 1, 0)
+
+    @pl.when(f == 0)
+    def _():
+        acc[...] = part
+
+    @pl.when(f > 0)
+    def _():
+        acc[...] += part
+
+    @pl.when(f == pl.num_programs(0) - 1)
+    def _():
+        out_ref[...] = acc[...].astype(bf16)
+
+
+def expert_out(pick, act, w_out, fc=768):
+    rows, ff = act.shape
+    return pl.pallas_call(
+        out_kernel,
+        out_shape=jax.ShapeDtypeStruct((rows, D), bf16),
+        grid_spec=pltpu.PrefetchScalarGridSpec(
+            num_scalar_prefetch=1,
+            grid=(ff // fc,),
+            in_specs=[
+                pl.BlockSpec((rows, fc), lambda f, p: (0, f)),
+                pl.BlockSpec((1, fc, D), lambda f, p: (p[0], f, 0)),
+            ],
+            out_specs=pl.BlockSpec((rows, D), lambda f, p: (0, 0)),
+            scratch_shapes=[pltpu.VMEM((rows, D), f32)],
+        ),
+        compiler_params=pltpu.CompilerParams(vmem_limit_bytes=VMEM),
+        cost_estimate=pl.CostEstimate(
+            flops=2 * rows * D * ff, bytes_accessed=2 * (rows * D + ff * D + rows * ff), transcendentals=0
+        ),
+        name="expert_out",
+    )(pick, act, w_out)
 
 
 def one_hot_slots(slot, slots):
@@ -743,6 +762,7 @@
     pick = jnp.stack([xi, ci]).astype(jnp.int32)
 
     tok = tokens.reshape(rows, D)
+    flat = tok.astype(f32)
     other = swap(tok, "x")
     near = swap(tok, "core")
 
@@ -771,29 +791,30 @@
     gain1 = norm1_gain.reshape(1, D)
     dy_low = cotangent.reshape(rows, D)
     dy = dy_low.astype(f32)
+    expert_id = ei * nx + xi
+    wr = lax.dynamic_slice(w_router, (0, expert_id), (D, 1)).astype(f32).reshape(1, D)
     counts = jnp.sum(hot, axis=0)
-    counts = add_shifts(add_pair(counts))
     counts = counts + swap(counts, "core")
+    counts = add_pair(counts)
     so_far = project(ctx_i, tok, gain1, w_own, ctx, None)
+    counts, dy_packed, *so_far = tie(counts, pack(dy_low), *so_far)
     so_far = project(ctx_i ^ 1, near, gain1, w_own, ctx, so_far)
-    dy_packed, counts, *so_far = tie(pack(dy_low), counts, *so_far)
+    other, dy_packed, *so_far = tie(other, dy_packed, *so_far)
+    far = swap(other, "core")
     dy_rows = trade(dy_packed)
-    other, *so_far = tie(other, *so_far)
-    far = swap(other, "core")
-    counts = counts + swap(tie(counts, other)[0], "x")
     so_far = project(ctx_i ^ 2, other, gain1, w_own, ctx, so_far)
     normed_all, qkvT, kv = project(ctx_i ^ 3, far, gain1, w_own, ctx, so_far)
     oT, osend, lse = attend(qkvT, kv, ctx)
     osend, dy_rows, counts = tie(osend, dy_rows, counts)
-    attT = turn(osend).reshape(D, rows)
-
+    attT = turn(osend)
+    counts = add_shifts(counts)
+    attT, counts = tie(attT, counts)
+    counts = counts + swap(counts, "x")
+    attT = attT.reshape(D, rows)
     mean_load = rows * ctx * dp * owners / experts
     load_term = balance_weight * (counts - mean_load) / (mean_load * mean_load)
-    expert_id = ei * nx + xi
     load = jnp.broadcast_to(lax.dynamic_slice(load_term, (expert_id,), (1,)).reshape(1, 1), (1, 128))
-    wr = lax.dynamic_slice(w_router, (0, expert_id), (D, 1)).astype(f32).reshape(1, D)
-
-    flat = tok.astype(f32)
+
     middle = flat + dg(attT, w_output, 0, 0)
     xh2, rstd2 = normal_form(middle)
     second = (xh2 * norm2_gain).astype(bf16)
@@ -802,10 +823,11 @@
     up = expert_up(pick, dy_rows, w_out)
     sig = jnp.pad(jnp.sum(hot * gating[:, None], axis=0), (0, D - experts))
     x_rows = trade(pack(second))
-    x_rows, gating, sig = tie(x_rows, gating, sig)
+    x_rows, gating, sig, slot, gain2 = tie(x_rows, gating, sig, slot[None], norm2_gain.reshape(1, D))
     active, grad_hidden, back_rows, router_row, gate = expert_mid(pick, x_rows, up, w_in, wr, load)
     returned = trade(back_rows)
-    keep, send, produced = expert_grads(pick, x_rows, dy_rows, gate, active, grad_hidden, w_out, dp, nx)
+    keep, send = expert_grads(pick, x_rows, dy_rows, gate, active, grad_hidden, dp, nx)
+    produced = expert_out(pick, tie(active, keep)[0], w_out)
     returned, keep, send, produced = tie(returned, keep, send, produced)
     taken = swap(send, "core")
     zi = lax.axis_index("dp")
@@ -821,25 +843,25 @@
     small = jnp.concatenate([router_rows, jnp.zeros((1, D), f32), sig[None]], axis=0)
     small = jnp.pad(small, ((0, -small.shape[0] % 8), (0, 0)))
     grad_middle, heads_grad, go, go_send, small = branch_back(
-        index(ci), returned, slot[None], dy_low, middle, norm2_gain.reshape(1, D), w_output, attT, small, experts, ctx
+        index(ci), returned, slot, dy_low, middle, gain2, w_output, attT, small, experts, ctx
     )
     do = turn(heads_grad)
 
+    moving = ring(chunk(zi - 1).astype(bf16), 0)
     go_got = swap(go_send, "core")
-    moving = chunk(zi - 1).astype(bf16)
     go, go_send, small = go_step(index(xi), go, go_got, small)
-    do, moving, go_send = tie(do, moving, go_send)
-    moving = ring(moving, 0)
+    do, go_send = tie(do, go_send)
     go_got = swap(go_send, "x")
 
     so_far = attend_back(qkvT, kv, do, 0, oT, lse, 0, None)
-    go_got, produced, *so_far = tie(go_got, produced, *so_far)
+    produced, *so_far = tie(produced, *so_far)
     went_back = trade(produced)
     so_far = attend_back(qkvT, kv, do, 1, oT, lse, 1, so_far)
     moving, *so_far = tie(moving, *so_far)
     moving = ring(moving, 1)
     for h in range(2, heads):
         so_far = attend_back(qkvT, kv, do, h, oT, lse, h, so_far)
+    go_got, *so_far = tie(go_got, *so_far)
     went_back, dT, dsend = tie(went_back, *so_far)
     output = (middle + gating[:, None] * dg(spread, went_back, 0, 0)).astype(bf16)
     got = turn(dsend)

time: 364 us -> 336 us (0.923)
  waiting for transfers between devices: 99 us -> 66.8 us
  starting transfers between devices: 53.9 us -> 58.2 us
    ppermute x12, waiting for transfers between devices: 44.2 us -> 32.1 us  [shift(): return lax.ppermute(v, axis, [(i, (i + step) % n) for i in range(n)])]
    all_to_all x3, waiting for transfers between devices: 16.1 us -> 4.93 us  [turn(): lax.all_to_all(v, ('x', 'core'), split_axis=0, concat_axis=0, tiled=True)]
    all_to_all x4, waiting for transfers between devices: 7.74 us -> 0.01 us  [trade(): lax.all_to_all(v.reshape(nx * owners, cap, D), ('x', 'expert'), split_axi...]
    pallas_call x1 -> x2, Pallas kernels: 24.2 us -> 27 us  [the longest x1 16.5 us: expert_grads(): pl.pallas_call(grads_kernel, out_shape=(part, part), grid_spec=pltpu.Pref...]
    unnamed x56 -> x68, local copies, waits for them, and re-layouts: 7.55 us -> 8.97 us
  transfers between devices with their start and end apart: 37 -> 37, of which waited for: 18 -> 16; matrix products, arithmetic and copies ran while one was open for 11% -> 12% of each run, Pallas kernels for 34% -> 37%
where the time goes in v5:
time: 336 us; the launch traced here: 330 us
  Pallas kernels  144 us (43%)
  waiting for transfers between devices  66.8 us (20%)
  starting transfers between devices  58.2 us (17%)
  other arithmetic  26.7 us (8%)
  local copies, waits for them, and re-layouts  18.8 us (6%)
  matrix products  12.5 us (4%)
    ppermute x12, waiting for transfers between devices, shift(): return lax.ppermute(v, axis, [(i, (i + step) % n) for i in range(n)])  32.1 us
    ppermute x18, waiting for transfers between devices, swap(): return lax.ppermute(v, axis, [(0, 1), (1, 0)])  29.8 us
    pallas_call x3, Pallas kernels, attend_back(): pl.pallas_call(functools.partial(attend_back_kernel, h % 2 * HD, hv % 2 *...  28 us
    pallas_call x1, Pallas kernels, expert_mid(): pl.pallas_call(mid_kernel, out_shape=(jax.ShapeDtypeStruct((rows, ff), bf...  21.4 us
    pallas_call x4, Pallas kernels, one_step(): pl.pallas_call(kernel, out_shape=tuple((jax.ShapeDtypeStruct(shape, dtype...  18.5 us
    ppermute x12, starting transfers between devices, shift(): return lax.ppermute(v, axis, [(i, (i + step) % n) for i in range(n)])  16.9 us
    pallas_call x1, Pallas kernels, expert_grads(): pl.pallas_call(grads_kernel, out_shape=(part, part), grid_spec=pltpu.Pref...  16.5 us
    ppermute x18, starting transfers between devices, swap(): return lax.ppermute(v, axis, [(0, 1), (1, 0)])  15.7 us
  transfers between devices with their start and end apart: 37, of which 16 were waited for; matrix products, arithmetic and copies ran while one was open for 12% of the time, Pallas kernels for 37%

profile of v5, /device:TPU:0, one launch (start us, length us, event | category | flops | bytes accessed | tf_op | source)
XLA Modules:
  0.0 330.4 jit_solution(4621803751492960844)
XLA Ops:
  10.4 3.8 %project.4 = (bf16[2048,768]{1,0:T(8,128)(2,1)}, bf16[576,2048]{1,0:T(8,128)(2,1)}, bf16[2048,384]{1,0:T(8,128)(2,1)}) custom-call(s32[1]{0:T(128)} %bitcast.5.place_ref, bf16[512,768]{1,0:T(8,128)(2,1)} %bitcast.107, f32[1,768]{1,0:T(1,128)} %reshape.294.gain_ref, bf16[768,576]{1,0:T(8,128)(2,1)} %pad_maximum_fusion.1.w_ref), custom_call_target="tpu_custom_call" | custom-call | flops 905969664 | bytes 3932160 | tf_op jit(solution)/shard_map/project/pallas_call | solution.py:51
  21.1 3.8 %project.5 = (bf16[2048,768]{1,0:T(8,128)(2,1)}, bf16[576,2048]{1,0:T(8,128)(2,1)}, bf16[2048,384]{1,0:T(8,128)(2,1)}) custom-call(s32[1]{0:T(128)} %bitcast.6.place_ref, bf16[512,768]{1,0:T(8,128)(2,1)} %copy-done.15, f32[1,768]{1,0:T(1,128)} %reshape.294.gain_ref, ...), custom_call_target="tpu_custom_call", output_to_operand_aliasing={{0}: (4, {}), {1}: (5, {}), {2}: (6, {})} | custom-call | flops 905969664 | bytes 3932160 | tf_op jit(solution)/shard_map/project/pallas_call | solution.py:51
  25.8 3.7 %all-to-all-start = ((bf16[4,256,768]{2,1,0:T(8,128)(2,1)}), bf16[4,256,768]{2,1,0:T(8,128)(2,1)S(1)}, u32[]{:S(2)}, u32[]{:S(2)}) async-start(bf16[4,256,768]{2,1,0:T(8,128)(2,1)} %bitcast.112), calls=%async_computation | async-start | bytes 3145728 | tf_op jit(solution)/shard_map/all_to_all | solution.py:781
  29.5 3.8 %project.6 = (bf16[2048,768]{1,0:T(8,128)(2,1)}, bf16[576,2048]{1,0:T(8,128)(2,1)}, bf16[2048,384]{1,0:T(8,128)(2,1)}) custom-call(s32[1]{0:T(128)} %bitcast.7.place_ref, bf16[512,768]{1,0:T(8,128)(2,1)} %copy-done.14, f32[1,768]{1,0:T(1,128)} %reshape.294.gain_ref, ...), custom_call_target="tpu_custom_call", output_to_operand_aliasing={{0}: (4, {}), {1}: (5, {}), {2}: (6, {})} | custom-call | flops 905969664 | bytes 3932160 | tf_op jit(solution)/shard_map/project/pallas_call | solution.py:51
  34.2 3.8 %project.7 = (bf16[2048,768]{1,0:T(8,128)(2,1)}, bf16[576,2048]{1,0:T(8,128)(2,1)}, bf16[2048,384]{1,0:T(8,128)(2,1)}) custom-call(s32[1]{0:T(128)} %bitcast.1.place_ref, bf16[512,768]{1,0:T(8,128)(2,1)} %copy-done.16, f32[1,768]{1,0:T(1,128)} %reshape.294.gain_ref, ...), custom_call_target="tpu_custom_call", output_to_operand_aliasing={{0}: (4, {}), {1}: (5, {}), {2}: (6, {})} | custom-call | flops 905969664 | bytes 3932160 | tf_op jit(solution)/shard_map/project/pallas_call | solution.py:51
  37.9 14.0 %attend.1 = (f32[192,2048]{1,0:T(8,128)}, bf16[4,3,64,512]{3,2,1,0:T(8,128)(2,1)}, f32[3,1,2048]{2,1,0:T(1,128)}) custom-call(bf16[576,2048]{1,0:T(8,128)(2,1)} %get-tuple-element.121.qT_ref.vT_ref.refs_0_.refs_2_, bf16[2048,384]{1,0:T(8,128)(2,1)} %get-tuple-element.122.k_ref.refs_1_.refs_3_, bf16[576,2048]{1,0:T(8,128)(2,1)} %get-tuple-element.121.qT_ref.vT_ref.refs_0_.refs_2_), custom_call_target="tpu_custom_call" | custom-call | flops 6442450944 | bytes 5505024 | tf_op jit(solution)/shard_map/attend/pallas_call | solution.py:115
  52.0 3.6 %all-to-all-start.1 = ((bf16[4,3,64,512]{3,2,1,0:T(8,128)(2,1)}), bf16[4,3,64,512]{3,2,1,0:T(8,128)(2,1)S(1)}, u32[]{:S(2)}, u32[]{:S(2)}) async-start(bf16[4,3,64,512]{3,2,1,0:T(8,128)(2,1)} %get-tuple-element.126), calls=%async_computation.1 | async-start | bytes 1572864 | tf_op jit(solution)/shard_map/all_to_all | solution.py:785
  56.8 3.6 %collective-permute-start.7 = (f32[4]{0:T(128)S(1)}, f32[4]{0:T(128)S(1)}, u32[]{:S(2)}, u32[]{:S(2)}) collective-permute-start(f32[4]{0:T(128)S(1)} %add.269), channel_id=1, source_target_pairs={{0,24},{8,0},{16,8},{24,16},{1,25},{9,1},{17,9},{25,17},{2,26},{10... | collective-permute-start | bytes 56 | tf_op jit(solution)/shard_map/ppermute | solution.py:696
  73.1 3.6 %all-to-all-start.2 = ((bf16[4,256,768]{2,1,0:T(8,128)(2,1)}), bf16[4,256,768]{2,1,0:T(8,128)(2,1)S(1)}, u32[]{:S(2)}, u32[]{:S(2)}) async-start(bf16[4,256,768]{2,1,0:T(8,128)(2,1)} %bitcast.116), calls=%async_computation.2 | async-start | bytes 3145728 | tf_op jit(solution)/shard_map/all_to_all | solution.py:781
  77.8 9.9 %expert_up.1.u_ref = bf16[1024,3072]{1,0:T(8,128)(2,1)} custom-call(s32[2]{0:T(128)} %pad_add_fusion.pick_ref, bf16[1024,768]{1,0:T(8,128)(2,1)} %bitcast.109, bf16[2,3072,768]{2,1,0:T(8,128)(2,1)} %wo_ref.3), custom_call_target="tpu_custom_call" | custom-call | flops 4831838208 | bytes 12582912 | tf_op jit(solution)/shard_map/expert_up/pallas_call | solution.py:242
  90.2 5.8 %collective-permute-done.8 = f32[4]{0:T(128)S(1)} collective-permute-done((f32[4]{0:T(128)S(1)}, f32[4]{0:T(128)S(1)}, u32[]{:S(2)}, u32[]{:S(2)}) %collective-permute-start.8) | collective-permute-done | bytes 48 | tf_op jit(solution)/shard_map/ppermute | solution.py:691
  97.8 21.4 %expert_mid.1 = (bf16[1024,3072]{1,0:T(8,128)(2,1)}, bf16[1024,3072]{1,0:T(8,128)(2,1)}, bf16[1024,768]{1,0:T(8,128)(2,1)}, f32[1,768]{1,0:T(1,128)}, f32[1024,128]{1,0:T(8,128)}) custom-call(s32[2]{0:T(128)} %pad_add_fusion.pick_ref, bf16[1024,768]{1,0:T(8,128)(2,1)} %bitcast.114, bf16[1024,3072]{1,0:T(8,128)(2,1)} %expert_up.1.u_ref, ...), custom_call_target="tpu_custom_call" | custom-call | flops 9663676416 | bytes 28311552 | tf_op jit(solution)/shard_map/expert_mid/pallas_call | solution.py:315
  119.2 4.0 %all-to-all-start.3 = ((bf16[4,256,768]{2,1,0:T(8,128)(2,1)}), bf16[4,256,768]{2,1,0:T(8,128)(2,1)S(1)}, u32[]{:S(2)}, u32[]{:S(2)}) async-start(bf16[4,256,768]{2,1,0:T(8,128)(2,1)} %bitcast.117), calls=%async_computation.3 | async-start | bytes 3145728 | tf_op jit(solution)/shard_map/all_to_all | solution.py:781
  123.2 16.5 %expert_grads.1 = (bf16[4,2,2,192,768]{4,3,2,1,0:T(8,128)(2,1)}, bf16[4,2,2,192,768]{4,3,2,1,0:T(8,128)(2,1)}) custom-call(s32[2]{0:T(128)} %pad_add_fusion.pick_ref, bf16[1024,768]{1,0:T(8,128)(2,1)} %bitcast.115, bf16[1024,768]{1,0:T(8,128)(2,1)} %bitcast.110, f32[1024,128]{1,0:T(8,128)} %get-tuple-element.134.gate_ref, ...), custom_call_target="tpu_custom_call" | custom-call | flops 9663676416 | bytes 25165824 | tf_op jit(solution)/shard_map/expert_grads/pallas_call | solution.py:385
  139.7 10.6 %expert_out.1 = bf16[1024,768]{1,0:T(8,128)(2,1)} custom-call(s32[2]{0:T(128)} %pad_add_fusion.pick_ref, bf16[1024,3072]{1,0:T(8,128)(2,1)} %get-tuple-element.139.act_ref, bf16[2,3072,768]{2,1,0:T(8,128)(2,1)} %wo_ref.3), custom_call_target="tpu_custom_call" | custom-call | flops 4831838208 | bytes 12582912 | tf_op jit(solution)/shard_map/expert_out/pallas_call | solution.py:428
  151.4 7.3 %branch_back.1 = (f32[512,768]{1,0:T(8,128)}, bf16[4,3,64,512]{3,2,1,0:T(8,128)(2,1)}, f32[2,192,768]{2,1,0:T(8,128)}, bf16[400,768]{1,0:T(8,128)(2,1)}, f32[8,768]{1,0:T(8,128)}) custom-call(s32[1]{0:T(128)} %bitcast.15.me_ref, bf16[1024,768]{1,0:T(8,128)(2,1)} %bitcast.113, s32[1,512]{1,0:T(1,128)} %multiply_add_fusion.slot_ref, ...), custom_call_target="tpu_custom_call" | custom-call | flops 2013265920 | bytes 10253316 | tf_op jit(solution)/shard_map/branch_back/pallas_call | solution.py:509
  158.9 3.5 %all-to-all-start.4 = ((bf16[4,3,64,512]{3,2,1,0:T(8,128)(2,1)}), bf16[4,3,64,512]{3,2,1,0:T(8,128)(2,1)S(1)}, u32[]{:S(2)}, u32[]{:S(2)}) async-start(bf16[4,3,64,512]{3,2,1,0:T(8,128)(2,1)} %get-tuple-element.146), calls=%async_computation.4 | async-start | bytes 1572864 | tf_op jit(solution)/shard_map/all_to_all | solution.py:785
  175.0 9.3 %attend_back_head0.1 = (bf16[3,192,2048]{2,1,0:T(8,128)(2,1)}, bf16[4,3,192,512]{3,2,1,0:T(8,128)(2,1)}) custom-call(bf16[576,2048]{1,0:T(8,128)(2,1)} %get-tuple-element.121.qT_ref.vT_ref.refs_0_.refs_2_, bf16[2048,384]{1,0:T(8,128)(2,1)} %get-tuple-element.122.k_ref.refs_1_.refs_3_, bf16[576,2048]{1,0:T(8,128)(2,1)} %get-tuple-element.121.qT_ref.vT_ref.refs_0_.refs_2_, ...), custom_call_target="tpu_custom_call" | custom-call | flops 5368709120 | bytes 3145728 | tf_op jit(solution)/shard_map/attend_back_head0/pallas_call | solution.py:213
  184.3 3.6 %all-to-all-start.5 = ((bf16[4,256,768]{2,1,0:T(8,128)(2,1)}), bf16[4,256,768]{2,1,0:T(8,128)(2,1)S(1)}, u32[]{:S(2)}, u32[]{:S(2)}) async-start(bf16[4,256,768]{2,1,0:T(8,128)(2,1)} %bitcast.20), calls=%async_computation.5 | async-start | bytes 3145728 | tf_op jit(solution)/shard_map/all_to_all | solution.py:781
  187.9 9.3 %attend_back_head1.1 = (bf16[3,192,2048]{2,1,0:T(8,128)(2,1)}, bf16[4,3,192,512]{3,2,1,0:T(8,128)(2,1)}) custom-call(bf16[576,2048]{1,0:T(8,128)(2,1)} %get-tuple-element.121.qT_ref.vT_ref.refs_0_.refs_2_, bf16[2048,384]{1,0:T(8,128)(2,1)} %get-tuple-element.122.k_ref.refs_1_.refs_3_, ...), custom_call_target="tpu_custom_call", output_to_operand_aliasing={{0}: (7, {}), {1}: (8, {})} | custom-call | flops 5368709120 | bytes 3145728 | tf_op jit(solution)/shard_map/attend_back_head1/pallas_call | solution.py:213
  204.6 9.3 %attend_back_head2.1 = (bf16[3,192,2048]{2,1,0:T(8,128)(2,1)}, bf16[4,3,192,512]{3,2,1,0:T(8,128)(2,1)}) custom-call(bf16[576,2048]{1,0:T(8,128)(2,1)} %get-tuple-element.121.qT_ref.vT_ref.refs_0_.refs_2_, bf16[2048,384]{1,0:T(8,128)(2,1)} %get-tuple-element.122.k_ref.refs_1_.refs_3_, ...), custom_call_target="tpu_custom_call", output_to_operand_aliasing={{0}: (7, {}), {1}: (8, {})} | custom-call | flops 5368709120 | bytes 3145728 | tf_op jit(solution)/shard_map/attend_back_head2/pallas_call | solution.py:213
  214.9 6.1 %weight_rows.1 = (f32[384,768]{1,0:T(8,128)}, bf16[400,768]{1,0:T(8,128)(2,1)}, f32[8,768]{1,0:T(8,128)}) custom-call(s32[1]{0:T(128)} %bitcast.30.half_ref, bf16[576,2048]{1,0:T(8,128)(2,1)} %bitcast.129, bf16[2048,768]{1,0:T(8,128)(2,1)} %get-tuple-element.174.normed_ref, f32[192,768]{1,0:T(8,128)} %get-tuple-element.175.go_ref, ...), custom_call_target="tpu_custom_call" | custom-call | flops 1811939328 | bytes 12263428 | tf_op jit(solution)/shard_map/weight_rows/pallas_call | solution.py:509
  223.1 3.6 %all-to-all-start.6 = ((bf16[4,3,192,512]{3,2,1,0:T(8,128)(2,1)}), bf16[4,3,192,512]{3,2,1,0:T(8,128)(2,1)S(1)}, u32[]{:S(2)}, u32[]{:S(2)}) async-start(bf16[4,3,192,512]{3,2,1,0:T(8,128)(2,1)} %get-tuple-element.172), calls=%async_computation.6 | async-start | bytes 4718592 | tf_op jit(solution)/shard_map/all_to_all | solution.py:785
  226.7 3.7 %collective-permute-done.14 = bf16[2,2,192,768]{3,2,1,0:T(8,128)(2,1)} collective-permute-done((bf16[2,2,192,768]{3,2,1,0:T(8,128)(2,1)}, bf16[2,2,192,768]{3,2,1,0:T(8,128)(2,1)}, u32[]{:S(2)}, u32[]{:S(2)}) %collective-permute-start.14) | collective-permute-done | bytes 1179680 | tf_op jit(solution)/shard_map/ppermute | solution.py:696
  230.5 3.6 %fusion = bf16[2,2,192,768]{3,2,1,0:T(8,128)(2,1)} fusion(bf16[2,2,192,768]{3,2,1,0:T(8,128)(2,1)} %collective-permute-done.14, bf16[4,2,2,192,768]{4,3,2,1,0:T(8,128)(2,1)} %collective-permute-done.11, s32[]{:T(128)S(6)} %select_n.114, bf16[4,2,2,192,768]{4,3,2,1,0:T(8,128)(2,1)} %get-tuple-element.158), kind=kLoop, calls=%fused_computation.7 | loop fusion | flops 3538944 | bytes 4718596 | tf_op jit(solution)/shard_map/convert_element_type | solution.py:840
  238.7 3.6 %collective-permute-start.17 = (bf16[112,768]{1,0:T(8,128)(2,1)}, bf16[112,768]{1,0:T(8,128)(2,1)S(1)}, u32[]{:S(2)}, u32[]{:S(2)}) collective-permute-start(bf16[112,768]{1,0:T(8,128)(2,1)} %get-tuple-element.187), channel_id=1, source_target_pairs={{0,24},{8,0},{16,8},{24,16},{1,25},{9,1},{17,9},{25,17},{2,26},{10... | collective-permute-start | bytes 516104 | tf_op jit(solution)/shard_map/ppermute | solution.py:696
  247.5 8.9 %collective-permute-done.16 = bf16[112,768]{1,0:T(8,128)(2,1)S(1)} collective-permute-done((bf16[112,768]{1,0:T(8,128)(2,1)}, bf16[112,768]{1,0:T(8,128)(2,1)S(1)}, u32[]{:S(2)}, u32[]{:S(2)}) %collective-permute-start.16) | collective-permute-done | bytes 172064 | tf_op jit(solution)/shard_map/ppermute | solution.py:696
  262.9 8.3 %collective-permute-done.19 = bf16[96,768]{1,0:T(8,128)(2,1)} collective-permute-done((bf16[96,768]{1,0:T(8,128)(2,1)S(1)}, bf16[96,768]{1,0:T(8,128)(2,1)}, u32[]{:S(2)}, u32[]{:S(2)}) %collective-permute-start.19) | collective-permute-done | bytes 147488 | tf_op jit(solution)/shard_map/ppermute | solution.py:696
  277.3 9.8 %collective-permute-done.21.refs_1_ = bf16[384,768]{1,0:T(8,128)(2,1)} collective-permute-done((bf16[384,768]{1,0:T(8,128)(2,1)}, bf16[384,768]{1,0:T(8,128)(2,1)}, u32[]{:S(2)}, u32[]{:S(2)}) %collective-permute-start.21) | collective-permute-done | bytes 589856 | tf_op jit(solution)/shard_map/ppermute | solution.py:691
  291.2 9.6 %collective-permute-done.23.refs_3_ = bf16[384,768]{1,0:T(8,128)(2,1)S(1)} collective-permute-done((bf16[384,768]{1,0:T(8,128)(2,1)}, bf16[384,768]{1,0:T(8,128)(2,1)S(1)}, u32[]{:S(2)}, u32[]{:S(2)}) %collective-permute-start.23) | collective-permute-done | bytes 589856 | tf_op jit(solution)/shard_map/ppermute | solution.py:691
  300.9 4.8 %collective-permute-done.28 = bf16[2,2,192,768]{3,2,1,0:T(8,128)(2,1)} collective-permute-done((bf16[2,2,192,768]{3,2,1,0:T(8,128)(2,1)}, bf16[2,2,192,768]{3,2,1,0:T(8,128)(2,1)}, u32[]{:S(2)}, u32[]{:S(2)}) %collective-permute-start.28) | collective-permute-done | bytes 1179680 | tf_op jit(solution)/shard_map/ppermute | solution.py:696
  314.2 10.2 %finish.1 = (f32[768,768]{1,0:T(8,128)}, f32[768,768]{1,0:T(8,128)}, f32[768,768]{1,0:T(8,128)}, f32[768,768]{1,0:T(8,128)}, f32[768,1]{1,0:T(8,128)}) custom-call(s32[4]{0:T(128)} %pad_add_fusion.1.me_ref, bf16[384,768]{1,0:T(8,128)(2,1)} %pad_maximum_fusion.2.refs_0_, bf16[384,768]{1,0:T(8,128)(2,1)} %collective-permute-done.21.refs_1_, ...), custom_call_target="tpu_custom_call" | custom-call | flops 4718592 | bytes 18874368 | tf_op jit(solution)/shard_map/finish/pallas_call | solution.py:669
  (194 shorter events, 100.8 us)
Async XLA Ops:
  0.6 24.3 %collective-permute-start = (bf16[512,768]{1,0:T(8,128)(2,1)}, bf16[512,768]{1,0:T(8,128)(2,1)S(1)}, u32[]{:S(2)}, u32[]{:S(2)}) collective-permute-start(bf16[512,768]{1,0:T(8,128)(2,1)} %bitcast.105), channel_id=1, source_target_pairs={{0,4},{4,0},{1,5},{5,1},{2,6},{6,2},{3,7},{7,3},{8,12},{12,8},{9,1... | collective-permute-start | bytes 2359304 | tf_op jit(solution)/shard_map/ppermute | solution.py:691
  3.6 16.6 %collective-permute-start.3 = (bf16[512,768]{1,0:T(8,128)(2,1)}, bf16[512,768]{1,0:T(8,128)(2,1)S(1)}, u32[]{:S(2)}, u32[]{:S(2)}) collective-permute-start(bf16[512,768]{1,0:T(8,128)(2,1)} %bitcast.106), channel_id=1, source_target_pairs={{0,2},{2,0},{1,3},{3,1},{4,6},{6,4},{5,7},{7,5},{8,10},{10,8},{9,1... | collective-permute-start | bytes 2359304 | tf_op jit(solution)/shard_map/ppermute | solution.py:691
  4.4 12.3 %collective-permute-start.1 = (f32[4]{0:T(128)S(1)}, f32[4]{0:T(128)S(1)}, u32[]{:S(2)}, u32[]{:S(2)}) collective-permute-start(f32[4]{0:T(128)S(1)} %convert_reduce_fusion.1), channel_id=1, source_target_pairs={{0,2},{2,0},{1,3},{3,1},{4,6},{6,4},{5,7},{7,5},{8,10},{10,8},{9,1... | collective-permute-start | bytes 56 | tf_op jit(solution)/shard_map/ppermute | solution.py:691
  24.9 8.4 %collective-permute-start.4 = (bf16[512,768]{1,0:T(8,128)(2,1)S(1)}, bf16[512,768]{1,0:T(8,128)(2,1)S(1)}, u32[]{:S(2)}, u32[]{:S(2)}) collective-permute-start(bf16[512,768]{1,0:T(8,128)(2,1)S(1)} %collective-permute-done.tok_ref), channel_id=1, source_target_pairs={{0,2},{2,0},{1,3},{3,1},{4,6},{6,4},{5,7},{7,5},{8,10},{10,8},{9,1... | collective-permute-start | bytes 2359304 | tf_op jit(solution)/shard_map/ppermute | solution.py:691
  25.8 26.2 %all-to-all-start = ((bf16[4,256,768]{2,1,0:T(8,128)(2,1)}), bf16[4,256,768]{2,1,0:T(8,128)(2,1)S(1)}, u32[]{:S(2)}, u32[]{:S(2)}) async-start(bf16[4,256,768]{2,1,0:T(8,128)(2,1)} %bitcast.112), calls=%async_computation | async-start | bytes 3145728 | tf_op jit(solution)/shard_map/all_to_all | solution.py:781
  52.0 15.3 %all-to-all-start.1 = ((bf16[4,3,64,512]{3,2,1,0:T(8,128)(2,1)}), bf16[4,3,64,512]{3,2,1,0:T(8,128)(2,1)S(1)}, u32[]{:S(2)}, u32[]{:S(2)}) async-start(bf16[4,3,64,512]{3,2,1,0:T(8,128)(2,1)} %get-tuple-element.126), calls=%async_computation.1 | async-start | bytes 1572864 | tf_op jit(solution)/shard_map/all_to_all | solution.py:785
  73.1 23.5 %all-to-all-start.2 = ((bf16[4,256,768]{2,1,0:T(8,128)(2,1)}), bf16[4,256,768]{2,1,0:T(8,128)(2,1)S(1)}, u32[]{:S(2)}, u32[]{:S(2)}) async-start(bf16[4,256,768]{2,1,0:T(8,128)(2,1)} %bitcast.116), calls=%async_computation.2 | async-start | bytes 3145728 | tf_op jit(solution)/shard_map/all_to_all | solution.py:781
  87.7 8.3 %collective-permute-start.8 = (f32[4]{0:T(128)S(1)}, f32[4]{0:T(128)S(1)}, u32[]{:S(2)}, u32[]{:S(2)}) collective-permute-start(f32[4]{0:T(128)S(1)} %add_add_fusion.1), channel_id=1, source_target_pairs={{0,4},{4,0},{1,5},{5,1},{2,6},{6,2},{3,7},{7,3},{8,12},{12,8},{9,1... | collective-permute-start | bytes 56 | tf_op jit(solution)/shard_map/ppermute | solution.py:691
  119.2 31.0 %all-to-all-start.3 = ((bf16[4,256,768]{2,1,0:T(8,128)(2,1)}), bf16[4,256,768]{2,1,0:T(8,128)(2,1)S(1)}, u32[]{:S(2)}, u32[]{:S(2)}) async-start(bf16[4,256,768]{2,1,0:T(8,128)(2,1)} %bitcast.117), calls=%async_computation.3 | async-start | bytes 3145728 | tf_op jit(solution)/shard_map/all_to_all | solution.py:781
  150.2 12.4 %collective-permute-start.11 = (bf16[4,2,2,192,768]{4,3,2,1,0:T(8,128)(2,1)}, bf16[4,2,2,192,768]{4,3,2,1,0:T(8,128)(2,1)}, u32[]{:S(2)}, u32[]{:S(2)}) collective-permute-start(bf16[4,2,2,192,768]{4,3,2,1,0:T(8,128)(2,1)} %get-tuple-element.159), channel_id=1, source_target_pairs={{0,2},{2,0},{1,3},{3,1},{4,6},{6,4},{5,7},{7,5},{8,10},{10,8},{9,1... | collective-permute-start | bytes 14155784 | tf_op jit(solution)/shard_map/ppermute | solution.py:691
  158.7 8.6 %collective-permute-start.9 = (bf16[400,768]{1,0:T(8,128)(2,1)}, bf16[400,768]{1,0:T(8,128)(2,1)S(1)}, u32[]{:S(2)}, u32[]{:S(2)}) collective-permute-start(bf16[400,768]{1,0:T(8,128)(2,1)} %get-tuple-element.148), channel_id=1, source_target_pairs={{0,2},{2,0},{1,3},{3,1},{4,6},{6,4},{5,7},{7,5},{8,10},{10,8},{9,1... | collective-permute-start | bytes 1843208 | tf_op jit(solution)/shard_map/ppermute | solution.py:691
  158.9 15.3 %all-to-all-start.4 = ((bf16[4,3,64,512]{3,2,1,0:T(8,128)(2,1)}), bf16[4,3,64,512]{3,2,1,0:T(8,128)(2,1)S(1)}, u32[]{:S(2)}, u32[]{:S(2)}) async-start(bf16[4,3,64,512]{3,2,1,0:T(8,128)(2,1)} %get-tuple-element.146), calls=%async_computation.4 | async-start | bytes 1572864 | tf_op jit(solution)/shard_map/all_to_all | solution.py:785
  165.6 31.7 %collective-permute-start.12 = (bf16[2,2,192,768]{3,2,1,0:T(8,128)(2,1)}, bf16[2,2,192,768]{3,2,1,0:T(8,128)(2,1)S(1)}, u32[]{:S(2)}, u32[]{:S(2)}) collective-permute-start(bf16[2,2,192,768]{3,2,1,0:T(8,128)(2,1)} %fusion.20), channel_id=1, source_target_pairs={{0,8},{8,16},{16,24},{24,0},{1,9},{9,17},{17,25},{25,1},{2,10},{10... | collective-permute-start | bytes 3538952 | tf_op jit(solution)/shard_map/ppermute | solution.py:696
  184.3 29.9 %all-to-all-start.5 = ((bf16[4,256,768]{2,1,0:T(8,128)(2,1)}), bf16[4,256,768]{2,1,0:T(8,128)(2,1)S(1)}, u32[]{:S(2)}, u32[]{:S(2)}) async-start(bf16[4,256,768]{2,1,0:T(8,128)(2,1)} %bitcast.20), calls=%async_computation.5 | async-start | bytes 3145728 | tf_op jit(solution)/shard_map/all_to_all | solution.py:781
  200.4 30.1 %collective-permute-start.14 = (bf16[2,2,192,768]{3,2,1,0:T(8,128)(2,1)}, bf16[2,2,192,768]{3,2,1,0:T(8,128)(2,1)}, u32[]{:S(2)}, u32[]{:S(2)}) collective-permute-start(bf16[2,2,192,768]{3,2,1,0:T(8,128)(2,1)} %fusion.1), channel_id=1, source_target_pairs={{0,8},{8,16},{16,24},{24,0},{1,9},{9,17},{17,25},{25,1},{2,10},{10... | collective-permute-start | bytes 3538952 | tf_op jit(solution)/shard_map/ppermute | solution.py:696
  202.6 11.7 %collective-permute-start.10 = (bf16[208,768]{1,0:T(8,128)(2,1)S(1)}, bf16[208,768]{1,0:T(8,128)(2,1)S(1)}, u32[]{:S(2)}, u32[]{:S(2)}) collective-permute-start(bf16[208,768]{1,0:T(8,128)(2,1)S(1)} %copy-done.32), channel_id=1, source_target_pairs={{0,4},{4,0},{1,5},{5,1},{2,6},{6,2},{3,7},{7,3},{8,12},{12,8},{9,1... | collective-permute-start | bytes 958472 | tf_op jit(solution)/shard_map/ppermute | solution.py:691
  221.0 15.1 %collective-permute-start.13 = (bf16[400,768]{1,0:T(8,128)(2,1)}, bf16[400,768]{1,0:T(8,128)(2,1)}, u32[]{:S(2)}, u32[]{:S(2)}) collective-permute-start(bf16[400,768]{1,0:T(8,128)(2,1)} %get-tuple-element.178), channel_id=1, source_target_pairs={{0,1},{1,0},{2,3},{3,2},{4,5},{5,4},{6,7},{7,6},{8,9},{9,8},{10,11... | collective-permute-start | bytes 1843208 | tf_op jit(solution)/shard_map/ppermute | solution.py:691
  223.1 52.1 %all-to-all-start.6 = ((bf16[4,3,192,512]{3,2,1,0:T(8,128)(2,1)}), bf16[4,3,192,512]{3,2,1,0:T(8,128)(2,1)S(1)}, u32[]{:S(2)}, u32[]{:S(2)}) async-start(bf16[4,3,192,512]{3,2,1,0:T(8,128)(2,1)} %get-tuple-element.172), calls=%async_computation.6 | async-start | bytes 4718592 | tf_op jit(solution)/shard_map/all_to_all | solution.py:785
  238.7 8.8 %collective-permute-start.17 = (bf16[112,768]{1,0:T(8,128)(2,1)}, bf16[112,768]{1,0:T(8,128)(2,1)S(1)}, u32[]{:S(2)}, u32[]{:S(2)}) collective-permute-start(bf16[112,768]{1,0:T(8,128)(2,1)} %get-tuple-element.187), channel_id=1, source_target_pairs={{0,24},{8,0},{16,8},{24,16},{1,25},{9,1},{17,9},{25,17},{2,26},{10... | collective-permute-start | bytes 516104 | tf_op jit(solution)/shard_map/ppermute | solution.py:696
  242.3 14.1 %collective-permute-start.16 = (bf16[112,768]{1,0:T(8,128)(2,1)}, bf16[112,768]{1,0:T(8,128)(2,1)S(1)}, u32[]{:S(2)}, u32[]{:S(2)}) collective-permute-start(bf16[112,768]{1,0:T(8,128)(2,1)} %get-tuple-element.186), channel_id=1, source_target_pairs={{0,16},{8,24},{16,0},{24,8},{1,17},{9,25},{17,1},{25,9},{2,18},{10... | collective-permute-start | bytes 516104 | tf_op jit(solution)/shard_map/ppermute | solution.py:696
  242.3 14.1 %collective-permute-start.15 = (bf16[112,768]{1,0:T(8,128)(2,1)}, bf16[112,768]{1,0:T(8,128)(2,1)S(1)}, u32[]{:S(2)}, u32[]{:S(2)}) collective-permute-start(bf16[112,768]{1,0:T(8,128)(2,1)} %get-tuple-element.185), channel_id=1, source_target_pairs={{0,8},{8,16},{16,24},{24,0},{1,9},{9,17},{17,25},{25,1},{2,10},{10... | collective-permute-start | bytes 516104 | tf_op jit(solution)/shard_map/ppermute | solution.py:696
  256.5 14.6 %collective-permute-start.19 = (bf16[96,768]{1,0:T(8,128)(2,1)S(1)}, bf16[96,768]{1,0:T(8,128)(2,1)}, u32[]{:S(2)}, u32[]{:S(2)}) collective-permute-start(bf16[96,768]{1,0:T(8,128)(2,1)S(1)} %add_convert_fusion.2), channel_id=1, source_target_pairs={{0,16},{8,24},{16,0},{24,8},{1,17},{9,25},{17,1},{25,9},{2,18},{10... | collective-permute-start | bytes 442376 | tf_op jit(solution)/shard_map/ppermute | solution.py:696
  258.4 12.7 %collective-permute-start.18 = (bf16[96,768]{1,0:T(8,128)(2,1)S(1)}, bf16[96,768]{1,0:T(8,128)(2,1)}, u32[]{:S(2)}, u32[]{:S(2)}) collective-permute-start(bf16[96,768]{1,0:T(8,128)(2,1)S(1)} %add_convert_fusion.2), channel_id=1, source_target_pairs={{0,8},{8,16},{16,24},{24,0},{1,9},{9,17},{17,25},{25,1},{2,10},{10... | collective-permute-start | bytes 442376 | tf_op jit(solution)/shard_map/ppermute | solution.py:696
  273.0 14.1 %collective-permute-start.21 = (bf16[384,768]{1,0:T(8,128)(2,1)}, bf16[384,768]{1,0:T(8,128)(2,1)}, u32[]{:S(2)}, u32[]{:S(2)}) collective-permute-start(bf16[384,768]{1,0:T(8,128)(2,1)} %pad_maximum_fusion.2.refs_0_), channel_id=1, source_target_pairs={{0,1},{1,0},{2,3},{3,2},{4,5},{5,4},{6,7},{7,6},{8,9},{9,8},{10,11... | collective-permute-start | bytes 1769480 | tf_op jit(solution)/shard_map/ppermute | solution.py:691
  274.5 16.2 %collective-permute-start.22 = (bf16[384,768]{1,0:T(8,128)(2,1)}, bf16[384,768]{1,0:T(8,128)(2,1)}, u32[]{:S(2)}, u32[]{:S(2)}) collective-permute-start(bf16[384,768]{1,0:T(8,128)(2,1)} %pad_maximum_fusion.2.refs_0_), channel_id=1, source_target_pairs={{0,4},{4,0},{1,5},{5,1},{2,6},{6,2},{3,7},{7,3},{8,12},{12,8},{9,1... | collective-permute-start | bytes 1769480 | tf_op jit(solution)/shard_map/ppermute | solution.py:691
  275.0 37.4 %collective-permute-start.24 = (bf16[384,768]{1,0:T(8,128)(2,1)}, bf16[384,768]{1,0:T(8,128)(2,1)}, u32[]{:S(2)}, u32[]{:S(2)}) collective-permute-start(bf16[384,768]{1,0:T(8,128)(2,1)} %pad_maximum_fusion.2.refs_0_), channel_id=1, source_target_pairs={{0,2},{2,0},{1,3},{3,1},{4,6},{6,4},{5,7},{7,5},{8,10},{10,8},{9,1... | collective-permute-start | bytes 1769480 | tf_op jit(solution)/shard_map/ppermute | solution.py:691
  275.0 30.7 %collective-permute-start.28 = (bf16[2,2,192,768]{3,2,1,0:T(8,128)(2,1)}, bf16[2,2,192,768]{3,2,1,0:T(8,128)(2,1)}, u32[]{:S(2)}, u32[]{:S(2)}) collective-permute-start(bf16[2,2,192,768]{3,2,1,0:T(8,128)(2,1)} %fusion), channel_id=1, source_target_pairs={{0,8},{8,16},{16,24},{24,0},{1,9},{9,17},{17,25},{25,1},{2,10},{10... | collective-permute-start | bytes 3538952 | tf_op jit(solution)/shard_map/ppermute | solution.py:696
  287.1 13.7 %collective-permute-start.23 = (bf16[384,768]{1,0:T(8,128)(2,1)}, bf16[384,768]{1,0:T(8,128)(2,1)S(1)}, u32[]{:S(2)}, u32[]{:S(2)}) collective-permute-start(bf16[384,768]{1,0:T(8,128)(2,1)} %collective-permute-done.21.refs_1_), channel_id=1, source_target_pairs={{0,4},{4,0},{1,5},{5,1},{2,6},{6,2},{3,7},{7,3},{8,12},{12,8},{9,1... | collective-permute-start | bytes 1769480 | tf_op jit(solution)/shard_map/ppermute | solution.py:691
  290.7 21.7 %collective-permute-start.25 = (bf16[384,768]{1,0:T(8,128)(2,1)}, bf16[384,768]{1,0:T(8,128)(2,1)S(1)}, u32[]{:S(2)}, u32[]{:S(2)}) collective-permute-start(bf16[384,768]{1,0:T(8,128)(2,1)} %collective-permute-done.21.refs_1_), channel_id=1, source_target_pairs={{0,2},{2,0},{1,3},{3,1},{4,6},{6,4},{5,7},{7,5},{8,10},{10,8},{9,1... | collective-permute-start | bytes 1769480 | tf_op jit(solution)/shard_map/ppermute | solution.py:691
  290.7 21.6 %collective-permute-start.26 = (bf16[384,768]{1,0:T(8,128)(2,1)}, bf16[384,768]{1,0:T(8,128)(2,1)S(1)}, u32[]{:S(2)}, u32[]{:S(2)}) collective-permute-start(bf16[384,768]{1,0:T(8,128)(2,1)} %collective-permute-done.22.refs_2_), channel_id=1, source_target_pairs={{0,2},{2,0},{1,3},{3,1},{4,6},{6,4},{5,7},{7,5},{8,10},{10,8},{9,1... | collective-permute-start | bytes 1769480 | tf_op jit(solution)/shard_map/ppermute | solution.py:691
  300.9 11.5 %collective-permute-start.27 = (bf16[384,768]{1,0:T(8,128)(2,1)S(1)}, bf16[384,768]{1,0:T(8,128)(2,1)S(1)}, u32[]{:S(2)}, u32[]{:S(2)}) collective-permute-start(bf16[384,768]{1,0:T(8,128)(2,1)S(1)} %collective-permute-done.23.refs_3_), channel_id=1, source_target_pairs={{0,2},{2,0},{1,3},{3,1},{4,6},{6,4},{5,7},{7,5},{8,10},{10,8},{9,1... | collective-permute-start | bytes 1769480 | tf_op jit(solution)/shard_map/ppermute | solution.py:691
  309.1 17.1 %collective-permute-start.29 = (bf16[2,192,768]{2,1,0:T(8,128)(2,1)}, bf16[2,192,768]{2,1,0:T(8,128)(2,1)}, u32[]{:S(2)}, u32[]{:S(2)}) collective-permute-start(bf16[2,192,768]{2,1,0:T(8,128)(2,1)} %fusion.29), channel_id=1, source_target_pairs={{0,4},{4,0},{1,5},{5,1},{2,6},{6,2},{3,7},{7,3},{8,12},{12,8},{9,1... | collective-permute-start | bytes 1769480 | tf_op jit(solution)/shard_map/ppermute | solution.py:691
  (39 other events, 230.5 us)

commit v6 on v5

--- a/solution.py
+++ b/solution.py
@@ -260,7 +260,7 @@
 
 
 def mid_kernel(
-    pick_ref, x_ref, u_ref, wi_ref, wr_ref, load_ref, act_ref, gh_ref, rows_ref, router_ref, gate_ref, acc, gg, gate
+    mean, pick_ref, x_ref, u_ref, wi_ref, wr_ref, count_ref, act_ref, gh_ref, rows_ref, router_ref, gate_ref, acc, gg, gate
 ):
     f = pl.program_id(0)
     n = pl.num_programs(0)
@@ -298,13 +298,16 @@
     def _():
         g = gate[:, :1]
         got = jnp.sum(gg[...], axis=1, keepdims=True)
-        sel = (g * (1.0 - g) * (got + load_ref[:, :1])).astype(bf16).astype(f32)
+        lane = lax.broadcasted_iota(jnp.int32, count_ref.shape, 1)
+        count = jnp.sum(jnp.where(lane == pick_ref[2], count_ref[...], 0.0), axis=1, keepdims=True)
+        load = balance_weight * (count - mean) / (mean * mean)
+        sel = (g * (1.0 - g) * (got + load)).astype(bf16).astype(f32)
         rows_ref[...] = (acc[...] + sel * wr_ref[...]).astype(bf16)
         router_ref[...] = jnp.sum(x_ref[...].astype(f32) * sel, axis=0, keepdims=True)
         gate_ref[...] = gate[...]
 
 
-def expert_mid(pick, x, u, w_in, wr, load, fc=768):
+def expert_mid(pick, x, u, w_in, wr, counts, mean, fc=768):
     rows = x.shape[0]
     ff = w_in.shape[2]
 
@@ -313,7 +316,7 @@
 
     wide = pl.BlockSpec((rows, fc), lambda f, p: (0, f))
     return pl.pallas_call(
-        mid_kernel,
+        functools.partial(mid_kernel, mean),
         out_shape=(
             jax.ShapeDtypeStruct((rows, ff), bf16),
             jax.ShapeDtypeStruct((rows, ff), bf16),
@@ -345,7 +348,7 @@
             transcendentals=rows * ff,
         ),
         name="expert_mid",
-    )(pick, x, u, w_in, wr, load)
+    )(pick, x, u, w_in, wr, counts)
 
 
 def grads_kernel(
@@ -621,70 +624,75 @@
 
 
 def finish_kernel(dp, me_ref, *refs):
-    pieces = refs[:8]
-    weights = refs[8:11]
-    outs = refs[11:15]
-    gain_ref = refs[15]
-    got, wide, in_sem, out_sem = refs[16:]
+    pieces = refs[:10]
+    weights = refs[10:13]
+    scale_ref = refs[13]
+    outs = refs[14:18]
+    gain_ref = refs[18]
+    got, wide, held, in_sem, out_sem, w_sem = refs[19:]
     z, xi, ci, yi = me_ref[0], me_ref[1], me_ref[2], me_ref[3]
     rows = pieces[0].shape[0] // dp
-    per = 4 * 2 // dp
-    copies = []
-    for n in range(8):
-        c, x, y = (n // 4) ^ ci, ((n // 2) % 2) ^ xi, (n % 2) ^ yi
-        for r in range(dp):
+    copies = [pltpu.make_async_copy(weights[p], held.at[p], w_sem.at[p]) for p in range(3)]
+    for n in range(10):
+        k = n % 5
+        c, x, y = (n // 5) ^ ci, int(k > 1) ^ xi, int(k != 0 and k != 2) ^ yi
+        for i in range(pieces[n].shape[0] // rows):
+            r = i + dp // 2 if k == 4 else i
             j = y * dp + lax.rem(z + dp - r, dp)
             p = lax.div(j * 4, 2 * dp)
             first = (x * 2 + c) * (D // 4) + lax.rem(j, 2 * dp // 4) * rows
             copy = pltpu.make_async_copy(
-                pieces[n].at[pl.ds(r * rows, rows)],
+                pieces[n].at[pl.ds(i * rows, rows)],
                 got.at[p, pl.ds(pl.multiple_of(first, rows), rows)],
-                in_sem.at[n, r],
+                in_sem.at[n, i],
             )
-            copy.start()
             copies.append(copy)
+    for copy in copies[3:] + copies[:3]:
+        copy.start()
     for copy in copies:
         copy.wait()
-    del per
     gain = jnp.zeros((D, 1), f32)
     backs = []
-    for p in range(4):
+    for p in (3, 0, 1, 2):
         if p < 3:
             g = got[p].T.astype(f32)
-            gain = gain + jnp.sum(g * weights[p][...].astype(f32), axis=1, keepdims=True)
+            gain = gain + jnp.sum(g * held[p].astype(f32), axis=1, keepdims=True)
         else:
             g = got[p].astype(f32)
         wide[p] = g
         back = pltpu.make_async_copy(wide.at[p], outs[p], out_sem.at[p])
         back.start()
         backs.append(back)
-    gain_ref[...] = gain
+    gain_ref[...] = jnp.broadcast_to(gain, (D, 128)).T[:8] / scale_ref[...]
     for back in backs:
         back.wait()
 
 
-def finish(me, pieces, weights, dp):
+def finish(me, pieces, weights, scale, dp):
     whole = jax.ShapeDtypeStruct((D, D), f32)
     anywhere = pl.BlockSpec(memory_space=pl.ANY)
     return pl.pallas_call(
         functools.partial(finish_kernel, dp),
-        out_shape=(whole,) * 4 + (jax.ShapeDtypeStruct((D, 1), f32),),
+        out_shape=(whole,) * 4 + (jax.ShapeDtypeStruct((8, D), f32),),
         grid_spec=pltpu.PrefetchScalarGridSpec(
             num_scalar_prefetch=1,
             grid=(1,),
-            in_specs=[anywhere] * 8 + [pl.BlockSpec((D, D), lambda i, p: (0, 0))] * 3,
-            out_specs=(anywhere,) * 4 + (pl.BlockSpec((D, 1), lambda i, p: (0, 0)),),
+            in_specs=[anywhere] * 13
+            + [pl.BlockSpec((1, D), lambda i, p: (0, 0))],
+            out_specs=(anywhere,) * 4 + (pl.BlockSpec((8, D), lambda i, p: (0, 0)),),
             scratch_shapes=[
                 pltpu.VMEM((4, D, D), bf16),
                 pltpu.VMEM((4, D, D), f32),
-                pltpu.SemaphoreType.DMA((8, dp)),
+                pltpu.VMEM((3, D, D), bf16),
+                pltpu.SemaphoreType.DMA((10, dp)),
                 pltpu.SemaphoreType.DMA((4,)),
+                pltpu.SemaphoreType.DMA((3,)),
             ],
         ),
         compiler_params=pltpu.CompilerParams(vmem_limit_bytes=VMEM),
         cost_estimate=pl.CostEstimate(flops=8 * D * D, bytes_accessed=32 * D * D, transcendentals=0),
         name="finish",
-    )(me, *pieces, *weights)
+    )(me, *pieces, *weights, scale)
 
 
 def swap(v, axis):
@@ -759,7 +767,8 @@
     cap = 2 * rows // experts
     mine = D // ctx
     heads = mine // HD
-    pick = jnp.stack([xi, ci]).astype(jnp.int32)
+    expert_id = ei * nx + xi
+    pick = jnp.stack([xi, ci, expert_id]).astype(jnp.int32)
 
     tok = tokens.reshape(rows, D)
     flat = tok.astype(f32)
@@ -767,7 +776,7 @@
     near = swap(tok, "core")
 
     route = routes.reshape(rows)
-    hot = (route[:, None] == jnp.arange(experts, dtype=jnp.int32)[None, :]).astype(f32)
+    hot = (route[:, None] == jnp.arange(128, dtype=jnp.int32)[None, :]).astype(f32)
     lower = jnp.arange(rows)[:, None] >= jnp.arange(rows)[None, :]
     before = dg(lower.astype(bf16), hot.astype(bf16), 1, 0)
     rank = (jnp.sum(before * hot, axis=1) - 1.0).astype(jnp.int32)
@@ -791,9 +800,8 @@
     gain1 = norm1_gain.reshape(1, D)
     dy_low = cotangent.reshape(rows, D)
     dy = dy_low.astype(f32)
-    expert_id = ei * nx + xi
     wr = lax.dynamic_slice(w_router, (0, expert_id), (D, 1)).astype(f32).reshape(1, D)
-    counts = jnp.sum(hot, axis=0)
+    counts = jnp.sum(hot, axis=0, keepdims=True)
     counts = counts + swap(counts, "core")
     counts = add_pair(counts)
     so_far = project(ctx_i, tok, gain1, w_own, ctx, None)
@@ -812,19 +820,17 @@
     counts = counts + swap(counts, "x")
     attT = attT.reshape(D, rows)
     mean_load = rows * ctx * dp * owners / experts
-    load_term = balance_weight * (counts - mean_load) / (mean_load * mean_load)
-    load = jnp.broadcast_to(lax.dynamic_slice(load_term, (expert_id,), (1,)).reshape(1, 1), (1, 128))
-
     middle = flat + dg(attT, w_output, 0, 0)
     xh2, rstd2 = normal_form(middle)
     second = (xh2 * norm2_gain).astype(bf16)
-    gating = jax.nn.sigmoid(jnp.sum(hot * dg(second, w_router, 1, 0), axis=1))
+    gating = jax.nn.sigmoid(jnp.sum(hot[:, :experts] * dg(second, w_router, 1, 0), axis=1))
 
     up = expert_up(pick, dy_rows, w_out)
-    sig = jnp.pad(jnp.sum(hot * gating[:, None], axis=0), (0, D - experts))
-    x_rows = trade(pack(second))
+    sig = jnp.pad(jnp.sum(hot[:, :experts] * gating[:, None], axis=0), (0, D - experts))
+    counts, packed = tie(counts, pack(second))
+    x_rows = trade(packed)
     x_rows, gating, sig, slot, gain2 = tie(x_rows, gating, sig, slot[None], norm2_gain.reshape(1, D))
-    active, grad_hidden, back_rows, router_row, gate = expert_mid(pick, x_rows, up, w_in, wr, load)
+    active, grad_hidden, back_rows, router_row, gate = expert_mid(pick, x_rows, up, w_in, wr, counts, mean_load)
     returned = trade(back_rows)
     keep, send = expert_grads(pick, x_rows, dy_rows, gate, active, grad_hidden, dp, nx)
     produced = expert_out(pick, tie(active, keep)[0], w_out)
@@ -836,8 +842,10 @@
         return at(keep, (i + dp) % dp).astype(f32) + at(taken, (i + dp) % dp).astype(f32)
 
     def ring(moving, step):
-        moving = shift(moving, "dp", 1).astype(f32) + chunk(zi - 2 - step)
-        return moving if step == dp - 2 else moving.astype(bf16)
+        return (shift(moving, "dp", 1).astype(f32) + chunk(zi - 2 - step)).astype(bf16)
+
+    def side(v, x):
+        return lax.dynamic_index_in_dim(v, x, 1, keepdims=False)
 
     router_rows = (jnp.arange(experts) == expert_id).astype(f32)[:, None] * router_row
     small = jnp.concatenate([router_rows, jnp.zeros((1, D), f32), sig[None]], axis=0)
@@ -854,20 +862,20 @@
     go_got = swap(go_send, "x")
 
     so_far = attend_back(qkvT, kv, do, 0, oT, lse, 0, None)
-    produced, *so_far = tie(produced, *so_far)
+    produced, go_got, *so_far = tie(produced, go_got, *so_far)
     went_back = trade(produced)
     so_far = attend_back(qkvT, kv, do, 1, oT, lse, 1, so_far)
     moving, *so_far = tie(moving, *so_far)
     moving = ring(moving, 1)
     for h in range(2, heads):
         so_far = attend_back(qkvT, kv, do, h, oT, lse, h, so_far)
-    go_got, *so_far = tie(go_got, *so_far)
     went_back, dT, dsend = tie(went_back, *so_far)
     output = (middle + gating[:, None] * dg(spread, went_back, 0, 0)).astype(bf16)
-    got = turn(dsend)
 
     ei2 = ei if owners == 2 else jnp.zeros_like(ei)
     half, send, small = weight_rows(index(ei2), dT.reshape(3 * mine, length), normed_all, go, go_got, small)
+    dsend, send = tie(dsend, send)
+    got = turn(dsend)
     if owners == 2:
         gift = swap(send, "expert")
         gift, moving = tie(gift, moving)
@@ -887,17 +895,14 @@
         share = share.astype(bf16)
         pieces.append(jnp.concatenate([share] + [shift(share, "dp", step) for step in range(1, dp)], axis=0))
     small = more
-    moving, *pieces = tie(moving, *pieces)
-    for step in range(2, dp - 1):
+    output, keep, taken = tie(output, keep, taken)
+    crossed = swap(side(chunk(zi), 1 - xi).astype(bf16), "x")
+    for step in range(2, dp - 2):
         moving = ring(moving, step)
-
-    if owners == 2:
-        pieces.append(swap(pieces[0], "expert"))
-    pieces += [swap(piece, "x") for piece in pieces]
-    pieces += [swap(piece, "core") for piece in pieces]
-    me = jnp.stack([zi, xi, ci, ei2]).astype(jnp.int32)
-    *grads, grad_norm1 = finish(me, pieces, (w_query, w_key, w_value), dp)
-    grad_norm1 = grad_norm1.reshape(D) / norm1_gain
+    moving, crossed, *pieces = tie(moving, crossed, *pieces)
+    own = shift(side(moving, xi), "dp", 1)
+    route_on = [(z * nx + x, (z + 1) % dp * nx + 1 - x) for z in range(dp) for x in range(nx)]
+    theirs = side(moving, 1 - xi)
 
     grad_normed = 0.0
     for p, w in enumerate((w_query, w_key, w_value)):
@@ -905,8 +910,25 @@
     xh1, rstd1 = normal_form(flat)
     grad_tokens = grad_middle + norm_back(grad_normed * norm1_gain, xh1, rstd1)
 
-    own = lax.dynamic_index_in_dim(moving, xi, 1, keepdims=False)
-    moved = swap(lax.dynamic_index_in_dim(moving, 1 - xi, 1, keepdims=False).astype(bf16), "x").astype(f32)
+    if owners == 2:
+        pieces.append(swap(pieces[0], "expert"))
+    beyond = swap(pieces[0], "x")
+    pieces[1], beyond, theirs, grad_tokens = tie(pieces[1], beyond, theirs, grad_tokens)
+    moved = lax.ppermute(theirs, ("dp", "x"), route_on)
+    rest = pieces[0].shape[0] // 2
+    if owners == 2:
+        corner = [swap(pieces[1][:rest], "x"), swap(beyond[rest:], "expert")]
+    else:
+        corner = [swap(pieces[1][:rest], "x"), swap(pieces[1][rest:], "x")]
+    own, *corner = tie(own, *corner)
+    pieces += [beyond, *corner]
+    pieces += [swap(piece, "core") for piece in pieces]
+    me = jnp.stack([zi, xi, ci, ei2]).astype(jnp.int32)
+    *grads, grad_norm1 = finish(me, pieces, (w_query, w_key, w_value), gain1, dp)
+    grad_norm1 = grad_norm1[0]
+
+    own = own.astype(f32) + side(chunk(zi), xi)
+    moved = moved.astype(f32) + crossed.astype(f32)
     first, latter = jnp.where(xi == 0, own, moved), jnp.where(xi == 0, moved, own)
     both = jnp.stack([first, latter], axis=1)
     grad_in = jnp.swapaxes(both[0], 1, 2)
@@ -915,6 +937,7 @@
     grad_router = jnp.transpose(small[:experts])
     grad_norm2 = small[experts]
     total_sig = small[experts + 1, :experts]
+    counts = counts[0, :experts]
     balance = balance_weight * jnp.sum((counts - mean_load) / mean_load * total_sig) / mean_load
 
     return (

time: 336 us -> 333 us (level)
  waiting for transfers between devices: 66.8 us -> 58.6 us
    ppermute x18 -> x20, waiting for transfers between devices: 29.8 us -> 18.8 us  [swap(): return lax.ppermute(v, axis, [(0, 1), (1, 0)])]
    all_to_all x4, waiting for transfers between devices: 0.01 us -> 7.11 us  [trade(): lax.all_to_all(v.reshape(nx * owners, cap, D), ('x', 'expert'), split_axi...]
    ppermute x12, waiting for transfers between devices: 32.1 us -> 28.1 us  [shift(): return lax.ppermute(v, axis, [(i, (i + step) % n) for i in range(n)])]
    unnamed x68 -> x82, local copies, waits for them, and re-layouts: 8.97 us -> 10.8 us
    ppermute x18 -> x20, starting transfers between devices: 15.7 us -> 15.9 us  [swap(): return lax.ppermute(v, axis, [(0, 1), (1, 0)])]
  transfers between devices with their start and end apart: 37 -> 40, of which waited for: 16 -> 16; matrix products, arithmetic and copies ran while one was open for 12% -> 14% of each run, Pallas kernels for 37% -> 38%
where the time goes in v6:
time: 333 us; the launch traced here: 327 us
  Pallas kernels  144 us (43%)
  starting transfers between devices  60.2 us (18%)
  waiting for transfers between devices  58.6 us (18%)
  other arithmetic  24.3 us (7%)
  local copies, waits for them, and re-layouts  21.7 us (7%)
  matrix products  14.9 us (4%)
    ppermute x12, waiting for transfers between devices, shift(): return lax.ppermute(v, axis, [(i, (i + step) % n) for i in range(n)])  28.1 us
    pallas_call x3, Pallas kernels, attend_back(): pl.pallas_call(functools.partial(attend_back_kernel, h % 2 * HD, hv % 2 *...  28 us
    pallas_call x1, Pallas kernels, expert_mid(): pl.pallas_call(functools.partial(mid_kernel, mean), out_shape=(jax.ShapeD...  21.4 us
    pallas_call x4, Pallas kernels, one_step(): pl.pallas_call(kernel, out_shape=tuple((jax.ShapeDtypeStruct(shape, dtype...  19 us
    ppermute x20, waiting for transfers between devices, swap(): return lax.ppermute(v, axis, [(0, 1), (1, 0)])  18.8 us
    ppermute x12, starting transfers between devices, shift(): return lax.ppermute(v, axis, [(i, (i + step) % n) for i in range(n)])  17.3 us
    pallas_call x1, Pallas kernels, expert_grads(): pl.pallas_call(grads_kernel, out_shape=(part, part), grid_spec=pltpu.Pref...  16.4 us
    all_to_all x4, starting transfers between devices, trade(): lax.all_to_all(v.reshape(nx * owners, cap, D), ('x', 'expert'), split_axi...  16.1 us
  transfers between devices with their start and end apart: 40, of which 16 were waited for; matrix products, arithmetic and copies ran while one was open for 14% of the time, Pallas kernels for 38%

profile of v6, /device:TPU:0, one launch (start us, length us, event | category | flops | bytes accessed | tf_op | source)
XLA Modules:
  0.0 327.3 jit_solution(5701546536066873101)
XLA Ops:
  0.6 3.0 collective-permute-start
  15.3 3.8 %project.4 = (bf16[2048,768]{1,0:T(8,128)(2,1)}, bf16[576,2048]{1,0:T(8,128)(2,1)}, bf16[2048,384]{1,0:T(8,128)(2,1)}) custom-call(s32[1]{0:T(128)} %bitcast.6.place_ref, bf16[512,768]{1,0:T(8,128)(2,1)} %bitcast.106, f32[1,768]{1,0:T(1,128)} %reshape.301.gain_ref.refs_13_, bf16[768,576]{1,0:T(8,128)(2,1)} %pad_maximum_fusion.1.w_ref), custom_call_target="tpu_custom_call" | custom-call | flops 905969664 | bytes 3932160 | tf_op jit(solution)/shard_map/project/pallas_call | solution.py:51
  19.9 3.8 %project.5 = (bf16[2048,768]{1,0:T(8,128)(2,1)}, bf16[576,2048]{1,0:T(8,128)(2,1)}, bf16[2048,384]{1,0:T(8,128)(2,1)}) custom-call(s32[1]{0:T(128)} %bitcast.7.place_ref, bf16[512,768]{1,0:T(8,128)(2,1)} %copy-done.15, f32[1,768]{1,0:T(1,128)} %reshape.301.gain_ref.refs_13_, ...), custom_call_target="tpu_custom_call", output_to_operand_aliasing={{0}: (4, {}), {1}: (5, {}), {2}: (6, {})} | custom-call | flops 905969664 | bytes 3932160 | tf_op jit(solution)/shard_map/project/pallas_call | solution.py:51
  24.6 3.7 %all-to-all-start = ((bf16[4,256,768]{2,1,0:T(8,128)(2,1)}), bf16[4,256,768]{2,1,0:T(8,128)(2,1)S(1)}, u32[]{:S(2)}, u32[]{:S(2)}) async-start(bf16[4,256,768]{2,1,0:T(8,128)(2,1)} %bitcast.111), calls=%async_computation | async-start | bytes 3145728 | tf_op jit(solution)/shard_map/all_to_all | solution.py:790
  28.3 3.8 %project.6 = (bf16[2048,768]{1,0:T(8,128)(2,1)}, bf16[576,2048]{1,0:T(8,128)(2,1)}, bf16[2048,384]{1,0:T(8,128)(2,1)}) custom-call(s32[1]{0:T(128)} %bitcast.8.place_ref, bf16[512,768]{1,0:T(8,128)(2,1)} %copy-done.14, f32[1,768]{1,0:T(1,128)} %reshape.301.gain_ref.refs_13_, ...), custom_call_target="tpu_custom_call", output_to_operand_aliasing={{0}: (4, {}), {1}: (5, {}), {2}: (6, {})} | custom-call | flops 905969664 | bytes 3932160 | tf_op jit(solution)/shard_map/project/pallas_call | solution.py:51
  33.0 3.8 %project.7 = (bf16[2048,768]{1,0:T(8,128)(2,1)}, bf16[576,2048]{1,0:T(8,128)(2,1)}, bf16[2048,384]{1,0:T(8,128)(2,1)}) custom-call(s32[1]{0:T(128)} %bitcast.1.place_ref, bf16[512,768]{1,0:T(8,128)(2,1)} %copy-done.16, f32[1,768]{1,0:T(1,128)} %reshape.301.gain_ref.refs_13_, ...), custom_call_target="tpu_custom_call", output_to_operand_aliasing={{0}: (4, {}), {1}: (5, {}), {2}: (6, {})} | custom-call | flops 905969664 | bytes 3932160 | tf_op jit(solution)/shard_map/project/pallas_call | solution.py:51
  36.7 14.0 %attend.1 = (f32[192,2048]{1,0:T(8,128)}, bf16[4,3,64,512]{3,2,1,0:T(8,128)(2,1)}, f32[3,1,2048]{2,1,0:T(1,128)}) custom-call(bf16[576,2048]{1,0:T(8,128)(2,1)} %get-tuple-element.134.qT_ref.vT_ref.refs_0_.refs_2_, bf16[2048,384]{1,0:T(8,128)(2,1)} %get-tuple-element.135.k_ref.refs_1_.refs_3_, bf16[576,2048]{1,0:T(8,128)(2,1)} %get-tuple-element.134.qT_ref.vT_ref.refs_0_.refs_2_), custom_call_target="tpu_custom_call" | custom-call | flops 6442450944 | bytes 5505024 | tf_op jit(solution)/shard_map/attend/pallas_call | solution.py:115
  50.7 3.8 %all-to-all-start.1 = ((bf16[4,3,64,512]{3,2,1,0:T(8,128)(2,1)}), bf16[4,3,64,512]{3,2,1,0:T(8,128)(2,1)S(1)}, u32[]{:S(2)}, u32[]{:S(2)}) async-start(bf16[4,3,64,512]{3,2,1,0:T(8,128)(2,1)} %get-tuple-element.139), calls=%async_computation.1 | async-start | bytes 1572864 | tf_op jit(solution)/shard_map/all_to_all | solution.py:794
  55.2 3.6 %collective-permute-start.7 = (f32[1,128]{1,0:T(1,128)S(1)}, f32[1,128]{1,0:T(1,128)S(1)}, u32[]{:S(2)}, u32[]{:S(2)}) collective-permute-start(f32[1,128]{1,0:T(1,128)S(1)} %add.277), channel_id=1, source_target_pairs={{0,24},{8,0},{16,8},{24,16},{1,25},{9,1},{17,9},{25,17},{2,26},{10... | collective-permute-start | bytes 1544 | tf_op jit(solution)/shard_map/ppermute | solution.py:704
  72.5 4.3 %all-to-all-start.2 = ((bf16[4,256,768]{2,1,0:T(8,128)(2,1)}), bf16[4,256,768]{2,1,0:T(8,128)(2,1)S(1)}, u32[]{:S(2)}, u32[]{:S(2)}) async-start(bf16[4,256,768]{2,1,0:T(8,128)(2,1)} %bitcast.115), calls=%async_computation.2 | async-start | bytes 3145728 | tf_op jit(solution)/shard_map/all_to_all | solution.py:790
  78.1 9.9 %expert_up.1.u_ref = bf16[1024,3072]{1,0:T(8,128)(2,1)} custom-call(s32[3]{0:T(128)} %pad_add_fusion.pick_ref, bf16[1024,768]{1,0:T(8,128)(2,1)} %bitcast.108, bf16[2,3072,768]{2,1,0:T(8,128)(2,1)} %wo_ref.3), custom_call_target="tpu_custom_call" | custom-call | flops 4831838208 | bytes 12582912 | tf_op jit(solution)/shard_map/expert_up/pallas_call | solution.py:242
  88.5 7.1 %all-to-all-done.2 = bf16[4,256,768]{2,1,0:T(8,128)(2,1)S(1)} async-done(((bf16[4,256,768]{2,1,0:T(8,128)(2,1)}), bf16[4,256,768]{2,1,0:T(8,128)(2,1)S(1)}, u32[]{:S(2)}, u32[]{:S(2)}) %all-to-all-start.2) | async-done | bytes 1572896 | tf_op jit(solution)/shard_map/all_to_all | solution.py:790
  96.8 21.4 %expert_mid.1 = (bf16[1024,3072]{1,0:T(8,128)(2,1)}, bf16[1024,3072]{1,0:T(8,128)(2,1)}, bf16[1024,768]{1,0:T(8,128)(2,1)}, f32[1,768]{1,0:T(1,128)}, f32[1024,128]{1,0:T(8,128)}) custom-call(s32[3]{0:T(128)} %pad_add_fusion.pick_ref, bf16[1024,768]{1,0:T(8,128)(2,1)} %bitcast.113, bf16[1024,3072]{1,0:T(8,128)(2,1)} %expert_up.1.u_ref, ...), custom_call_target="tpu_custom_call" | custom-call | flops 9663676416 | bytes 28311552 | tf_op jit(solution)/shard_map/expert_mid/pallas_call | solution.py:318
  118.2 4.0 %all-to-all-start.3 = ((bf16[4,256,768]{2,1,0:T(8,128)(2,1)}), bf16[4,256,768]{2,1,0:T(8,128)(2,1)S(1)}, u32[]{:S(2)}, u32[]{:S(2)}) async-start(bf16[4,256,768]{2,1,0:T(8,128)(2,1)} %bitcast.116), calls=%async_computation.3 | async-start | bytes 3145728 | tf_op jit(solution)/shard_map/all_to_all | solution.py:790
  122.2 16.4 %expert_grads.1 = (bf16[4,2,2,192,768]{4,3,2,1,0:T(8,128)(2,1)}, bf16[4,2,2,192,768]{4,3,2,1,0:T(8,128)(2,1)}) custom-call(s32[3]{0:T(128)} %pad_add_fusion.pick_ref, bf16[1024,768]{1,0:T(8,128)(2,1)} %bitcast.114, bf16[1024,768]{1,0:T(8,128)(2,1)} %bitcast.109, f32[1024,128]{1,0:T(8,128)} %get-tuple-element.149.gate_ref, ...), custom_call_target="tpu_custom_call" | custom-call | flops 9663676416 | bytes 25165824 | tf_op jit(solution)/shard_map/expert_grads/pallas_call | solution.py:388
  138.6 10.6 %expert_out.1 = bf16[1024,768]{1,0:T(8,128)(2,1)} custom-call(s32[3]{0:T(128)} %pad_add_fusion.pick_ref, bf16[1024,3072]{1,0:T(8,128)(2,1)} %get-tuple-element.154.act_ref, bf16[2,3072,768]{2,1,0:T(8,128)(2,1)} %wo_ref.3), custom_call_target="tpu_custom_call" | custom-call | flops 4831838208 | bytes 12582912 | tf_op jit(solution)/shard_map/expert_out/pallas_call | solution.py:431
  150.4 7.2 %branch_back.1 = (f32[512,768]{1,0:T(8,128)}, bf16[4,3,64,512]{3,2,1,0:T(8,128)(2,1)}, f32[2,192,768]{2,1,0:T(8,128)}, bf16[400,768]{1,0:T(8,128)(2,1)}, f32[8,768]{1,0:T(8,128)}) custom-call(s32[1]{0:T(128)} %bitcast.16.me_ref, bf16[1024,768]{1,0:T(8,128)(2,1)} %bitcast.112, s32[1,512]{1,0:T(1,128)} %multiply_add_fusion.slot_ref, ...), custom_call_target="tpu_custom_call" | custom-call | flops 2013265920 | bytes 10253316 | tf_op jit(solution)/shard_map/branch_back/pallas_call | solution.py:512
  157.6 3.5 %all-to-all-start.4 = ((bf16[4,3,64,512]{3,2,1,0:T(8,128)(2,1)}), bf16[4,3,64,512]{3,2,1,0:T(8,128)(2,1)S(1)}, u32[]{:S(2)}, u32[]{:S(2)}) async-start(bf16[4,3,64,512]{3,2,1,0:T(8,128)(2,1)} %get-tuple-element.161), calls=%async_computation.4 | async-start | bytes 1572864 | tf_op jit(solution)/shard_map/all_to_all | solution.py:794
  173.6 9.3 %attend_back_head0.1 = (bf16[3,192,2048]{2,1,0:T(8,128)(2,1)}, bf16[4,3,192,512]{3,2,1,0:T(8,128)(2,1)}) custom-call(bf16[576,2048]{1,0:T(8,128)(2,1)} %get-tuple-element.134.qT_ref.vT_ref.refs_0_.refs_2_, bf16[2048,384]{1,0:T(8,128)(2,1)} %get-tuple-element.135.k_ref.refs_1_.refs_3_, bf16[576,2048]{1,0:T(8,128)(2,1)} %get-tuple-element.134.qT_ref.vT_ref.refs_0_.refs_2_, ...), custom_call_target="tpu_custom_call" | custom-call | flops 5368709120 | bytes 3145728 | tf_op jit(solution)/shard_map/attend_back_head0/pallas_call | solution.py:213
  183.7 4.0 %all-to-all-start.5 = ((bf16[4,256,768]{2,1,0:T(8,128)(2,1)}), bf16[4,256,768]{2,1,0:T(8,128)(2,1)S(1)}, u32[]{:S(2)}, u32[]{:S(2)}) async-start(bf16[4,256,768]{2,1,0:T(8,128)(2,1)} %bitcast.21), calls=%async_computation.5 | async-start | bytes 3145728 | tf_op jit(solution)/shard_map/all_to_all | solution.py:790
  187.7 9.4 %attend_back_head1.1 = (bf16[3,192,2048]{2,1,0:T(8,128)(2,1)}, bf16[4,3,192,512]{3,2,1,0:T(8,128)(2,1)}) custom-call(bf16[576,2048]{1,0:T(8,128)(2,1)} %get-tuple-element.134.qT_ref.vT_ref.refs_0_.refs_2_, bf16[2048,384]{1,0:T(8,128)(2,1)} %get-tuple-element.135.k_ref.refs_1_.refs_3_, ...), custom_call_target="tpu_custom_call", output_to_operand_aliasing={{0}: (7, {}), {1}: (8, {})} | custom-call | flops 5368709120 | bytes 3145728 | tf_op jit(solution)/shard_map/attend_back_head1/pallas_call | solution.py:213
  197.1 3.1 fusion.1
  202.0 9.3 %attend_back_head2.1 = (bf16[3,192,2048]{2,1,0:T(8,128)(2,1)}, bf16[4,3,192,512]{3,2,1,0:T(8,128)(2,1)}) custom-call(bf16[576,2048]{1,0:T(8,128)(2,1)} %get-tuple-element.134.qT_ref.vT_ref.refs_0_.refs_2_, bf16[2048,384]{1,0:T(8,128)(2,1)} %get-tuple-element.135.k_ref.refs_1_.refs_3_, ...), custom_call_target="tpu_custom_call", output_to_operand_aliasing={{0}: (7, {}), {1}: (8, {})} | custom-call | flops 5368709120 | bytes 3145728 | tf_op jit(solution)/shard_map/attend_back_head2/pallas_call | solution.py:213
  211.3 6.7 %weight_rows.1 = (f32[384,768]{1,0:T(8,128)}, bf16[400,768]{1,0:T(8,128)(2,1)}, f32[8,768]{1,0:T(8,128)}) custom-call(s32[1]{0:T(128)} %bitcast.26.half_ref, bf16[576,2048]{1,0:T(8,128)(2,1)} %bitcast.129, bf16[2048,768]{1,0:T(8,128)(2,1)} %get-tuple-element.187.normed_ref, f32[192,768]{1,0:T(8,128)} %get-tuple-element.188.go_ref, ...), custom_call_target="tpu_custom_call" | custom-call | flops 1811939328 | bytes 12263428 | tf_op jit(solution)/shard_map/weight_rows/pallas_call | solution.py:512
  218.0 3.6 %all-to-all-start.6 = ((bf16[4,3,192,512]{3,2,1,0:T(8,128)(2,1)}), bf16[4,3,192,512]{3,2,1,0:T(8,128)(2,1)S(1)}, u32[]{:S(2)}, u32[]{:S(2)}) async-start(bf16[4,3,192,512]{3,2,1,0:T(8,128)(2,1)} %get-tuple-element.207), calls=%async_computation.6 | async-start | bytes 4718592 | tf_op jit(solution)/shard_map/all_to_all | solution.py:794
  224.2 4.0 %add_convert_fusion.1 = bf16[512,768]{1,0:T(8,128)(2,1)} fusion(f32[512,768]{1,0:T(8,128)} %copy-done.4, bf16[1024,768]{1,0:T(8,128)(2,1)} %bitcast.110, s32[512]{0:T(512)S(1)} %copy-done.37, f32[512]{0:T(512)S(1)} %add_divide_fusion), kind=kOutput, calls=%fused_computation.27 | convolution fusion | flops 807010304 | bytes 3936256 | tf_op jit(solution)/shard_map/dot_general | solution.py:26
  232.3 6.6 %collective-permute-done.13.got_ref = bf16[400,768]{1,0:T(8,128)(2,1)S(1)} collective-permute-done((bf16[400,768]{1,0:T(8,128)(2,1)}, bf16[400,768]{1,0:T(8,128)(2,1)S(1)}, u32[]{:S(2)}, u32[]{:S(2)}) %collective-permute-start.13) | collective-permute-done | bytes 614432 | tf_op jit(solution)/shard_map/ppermute | solution.py:699
  250.6 10.1 %collective-permute-done.17 = bf16[112,768]{1,0:T(8,128)(2,1)S(1)} collective-permute-done((bf16[112,768]{1,0:T(8,128)(2,1)}, bf16[112,768]{1,0:T(8,128)(2,1)S(1)}, u32[]{:S(2)}, u32[]{:S(2)}) %collective-permute-start.17) | collective-permute-done | bytes 172064 | tf_op jit(solution)/shard_map/ppermute | solution.py:704
  266.0 10.5 %collective-permute-done.20 = bf16[96,768]{1,0:T(8,128)(2,1)S(1)} collective-permute-done((bf16[96,768]{1,0:T(8,128)(2,1)S(1)}, bf16[96,768]{1,0:T(8,128)(2,1)S(1)}, u32[]{:S(2)}, u32[]{:S(2)}) %collective-permute-start.20) | collective-permute-done | bytes 147488 | tf_op jit(solution)/shard_map/ppermute | solution.py:704
  288.6 3.9 %collective-permute-done.22.refs_1_ = bf16[384,768]{1,0:T(8,128)(2,1)} collective-permute-done((bf16[384,768]{1,0:T(8,128)(2,1)}, bf16[384,768]{1,0:T(8,128)(2,1)}, u32[]{:S(2)}, u32[]{:S(2)}) %collective-permute-start.22) | collective-permute-done | bytes 589856 | tf_op jit(solution)/shard_map/ppermute | solution.py:699
  303.3 4.8 %collective-permute-done.26.refs_4_ = bf16[192,768]{1,0:T(8,128)(2,1)S(1)} collective-permute-done((bf16[192,768]{1,0:T(8,128)(2,1)S(1)}, bf16[192,768]{1,0:T(8,128)(2,1)S(1)}, u32[]{:S(2)}, u32[]{:S(2)}) %collective-permute-start.26) | collective-permute-done | bytes 294944 | tf_op jit(solution)/shard_map/ppermute | solution.py:699
  311.7 9.8 %finish.1 = (f32[768,768]{1,0:T(8,128)}, f32[768,768]{1,0:T(8,128)}, f32[768,768]{1,0:T(8,128)}, f32[768,768]{1,0:T(8,128)}, f32[8,768]{1,0:T(8,128)}) custom-call(s32[4]{0:T(128)} %pad_add_fusion.1.me_ref, bf16[384,768]{1,0:T(8,128)(2,1)} %pad_maximum_fusion.2.refs_0_, bf16[384,768]{1,0:T(8,128)(2,1)} %collective-permute-done.22.refs_1_, ...), custom_call_target="tpu_custom_call" | custom-call | flops 4718592 | bytes 18874368 | tf_op jit(solution)/shard_map/finish/pallas_call | solution.py:674
  (215 shorter events, 101.1 us)
Async XLA Ops:
  0.6 23.0 %collective-permute-start = (bf16[512,768]{1,0:T(8,128)(2,1)}, bf16[512,768]{1,0:T(8,128)(2,1)S(1)}, u32[]{:S(2)}, u32[]{:S(2)}) collective-permute-start(bf16[512,768]{1,0:T(8,128)(2,1)} %bitcast.104), channel_id=1, source_target_pairs={{0,4},{4,0},{1,5},{5,1},{2,6},{6,2},{3,7},{7,3},{8,12},{12,8},{9,1... | collective-permute-start | bytes 2359304 | tf_op jit(solution)/shard_map/ppermute | solution.py:699
  3.6 15.4 %collective-permute-start.3 = (bf16[512,768]{1,0:T(8,128)(2,1)}, bf16[512,768]{1,0:T(8,128)(2,1)S(1)}, u32[]{:S(2)}, u32[]{:S(2)}) collective-permute-start(bf16[512,768]{1,0:T(8,128)(2,1)} %bitcast.105), channel_id=1, source_target_pairs={{0,2},{2,0},{1,3},{3,1},{4,6},{6,4},{5,7},{7,5},{8,10},{10,8},{9,1... | collective-permute-start | bytes 2359304 | tf_op jit(solution)/shard_map/ppermute | solution.py:699
  4.4 9.3 %collective-permute-start.1 = (f32[1,128]{1,0:T(1,128)S(1)}, f32[1,128]{1,0:T(1,128)S(1)}, u32[]{:S(2)}, u32[]{:S(2)}) collective-permute-start(f32[1,128]{1,0:T(1,128)S(1)} %bitcast.127), channel_id=1, source_target_pairs={{0,2},{2,0},{1,3},{3,1},{4,6},{6,4},{5,7},{7,5},{8,10},{10,8},{9,1... | collective-permute-start | bytes 1544 | tf_op jit(solution)/shard_map/ppermute | solution.py:699
  23.7 8.4 %collective-permute-start.4 = (bf16[512,768]{1,0:T(8,128)(2,1)S(1)}, bf16[512,768]{1,0:T(8,128)(2,1)S(1)}, u32[]{:S(2)}, u32[]{:S(2)}) collective-permute-start(bf16[512,768]{1,0:T(8,128)(2,1)S(1)} %collective-permute-done.tok_ref), channel_id=1, source_target_pairs={{0,2},{2,0},{1,3},{3,1},{4,6},{6,4},{5,7},{7,5},{8,10},{10,8},{9,1... | collective-permute-start | bytes 2359304 | tf_op jit(solution)/shard_map/ppermute | solution.py:699
  24.6 26.2 %all-to-all-start = ((bf16[4,256,768]{2,1,0:T(8,128)(2,1)}), bf16[4,256,768]{2,1,0:T(8,128)(2,1)S(1)}, u32[]{:S(2)}, u32[]{:S(2)}) async-start(bf16[4,256,768]{2,1,0:T(8,128)(2,1)} %bitcast.111), calls=%async_computation | async-start | bytes 3145728 | tf_op jit(solution)/shard_map/all_to_all | solution.py:790
  50.7 15.4 %all-to-all-start.1 = ((bf16[4,3,64,512]{3,2,1,0:T(8,128)(2,1)}), bf16[4,3,64,512]{3,2,1,0:T(8,128)(2,1)S(1)}, u32[]{:S(2)}, u32[]{:S(2)}) async-start(bf16[4,3,64,512]{3,2,1,0:T(8,128)(2,1)} %get-tuple-element.139), calls=%async_computation.1 | async-start | bytes 1572864 | tf_op jit(solution)/shard_map/all_to_all | solution.py:794
  66.1 5.9 %collective-permute-start.8 = (f32[1,128]{1,0:T(1,128)S(1)}, f32[1,128]{1,0:T(1,128)S(1)}, u32[]{:S(2)}, u32[]{:S(2)}) collective-permute-start(f32[1,128]{1,0:T(1,128)S(1)} %add_add_fusion), channel_id=1, source_target_pairs={{0,4},{4,0},{1,5},{5,1},{2,6},{6,2},{3,7},{7,3},{8,12},{12,8},{9,1... | collective-permute-start | bytes 1544 | tf_op jit(solution)/shard_map/ppermute | solution.py:699
  72.5 23.1 %all-to-all-start.2 = ((bf16[4,256,768]{2,1,0:T(8,128)(2,1)}), bf16[4,256,768]{2,1,0:T(8,128)(2,1)S(1)}, u32[]{:S(2)}, u32[]{:S(2)}) async-start(bf16[4,256,768]{2,1,0:T(8,128)(2,1)} %bitcast.115), calls=%async_computation.2 | async-start | bytes 3145728 | tf_op jit(solution)/shard_map/all_to_all | solution.py:790
  118.2 31.0 %all-to-all-start.3 = ((bf16[4,256,768]{2,1,0:T(8,128)(2,1)}), bf16[4,256,768]{2,1,0:T(8,128)(2,1)S(1)}, u32[]{:S(2)}, u32[]{:S(2)}) async-start(bf16[4,256,768]{2,1,0:T(8,128)(2,1)} %bitcast.116), calls=%async_computation.3 | async-start | bytes 3145728 | tf_op jit(solution)/shard_map/all_to_all | solution.py:790
  149.2 12.6 %collective-permute-start.11 = (bf16[4,2,2,192,768]{4,3,2,1,0:T(8,128)(2,1)}, bf16[4,2,2,192,768]{4,3,2,1,0:T(8,128)(2,1)}, u32[]{:S(2)}, u32[]{:S(2)}) collective-permute-start(bf16[4,2,2,192,768]{4,3,2,1,0:T(8,128)(2,1)} %get-tuple-element.174), channel_id=1, source_target_pairs={{0,2},{2,0},{1,3},{3,1},{4,6},{6,4},{5,7},{7,5},{8,10},{10,8},{9,1... | collective-permute-start | bytes 14155784 | tf_op jit(solution)/shard_map/ppermute | solution.py:699
  157.6 15.1 %all-to-all-start.4 = ((bf16[4,3,64,512]{3,2,1,0:T(8,128)(2,1)}), bf16[4,3,64,512]{3,2,1,0:T(8,128)(2,1)S(1)}, u32[]{:S(2)}, u32[]{:S(2)}) async-start(bf16[4,3,64,512]{3,2,1,0:T(8,128)(2,1)} %get-tuple-element.161), calls=%async_computation.4 | async-start | bytes 1572864 | tf_op jit(solution)/shard_map/all_to_all | solution.py:794
  164.7 32.4 %collective-permute-start.12 = (bf16[2,2,192,768]{3,2,1,0:T(8,128)(2,1)}, bf16[2,2,192,768]{3,2,1,0:T(8,128)(2,1)S(1)}, u32[]{:S(2)}, u32[]{:S(2)}) collective-permute-start(bf16[2,2,192,768]{3,2,1,0:T(8,128)(2,1)} %fusion.16), channel_id=1, source_target_pairs={{0,8},{8,16},{16,24},{24,0},{1,9},{9,17},{17,25},{25,1},{2,10},{10... | collective-permute-start | bytes 3538952 | tf_op jit(solution)/shard_map/ppermute | solution.py:704
  172.8 10.2 %collective-permute-start.10 = (bf16[208,768]{1,0:T(8,128)(2,1)}, bf16[208,768]{1,0:T(8,128)(2,1)S(1)}, u32[]{:S(2)}, u32[]{:S(2)}) collective-permute-start(bf16[208,768]{1,0:T(8,128)(2,1)} %get-tuple-element.166), channel_id=1, source_target_pairs={{0,4},{4,0},{1,5},{5,1},{2,6},{6,2},{3,7},{7,3},{8,12},{12,8},{9,1... | collective-permute-start | bytes 958472 | tf_op jit(solution)/shard_map/ppermute | solution.py:699
  183.7 27.6 %all-to-all-start.5 = ((bf16[4,256,768]{2,1,0:T(8,128)(2,1)}), bf16[4,256,768]{2,1,0:T(8,128)(2,1)S(1)}, u32[]{:S(2)}, u32[]{:S(2)}) async-start(bf16[4,256,768]{2,1,0:T(8,128)(2,1)} %bitcast.21), calls=%async_computation.5 | async-start | bytes 3145728 | tf_op jit(solution)/shard_map/all_to_all | solution.py:790
  200.2 29.7 %collective-permute-start.14 = (bf16[2,2,192,768]{3,2,1,0:T(8,128)(2,1)}, bf16[2,2,192,768]{3,2,1,0:T(8,128)(2,1)}, u32[]{:S(2)}, u32[]{:S(2)}) collective-permute-start(bf16[2,2,192,768]{3,2,1,0:T(8,128)(2,1)} %fusion.1), channel_id=1, source_target_pairs={{0,8},{8,16},{16,24},{24,0},{1,9},{9,17},{17,25},{25,1},{2,10},{10... | collective-permute-start | bytes 3538952 | tf_op jit(solution)/shard_map/ppermute | solution.py:704
  218.0 63.7 %all-to-all-start.6 = ((bf16[4,3,192,512]{3,2,1,0:T(8,128)(2,1)}), bf16[4,3,192,512]{3,2,1,0:T(8,128)(2,1)S(1)}, u32[]{:S(2)}, u32[]{:S(2)}) async-start(bf16[4,3,192,512]{3,2,1,0:T(8,128)(2,1)} %get-tuple-element.207), calls=%async_computation.6 | async-start | bytes 4718592 | tf_op jit(solution)/shard_map/all_to_all | solution.py:794
  222.2 16.7 %collective-permute-start.13 = (bf16[400,768]{1,0:T(8,128)(2,1)}, bf16[400,768]{1,0:T(8,128)(2,1)S(1)}, u32[]{:S(2)}, u32[]{:S(2)}) collective-permute-start(bf16[400,768]{1,0:T(8,128)(2,1)} %get-tuple-element.192), channel_id=1, source_target_pairs={{0,1},{1,0},{2,3},{3,2},{4,5},{5,4},{6,7},{7,6},{8,9},{9,8},{10,11... | collective-permute-start | bytes 1843208 | tf_op jit(solution)/shard_map/ppermute | solution.py:699
  242.3 8.3 %collective-permute-start.18 = (bf16[112,768]{1,0:T(8,128)(2,1)}, bf16[112,768]{1,0:T(8,128)(2,1)S(1)}, u32[]{:S(2)}, u32[]{:S(2)}) collective-permute-start(bf16[112,768]{1,0:T(8,128)(2,1)} %get-tuple-element.203), channel_id=1, source_target_pairs={{0,24},{8,0},{16,8},{24,16},{1,25},{9,1},{17,9},{25,17},{2,26},{10... | collective-permute-start | bytes 516104 | tf_op jit(solution)/shard_map/ppermute | solution.py:704
  244.5 16.2 %collective-permute-start.17 = (bf16[112,768]{1,0:T(8,128)(2,1)}, bf16[112,768]{1,0:T(8,128)(2,1)S(1)}, u32[]{:S(2)}, u32[]{:S(2)}) collective-permute-start(bf16[112,768]{1,0:T(8,128)(2,1)} %get-tuple-element.202), channel_id=1, source_target_pairs={{0,16},{8,24},{16,0},{24,8},{1,17},{9,25},{17,1},{25,9},{2,18},{10... | collective-permute-start | bytes 516104 | tf_op jit(solution)/shard_map/ppermute | solution.py:704
  245.3 15.4 %collective-permute-start.16 = (bf16[112,768]{1,0:T(8,128)(2,1)}, bf16[112,768]{1,0:T(8,128)(2,1)S(1)}, u32[]{:S(2)}, u32[]{:S(2)}) collective-permute-start(bf16[112,768]{1,0:T(8,128)(2,1)} %get-tuple-element.201), channel_id=1, source_target_pairs={{0,8},{8,16},{16,24},{24,0},{1,9},{9,17},{17,25},{25,1},{2,10},{10... | collective-permute-start | bytes 516104 | tf_op jit(solution)/shard_map/ppermute | solution.py:704
  248.9 28.5 %collective-permute-start.15 = (bf16[2,192,768]{2,1,0:T(8,128)(2,1)S(1)}, bf16[2,192,768]{2,1,0:T(8,128)(2,1)S(1)}, u32[]{:S(2)}, u32[]{:S(2)}) collective-permute-start(bf16[2,192,768]{2,1,0:T(8,128)(2,1)S(1)} %fusion.25), channel_id=1, source_target_pairs={{0,4},{4,0},{1,5},{5,1},{2,6},{6,2},{3,7},{7,3},{8,12},{12,8},{9,1... | collective-permute-start | bytes 1769480 | tf_op jit(solution)/shard_map/ppermute | solution.py:699
  260.9 15.7 %collective-permute-start.20 = (bf16[96,768]{1,0:T(8,128)(2,1)S(1)}, bf16[96,768]{1,0:T(8,128)(2,1)S(1)}, u32[]{:S(2)}, u32[]{:S(2)}) collective-permute-start(bf16[96,768]{1,0:T(8,128)(2,1)S(1)} %add_convert_fusion.2), channel_id=1, source_target_pairs={{0,16},{8,24},{16,0},{24,8},{1,17},{9,25},{17,1},{25,9},{2,18},{10... | collective-permute-start | bytes 442376 | tf_op jit(solution)/shard_map/ppermute | solution.py:704
  263.1 13.4 %collective-permute-start.19 = (bf16[96,768]{1,0:T(8,128)(2,1)S(1)}, bf16[96,768]{1,0:T(8,128)(2,1)S(1)}, u32[]{:S(2)}, u32[]{:S(2)}) collective-permute-start(bf16[96,768]{1,0:T(8,128)(2,1)S(1)} %add_convert_fusion.2), channel_id=1, source_target_pairs={{0,8},{8,16},{16,24},{24,0},{1,9},{9,17},{17,25},{25,1},{2,10},{10... | collective-permute-start | bytes 442376 | tf_op jit(solution)/shard_map/ppermute | solution.py:704
  277.4 15.1 %collective-permute-start.22 = (bf16[384,768]{1,0:T(8,128)(2,1)}, bf16[384,768]{1,0:T(8,128)(2,1)}, u32[]{:S(2)}, u32[]{:S(2)}) collective-permute-start(bf16[384,768]{1,0:T(8,128)(2,1)} %pad_maximum_fusion.2.refs_0_), channel_id=1, source_target_pairs={{0,1},{1,0},{2,3},{3,2},{4,5},{5,4},{6,7},{7,6},{8,9},{9,8},{10,11... | collective-permute-start | bytes 1769480 | tf_op jit(solution)/shard_map/ppermute | solution.py:699
  279.0 14.8 %collective-permute-start.23 = (bf16[384,768]{1,0:T(8,128)(2,1)}, bf16[384,768]{1,0:T(8,128)(2,1)}, u32[]{:S(2)}, u32[]{:S(2)}) collective-permute-start(bf16[384,768]{1,0:T(8,128)(2,1)} %pad_maximum_fusion.2.refs_0_), channel_id=1, source_target_pairs={{0,4},{4,0},{1,5},{5,1},{2,6},{6,2},{3,7},{7,3},{8,12},{12,8},{9,1... | collective-permute-start | bytes 1769480 | tf_op jit(solution)/shard_map/ppermute | solution.py:699
  280.3 27.9 %collective-permute-start.27 = (bf16[384,768]{1,0:T(8,128)(2,1)}, bf16[384,768]{1,0:T(8,128)(2,1)}, u32[]{:S(2)}, u32[]{:S(2)}) collective-permute-start(bf16[384,768]{1,0:T(8,128)(2,1)} %pad_maximum_fusion.2.refs_0_), channel_id=1, source_target_pairs={{0,2},{2,0},{1,3},{3,1},{4,6},{6,4},{5,7},{7,5},{8,10},{10,8},{9,1... | collective-permute-start | bytes 1769480 | tf_op jit(solution)/shard_map/ppermute | solution.py:699
  281.4 18.1 %collective-permute-start.24 = (bf16[2,192,768]{2,1,0:T(8,128)(2,1)}, bf16[2,192,768]{2,1,0:T(8,128)(2,1)}, u32[]{:S(2)}, u32[]{:S(2)}) collective-permute-start(bf16[2,192,768]{2,1,0:T(8,128)(2,1)} %get-tuple-element.231), channel_id=1, source_target_pairs={{0,8},{8,16},{16,24},{24,0},{1,9},{9,17},{17,25},{25,1},{2,10},{10... | collective-permute-start | bytes 1769480 | tf_op jit(solution)/shard_map/ppermute | solution.py:704
  294.8 7.3 %collective-permute-start.25 = (bf16[192,768]{1,0:T(8,128)(2,1)S(1)}, bf16[192,768]{1,0:T(8,128)(2,1)S(1)}, u32[]{:S(2)}, u32[]{:S(2)}) collective-permute-start(bf16[192,768]{1,0:T(8,128)(2,1)S(1)} %slice.83), channel_id=1, source_target_pairs={{0,4},{4,0},{1,5},{5,1},{2,6},{6,2},{3,7},{7,3},{8,12},{12,8},{9,1... | collective-permute-start | bytes 884744 | tf_op jit(solution)/shard_map/ppermute | solution.py:699
  296.9 13.0 %collective-permute-start.28 = (bf16[384,768]{1,0:T(8,128)(2,1)}, bf16[384,768]{1,0:T(8,128)(2,1)S(1)}, u32[]{:S(2)}, u32[]{:S(2)}) collective-permute-start(bf16[384,768]{1,0:T(8,128)(2,1)} %collective-permute-done.22.refs_1_), channel_id=1, source_target_pairs={{0,2},{2,0},{1,3},{3,1},{4,6},{6,4},{5,7},{7,5},{8,10},{10,8},{9,1... | collective-permute-start | bytes 1769480 | tf_op jit(solution)/shard_map/ppermute | solution.py:699
  297.9 12.1 %collective-permute-start.29 = (bf16[384,768]{1,0:T(8,128)(2,1)}, bf16[384,768]{1,0:T(8,128)(2,1)S(1)}, u32[]{:S(2)}, u32[]{:S(2)}) collective-permute-start(bf16[384,768]{1,0:T(8,128)(2,1)} %collective-permute-done.23.refs_2_), channel_id=1, source_target_pairs={{0,2},{2,0},{1,3},{3,1},{4,6},{6,4},{5,7},{7,5},{8,10},{10,8},{9,1... | collective-permute-start | bytes 1769480 | tf_op jit(solution)/shard_map/ppermute | solution.py:699
  299.5 8.6 %collective-permute-start.26 = (bf16[192,768]{1,0:T(8,128)(2,1)S(1)}, bf16[192,768]{1,0:T(8,128)(2,1)S(1)}, u32[]{:S(2)}, u32[]{:S(2)}) collective-permute-start(bf16[192,768]{1,0:T(8,128)(2,1)S(1)} %slice.84), channel_id=1, source_target_pairs={{0,1},{1,0},{2,3},{3,2},{4,5},{5,4},{6,7},{7,6},{8,9},{9,8},{10,11... | collective-permute-start | bytes 884744 | tf_op jit(solution)/shard_map/ppermute | solution.py:699
  302.0 20.9 %collective-permute-start.32 = (bf16[2,192,768]{2,1,0:T(8,128)(2,1)S(1)}, bf16[2,192,768]{2,1,0:T(8,128)(2,1)S(1)}, u32[]{:S(2)}, u32[]{:S(2)}) collective-permute-start(bf16[2,192,768]{2,1,0:T(8,128)(2,1)S(1)} %copy-done.23), channel_id=1, source_target_pairs={{0,12},{4,8},{8,20},{12,16},{16,28},{20,24},{24,4},{28,0},{1,13},{... | collective-permute-start | bytes 1769480 | tf_op jit(solution)/shard_map/ppermute | solution.py:917
  (49 other events, 345.7 us)
